TPU v7x, 128 devices: a whole 4x4x4 slice. The times are simulated.
128 devices in a mesh: mesh: 16 (over y, x_hi, core), mode: 8 (over z, x_lo).
Axes of the slice: x: 4 (x_hi: 2, x_lo: 2; x = x_hi * 2 + x_lo), y: 4, z: 4, core: 2. Of those that a mesh axis runs over, the one named last changes fastest.
Arguments:
- mode_shapes: bfloat16 [4000, 3, 65536], P('mode', None, 'mesh'), may hold values from -0.09375 to 0.09375
- load_nodal: bfloat16 [3, 65536, 384], P(None, 'mesh'), may hold values from -0.125 to 0.125
- mode_freq: float32 [4000], P('mode'), may hold values from 1 to 4
- damping: float32 [4000], P('mode'), may hold values from 0.3 to 0.6
- drive_freq: float32 [4], replicated, may hold values from 1 to 4
- send_lists: int32 [2, 4096], P(None, 'mesh'), may hold values from 0 to 4095
- connectivity: int32 [8, 65536], P(None, ('mesh', 'mode')), may hold values from 0 to 4607
- shape_grads: float32 [3, 8, 65536], P(None, None, ('mesh', 'mode')), may hold values from -3 to 3
- modulus: float32 [65536], P(('mesh', 'mode')), may hold values from 0.7 to 1.4
Outputs:
- stress_spectra: float32 [4, 36, 65536], P(None, None, ('mesh', 'mode'))
Inputs may be any that keep to these rules, and one draw needn't show every extreme that they name: `connectivity`: numbers below 4096 are the partition's own nodes, then 256 nodes received from the partition before, then 256 from the one after. `send_lists`: each entry is a node of the sending partition in its own numbering.
All inputs are finite; a program needn't handle non-finite values.
Results may differ from a plain program's by a relative error of at most 0.012.
Values may be sent and summed in bfloat16 or wider, within the bound.
No kernel may reach another device: no remote copies, remote signals or barrier semaphores. Data moves between devices by JAX's collectives and lax.ppermute only.
A program may use at most 128 MiB of HBM per device.

v0:
```python
import jax
import jax.numpy as jnp
from jax import lax
from jax.sharding import PartitionSpec as P

POISSON = 0.3


def with_halo(cells, sides, width):
    for axis, dim in sides:
        count = lax.axis_size(axis)
        ends = count - 1
        head = lax.slice_in_dim(cells, 0, width, axis=dim)
        tail = lax.slice_in_dim(cells, cells.shape[dim] - width, cells.shape[dim], axis=dim)
        cells = jnp.concatenate(
            [
                lax.ppermute(tail, axis, [(i, (i + 1) % count) for i in range(ends)]),
                cells,
                lax.ppermute(head, axis, [((i + 1) % count, i) for i in range(ends)]),
            ],
            axis=dim,
        )
    return cells


def transfer_factor(mode_freq, damping, drive_freq):
    natural = mode_freq[:, None]
    forcing = drive_freq[None, :]
    real_gap = natural * natural - forcing * forcing
    loss_term = 2.0 * damping[:, None] * natural * forcing
    magnitude = real_gap * real_gap + loss_term * loss_term
    return (real_gap / magnitude, -loss_term / magnitude)


def apply_factor(load_pairs, factor_re, factor_im):
    load_re = load_pairs[..., 0]
    load_im = load_pairs[..., 1]
    out_re = factor_re * load_re - factor_im * load_im
    out_im = factor_re * load_im + factor_im * load_re
    return jnp.stack([out_re, out_im], axis=-1)


def element_spectra(local_nodes, connectivity, shape_grads, modulus, freq_count):
    corners, elem_count = connectivity.shape
    col_count = local_nodes.shape[2]
    picked = jnp.take(local_nodes, connectivity.reshape(-1), axis=1).reshape(
        3, corners, elem_count, col_count
    )
    disp_grad = jnp.einsum(
        "caek,dae->cdek", picked.astype(jnp.float32), shape_grads, precision=lax.Precision.HIGHEST
    )
    lame_first = (modulus * (POISSON / ((1.0 + POISSON) * (1.0 - 2.0 * POISSON))))[:, None]
    shear_mod = (modulus * (1.0 / (2.0 * (1.0 + POISSON))))[:, None]
    volume_strain = disp_grad[0, 0] + disp_grad[1, 1] + disp_grad[2, 2]
    stress = jnp.stack(
        [
            lame_first * volume_strain + 2.0 * shear_mod * disp_grad[0, 0],
            lame_first * volume_strain + 2.0 * shear_mod * disp_grad[1, 1],
            lame_first * volume_strain + 2.0 * shear_mod * disp_grad[2, 2],
            shear_mod * (disp_grad[1, 2] + disp_grad[2, 1]),
            shear_mod * (disp_grad[2, 0] + disp_grad[0, 2]),
            shear_mod * (disp_grad[0, 1] + disp_grad[1, 0]),
        ],
        axis=0,
    )
    stress_parts = stress.reshape(6, elem_count, freq_count, col_count // (2 * freq_count), 2)
    real_part = stress_parts[..., 0]
    imag_part = stress_parts[..., 1]
    entries = []
    for row_index in range(6):
        for col_index in range(row_index, 6):
            entries.append(
                jnp.sum(
                    real_part[row_index] * real_part[col_index]
                    + imag_part[row_index] * imag_part[col_index],
                    axis=-1,
                )
            )
    for row_index in range(6):
        for col_index in range(row_index + 1, 6):
            entries.append(
                jnp.sum(
                    imag_part[row_index] * real_part[col_index]
                    - real_part[row_index] * imag_part[col_index],
                    axis=-1,
                )
            )
    return jnp.transpose(jnp.stack(entries, axis=0), (2, 0, 1))


def local(
    mode_shapes,
    load_nodal,
    mode_freq,
    damping,
    drive_freq,
    send_lists,
    connectivity,
    shape_grads,
    modulus,
):
    mode_count = mode_shapes.shape[0]
    freq_count = drive_freq.shape[0]
    bound_count = send_lists.shape[1]
    partial_loads = jnp.dot(
        mode_shapes.reshape(mode_count, -1),
        load_nodal.reshape(-1, load_nodal.shape[2]),
        preferred_element_type=jnp.float32,
    )
    col_count = partial_loads.shape[1]
    load_count = col_count // (2 * freq_count)
    factor_re, factor_im = transfer_factor(mode_freq, damping, drive_freq)
    modal_load = lax.psum(partial_loads, "mesh")
    response = apply_factor(
        modal_load.reshape(mode_count, freq_count, load_count, 2),
        factor_re[:, :, None],
        factor_im[:, :, None],
    )
    response = response.reshape(mode_count, col_count).astype(jnp.bfloat16)
    partial_value = jnp.einsum(
        "mcn,mk->cnk", mode_shapes, response, preferred_element_type=jnp.float32
    )
    flat_lists = send_lists.reshape(-1)
    displacement = lax.psum(partial_value.astype(jnp.bfloat16), "mode")
    rim_rows = jnp.take(displacement, flat_lists, axis=1).reshape(3, 2, bound_count, col_count)
    extended = with_halo(rim_rows, (("mesh", 1),), 1)
    local_nodes = jnp.concatenate([displacement, extended[:, 0], extended[:, 3]], axis=1)
    return element_spectra(local_nodes, connectivity, shape_grads, modulus, freq_count)


def solution(mesh):
    in_specs = (
        P("mode", None, "mesh"),
        P(None, "mesh", None),
        P("mode"),
        P("mode"),
        P(),
        P(None, "mesh"),
        P(None, ("mesh", "mode")),
        P(None, None, ("mesh", "mode")),
        P(("mesh", "mode")),
    )
    out_specs = P(None, None, ("mesh", "mode"))
    return jax.shard_map(local, mesh=mesh, in_specs=in_specs, out_specs=out_specs, check_vma=False)
```

profile of v0, /device:TPU:1, one launch (start us, length us, event | category | flops | bytes accessed | tf_op | source)
XLA Modules:
  0.0 752.6 jit_solution(8146254320350772132)
XLA Ops:
  6.5 12.7 %convolution_bitcast_fusion = f32[500,384]{0,1:T(8,128)S(1)} fusion(bf16[500,3,4096]{2,0,1:T(8,128)(2,1)} %param.9, bf16[3,4096,384]{2,1,0:T(8,128)(2,1)} %param.10), kind=kOutput, calls=%fused_computation.9 | convolution fusion | flops 4718592000 | bytes 22493184 | tf_op jit(solution)/shard_map/dot_general | solution.py:105
  21.1 142.5 %all-reduce.3.cloned.1.call-done = f32[500,4,48,2]{0,3,2,1:T(2,128)} async-done(((f32[500,4,48,2]{0,3,2,1:T(2,128)}), f32[500,4,48,2]{0,3,2,1:T(2,128)}) %all-reduce.3.cloned.1.call-update) | async-done | bytes 768016 | tf_op jit(solution)/shard_map/psum | solution.py:113
  163.6 2.4 subtract_convert_fusion
  167.3 12.0 %convert_bitcast_fusion = bf16[3,4096,384]{1,2,0:T(8,128)(2,1)} fusion(bf16[500,3,4096]{2,0,1:T(8,128)(2,1)} %param.9, bf16[500,384]{0,1:T(8,128)(2,1)S(1)} %convert_element_type.11), kind=kOutput, calls=%fused_computation.5 | convolution fusion | flops 4723310592 | bytes 22109184 | tf_op jit(solution)/shard_map/mcn,mk->cnk/dot_general | solution.py:120
  180.8 378.7 %all-reduce.5.cloned.1.call-done = bf16[3,4096,384]{1,2,0:T(8,128)(2,1)} async-done(((bf16[3,4096,384]{1,2,0:T(8,128)(2,1)}), bf16[3,4096,384]{1,2,0:T(8,128)(2,1)}) %all-reduce.5.cloned.1.call-update) | async-done | bytes 9437200 | tf_op jit(solution)/shard_map/psum | solution.py:124
  559.5 19.3 %copy.16 = bf16[3,4096,384]{2,0,1:T(4,128)(2,1)} copy(bf16[3,4096,384]{1,2,0:T(8,128)(2,1)} %all-reduce.5.cloned.1.call-done) | data formatting | bytes 18874368 | tf_op jit(solution)/shard_map/psum | solution.py:124
  578.8 7.0 gather_fusion
  587.3 4.9 collective-permute-start
  592.2 2.1 collective-permute-start.1
  594.6 4.4 collective-permute-done
  599.0 8.2 %collective-permute-done.1 = bf16[3,1,256,384]{2,3,0,1:T(8,128)(2,1)S(1)} collective-permute-done((bf16[3,1,256,384]{2,3,0,1:T(8,128)(2,1)S(1)}, bf16[3,1,256,384]{2,3,0,1:T(8,128)(2,1)S(1)}, u32[]{:S(2)}, u32[]{:S(2)}) %collective-permute-start.1) | collective-permute-done | bytes 589856 | tf_op jit(solution)/shard_map/ppermute | solution.py:19
  607.2 9.0 %pad_maximum_fusion = bf16[3,4608,384]{1,2,0:T(8,128)(2,1)} fusion(bf16[3,256,384]{1,2,0:T(8,128)(2,1)S(1)} %bitcast.124, bf16[3,256,384]{1,2,0:T(8,128)(2,1)S(1)} %bitcast.123, bf16[3,4096,384]{1,2,0:T(8,128)(2,1)} %all-reduce.5.cloned.1.call-done), kind=kLoop, calls=%fused_computation.2 | loop fusion | flops 31850496 | bytes 21233664 | tf_op jit(solution)/shard_map/concatenate | solution.py:127
  616.2 21.6 %copy.19 = bf16[3,4608,384]{2,0,1:T(4,128)(2,1)} copy(bf16[3,4608,384]{1,2,0:T(8,128)(2,1)} %pad_maximum_fusion) | data formatting | bytes 21233664 | tf_op jit(solution)/shard_map/concatenate | solution.py:127
  637.8 43.5 %gather_fusion.1 = bf16[4096,3,384]{2,1,0:T(4,128)(2,1)} fusion(bf16[3,4608,384]{2,0,1:T(4,128)(2,1)} %copy.19, s32[4096]{0:T(1024)S(1)} %broadcast_clamp_fusion), kind=kCustom, calls=%fused_computation.1 | custom fusion | bytes 18890752 | tf_op jit(solution)/shard_map/jit(_take)/gather | solution.py:46
  681.4 20.6 %fusion.2 = f32[3,3,512,384]{3,1,0,2:T(4,128)S(1)} fusion(f32[3,8,512,1]{1,0,3,2:T(4,128)S(1)} %copy-done, bf16[3,8,512,384]{3,0,2,1:T(4,128)(2,1)} %bitcast.115, pred[8,512]{0,1:T(8,128)(4,1)S(1)} %copy.13), kind=kOutput, calls=%fused_computation.7 | convolution fusion | flops 174587904 | bytes 16568320 | tf_op jit(solution)/shard_map/caek,dae->cdek/dot_general | solution.py:49
  702.0 4.9 slice_add_fusion.1
  706.9 3.5 copy.22
  710.5 3.6 copy.23
  714.0 2.0 copy.24
  719.6 1.8 broadcast_multiply_fusion.1
  721.5 3.7 multiply_add_fusion
  726.3 5.8 subtract_reduce_fusion.7
  732.1 7.2 subtract_reduce_fusion.10
  739.3 5.3 subtract_reduce_fusion
  (82 shorter events, 11.6 us)
Async XLA Ops:
  6.5 14.4 %copy-start.7 = (f32[4]{0:T(128)S(1)}, f32[4]{0:T(128)}, u32[]{:S(2)}) copy-start(f32[4]{0:T(128)} %param.13) | copy-start | bytes 52
  6.5 14.5 %copy-start.4 = (f32[500]{0:T(512)S(1)}, f32[500]{0:T(512)}, u32[]{:S(2)}) copy-start(f32[500]{0:T(512)} %param.11) | copy-start | bytes 6004
  6.5 14.5 %copy-start.5 = (f32[500]{0:T(512)S(1)}, f32[500]{0:T(512)}, u32[]{:S(2)}) copy-start(f32[500]{0:T(512)} %param.12) | copy-start | bytes 6004
  6.5 157.1 %all-reduce.3.cloned.1.call-start = ((), (), s32[]{:S(2)}) async-start(), calls=%async_computation | async-start | bytes 1572864 | tf_op jit(solution)/shard_map/psum | solution.py:113
  20.7 538.8 %all-reduce.5.cloned.1.call-start = ((), (), s32[]{:S(2)}) async-start(), calls=%async_computation.1 | async-start | bytes 18874368 | tf_op jit(solution)/shard_map/psum | solution.py:124
  167.2 12.1 %copy-start.3 = (s32[2,256]{1,0:T(2,128)S(1)}, s32[2,256]{1,0:T(2,128)}, u32[]{:S(2)}) copy-start(s32[2,256]{1,0:T(2,128)} %param.14) | copy-start | bytes 6148
  167.2 12.1 %copy-start.1 = (s32[8,512]{1,0:T(8,128)S(1)}, s32[8,512]{1,0:T(8,128)}, u32[]{:S(2)}) copy-start(s32[8,512]{1,0:T(8,128)} %param.15) | copy-start | bytes 49156
  167.3 12.1 %copy-start.2 = (f32[3,8,512]{2,1,0:T(8,128)S(1)}, f32[3,8,512]{2,1,0:T(8,128)}, u32[]{:S(2)}) copy-start(f32[3,8,512]{2,1,0:T(8,128)} %param.16) | copy-start | bytes 147460
  180.8 413.7 %copy-start.6 = (f32[512]{0:T(512)S(1)}, f32[512]{0:T(512)}, u32[]{:S(2)}) copy-start(f32[512]{0:T(512)} %param.17) | copy-start | bytes 6148
  587.3 11.7 %collective-permute-start = (bf16[3,1,256,384]{2,3,0,1:T(8,128)(2,1)S(1)}, bf16[3,1,256,384]{2,3,0,1:T(8,128)(2,1)S(1)}, u32[]{:S(2)}, u32[]{:S(2)}) collective-permute-start(bf16[3,1,256,384]{2,3,0,1:T(8,128)(2,1)S(1)} %get-tuple-element.86), channel_id=1, source_target_pairs={{0,8},{8,16},{16,24},{24,32},{32,40},{40,48},{48,56},{56,64},{64,7... | collective-permute-start | bytes 1769480 | tf_op jit(solution)/shard_map/ppermute | solution.py:17
  592.2 15.1 %collective-permute-start.1 = (bf16[3,1,256,384]{2,3,0,1:T(8,128)(2,1)S(1)}, bf16[3,1,256,384]{2,3,0,1:T(8,128)(2,1)S(1)}, u32[]{:S(2)}, u32[]{:S(2)}) collective-permute-start(bf16[3,1,256,384]{2,3,0,1:T(8,128)(2,1)S(1)} %get-tuple-element.87), channel_id=1, source_target_pairs={{8,0},{16,8},{24,16},{32,24},{40,32},{48,40},{56,48},{64,56},{72,6... | collective-permute-start | bytes 1769480 | tf_op jit(solution)/shard_map/ppermute | solution.py:19
  637.8 43.5 %copy-start = (f32[3,8,512,1]{1,0,3,2:T(4,128)S(1)}, f32[3,8,512,1]{1,0,3,2:T(4,128)}, u32[]{:S(2)}) copy-start(f32[3,8,512,1]{1,0,3,2:T(4,128)} %copy.30) | copy-start | bytes 147460
  745.0 0.7 copy-start.8
Sparse Core Ops, SparseCore 0:
  20.9 142.7 all-reduce.2
  179.4 380.0 all-reduce.4
where the time goes:
time: 754 us; the launch traced here: 753 us
  waiting for transfers between devices  534 us (71%)
  local copies, waits for them, and re-layouts  110 us (15%)
  matrix products  45.4 us (6%)
  other arithmetic  42.3 us (6%)
  between operations  13.8 us (2%)
    psum x1, waiting for transfers between devices, local(): displacement = lax.psum(partial_value.astype(jnp.bfloat16), 'mode')  379 us
    psum x1, waiting for transfers between devices, local(): modal_load = lax.psum(partial_loads, 'mesh')  143 us
    gather x1, local copies, waits for them, and re-layouts, element_spectra(): jnp.take(local_nodes, connectivity.reshape(-1), axis=1)  43.5 us
    concatenate x1, local copies, waits for them, and re-layouts, local(): jnp.concatenate([displacement, extended[:, 0], extended[:, 3]], axis=1)  21.6 us
    dot_general x1, matrix products, element_spectra(): jnp.einsum('caek,dae->cdek', picked.astype(jnp.float32), shape_grads, pre...  20.6 us
    reduce_sum x4, other arithmetic, element_spectra(): jnp.sum(imag_part[row_index] * real_part[col_index] - real_part[row_index...  19.4 us
    psum x1, local copies, waits for them, and re-layouts, local(): displacement = lax.psum(partial_value.astype(jnp.bfloat16), 'mode')  19.3 us
  transfers between devices with their start and end apart: 4, of which 4 were waited for; matrix products, arithmetic and copies ran while one was open for 0% of the time, Pallas kernels for 0%

commit v1 on v0

v1 whole, which is shorter than its diff:
```python
import functools

import jax
import jax.numpy as jnp
from jax import lax
from jax.experimental import pallas as pl
from jax.experimental.pallas import tpu as pltpu
from jax.sharding import PartitionSpec as P

POISSON = 0.3
F32 = jnp.float32
BF16 = jnp.bfloat16
MIB = 1024 * 1024
Z, XLO = 4, 2
Y, XHI, CORE = 4, 2, 2
HALF = 256


def params(mib):
    return pltpu.CompilerParams(vmem_limit_bytes=mib * MIB)


def mode_index(z, x):
    return (z % Z) * XLO + x


def mesh_index(y, h, c):
    return ((y % Y) * XHI + h) * CORE + c


def mode_perm(dz, flip=0):
    return [(mode_index(z, x), mode_index(z + dz, x ^ flip)) for z in range(Z) for x in range(XLO)]


def mesh_perm(dy, flip_h=0, flip_c=0):
    return [
        (mesh_index(y, h, c), mesh_index(y + dy, h ^ flip_h, c ^ flip_c))
        for y in range(Y)
        for h in range(XHI)
        for c in range(CORE)
    ]


def loads_kernel(core_ref, shapes_ref, load_ref, mine_ref, theirs_ref, acc):
    step = pl.program_id(0)
    modes = shapes_ref.shape[1]

    @pl.when(step == 0)
    def _():
        acc[...] = jnp.zeros_like(acc)

    acc[:modes, :] += jnp.dot(shapes_ref[0], load_ref[0], preferred_element_type=F32)

    @pl.when(step == pl.num_programs(0) - 1)
    def _():
        core = core_ref[0]
        mine_ref[...] = acc[pl.ds(core * HALF, HALF), :]
        theirs_ref[...] = acc[pl.ds((1 - core) * HALF, HALF), :].astype(BF16)


def partial_loads(core, shapes, load):
    comps, modes, nodes = shapes.shape
    cols = load.shape[2]
    block = 1024
    per = nodes // block
    return pl.pallas_call(
        loads_kernel,
        out_shape=(
            jax.ShapeDtypeStruct((HALF, cols), F32),
            jax.ShapeDtypeStruct((HALF, cols), BF16),
        ),
        grid=(comps * per,),
        in_specs=[
            pl.BlockSpec(memory_space=pltpu.SMEM),
            pl.BlockSpec((1, modes, block), lambda i: (i // per, 0, i % per)),
            pl.BlockSpec((1, block, cols), lambda i: (i // per, i % per, 0)),
        ],
        out_specs=(
            pl.BlockSpec((HALF, cols), lambda i: (0, 0)),
            pl.BlockSpec((HALF, cols), lambda i: (0, 0)),
        ),
        scratch_shapes=[pltpu.VMEM((2 * HALF, cols), F32)],
        compiler_params=params(32),
        cost_estimate=pl.CostEstimate(
            flops=2 * modes * comps * nodes * cols,
            bytes_accessed=2 * comps * nodes * (modes + cols),
            transcendentals=0,
        ),
        name="modal_loads",
    )(core, shapes, load)


def response_kernel(a_ref, b_ref, c_ref, d_ref, direct_ref, cross_ref, out_ref):
    total = (
        a_ref[...].astype(F32)
        + b_ref[...].astype(F32)
        + c_ref[...].astype(F32)
        + d_ref[...].astype(F32)
    )
    cols = total.shape[1]
    even = lax.broadcasted_iota(jnp.int32, total.shape, 1) % 2 == 0
    other = jnp.where(even, pltpu.roll(total, cols - 1, 1), pltpu.roll(total, 1, 1))
    out_ref[...] = (direct_ref[...] * total + cross_ref[...] * other).astype(BF16)


def half_response(parts, direct, cross):
    return pl.pallas_call(
        response_kernel,
        out_shape=jax.ShapeDtypeStruct(direct.shape, BF16),
        compiler_params=params(32),
        name="modal_response",
    )(*parts, direct, cross)


def disp_kernel(core_ref, mine_ref, theirs_ref, order_ref, shapes_ref, out_ref, mark_ref, resp, resp_t):
    modes = shapes_ref.shape[1]

    @pl.when(pl.program_id(0) == 0)
    def _():
        core = core_ref[0]
        resp[pl.ds(core * HALF, HALF), :] = mine_ref[...]
        resp[pl.ds((1 - core) * HALF, HALF), :] = theirs_ref[...]
        turned = lax.dot_general(
            order_ref[...], resp[...], (((1,), (1,)), ((), ())), preferred_element_type=F32
        )
        resp_t[...] = turned[:, :modes].astype(BF16)
        mark_ref[...] = jnp.zeros_like(mark_ref)

    value = jnp.dot(resp_t[...], shapes_ref[0], preferred_element_type=F32)
    parts, _, rows, width = out_ref.shape
    out_ref[...] = value.astype(BF16).reshape(parts, 1, rows, width)


def partial_disp(core, mine, theirs, order, shapes, parts):
    comps, modes, nodes = shapes.shape
    cols = mine.shape[1]
    rows = cols // parts
    block = 1024
    per = nodes // block
    return pl.pallas_call(
        disp_kernel,
        out_shape=(
            jax.ShapeDtypeStruct((parts, comps, rows, nodes), BF16),
            jax.ShapeDtypeStruct((8, 128), F32),
        ),
        grid=(comps * per,),
        in_specs=[
            pl.BlockSpec(memory_space=pltpu.SMEM),
            pl.BlockSpec((HALF, cols), lambda i: (0, 0)),
            pl.BlockSpec((HALF, cols), lambda i: (0, 0)),
            pl.BlockSpec((cols, cols), lambda i: (0, 0)),
            pl.BlockSpec((1, modes, block), lambda i: (i // per, 0, i % per)),
        ],
        out_specs=(
            pl.BlockSpec((parts, 1, rows, block), lambda i: (0, i // per, 0, i % per)),
            pl.BlockSpec((8, 128), lambda i: (0, 0)),
        ),
        scratch_shapes=[pltpu.VMEM((2 * HALF, cols), BF16), pltpu.VMEM((cols, modes), BF16)],
        compiler_params=params(32),
        cost_estimate=pl.CostEstimate(
            flops=2 * modes * comps * nodes * cols,
            bytes_accessed=2 * comps * nodes * (modes + cols),
            transcendentals=0,
        ),
        name="mode_displacement",
    )(core, mine, theirs, order, shapes)


NODE_BLOCK = 256
ROWS = 16


def weights_kernel(mark_ref, conn_ref, grads_ref, out_ref):
    del mark_ref
    first = (pl.program_id(0) * NODE_BLOCK).astype(F32)
    corners, width = conn_ref.shape
    lanes = 128
    base = lax.broadcasted_iota(jnp.int32, (ROWS, lanes), 0).astype(F32).astype(BF16)
    for piece in range(width // lanes):
        cut = pl.ds(piece * lanes, lanes)
        keys = (conn_ref[:, cut] - first).astype(BF16)
        grads = grads_ref[:, cut].astype(BF16)
        key = [jnp.broadcast_to(keys[a : a + 1, :], (ROWS, lanes)) for a in range(corners)]
        grad = [jnp.broadcast_to(grads[i : i + 1, :], (ROWS, lanes)) for i in range(3 * corners)]
        zero = jnp.zeros((ROWS, lanes), BF16)
        for row in range(NODE_BLOCK // ROWS):
            node = base + BF16(row * ROWS)
            sums = [None] * 3
            for a in range(corners):
                hit = node == key[a]
                for d in range(3):
                    term = jnp.where(hit, grad[d * corners + a], zero)
                    sums[d] = term if a == 0 else sums[d] + term
            for d in range(3):
                out_ref[d, pl.ds(row * ROWS, ROWS), cut] = sums[d]


def element_weights(mark, conn, grads, nodes):
    corners, elems = conn.shape
    width = 512
    return pl.pallas_call(
        weights_kernel,
        out_shape=jax.ShapeDtypeStruct((3, nodes, elems), BF16),
        grid=(nodes // NODE_BLOCK, elems // width),
        in_specs=[
            pl.BlockSpec(memory_space=pl.ANY),
            pl.BlockSpec((corners, width), lambda i, j: (0, j)),
            pl.BlockSpec((3 * corners, width), lambda i, j: (0, j)),
        ],
        out_specs=pl.BlockSpec((3, NODE_BLOCK, width), lambda i, j: (0, i, j)),
        compiler_params=params(32),
        cost_estimate=pl.CostEstimate(
            flops=6 * corners * nodes * elems * 20,
            bytes_accessed=6 * nodes * elems,
            transcendentals=0,
        ),
        name="element_weights",
    )(mark, conn, grads)


def spectra_kernel(own_ref, oth_ref, own_rim_ref, oth_rim_ref, weights_ref, modulus_ref, out_ref):
    inner = own_ref.shape[1]
    rows = own_ref.shape[0] // 3
    half = rows // 2
    width = weights_ref.shape[2]
    lame = modulus_ref[...] * (POISSON / ((1.0 + POISSON) * (1.0 - 2.0 * POISSON)))
    shear = modulus_ref[...] * (1.0 / (2.0 * (1.0 + POISSON)))
    real = [[0.0] * 6 for _ in range(6)]
    imag = [[0.0] * 6 for _ in range(6)]
    for values, rim in ((own_ref, own_rim_ref), (oth_ref, oth_rim_ref)):
        grads = []
        for d in range(3):
            grads.append(
                jnp.dot(values[...], weights_ref[d, :inner, :], preferred_element_type=F32)
                + jnp.dot(rim[...], weights_ref[d, inner:, :], preferred_element_type=F32)
            )

        def at(c, d):
            return grads[d][c * rows : (c + 1) * rows, :]

        volume = lame * (at(0, 0) + at(1, 1) + at(2, 2))
        twice = 2.0 * shear
        stress = [
            volume + twice * at(0, 0),
            volume + twice * at(1, 1),
            volume + twice * at(2, 2),
            shear * (at(1, 2) + at(2, 1)),
            shear * (at(2, 0) + at(0, 2)),
            shear * (at(0, 1) + at(1, 0)),
        ]
        re = [s[:half, :] for s in stress]
        im = [s[half:, :] for s in stress]

        def fold(x):
            return sum(x[8 * i : 8 * i + 8, :] for i in range(half // 8))

        for i in range(6):
            for j in range(i, 6):
                real[i][j] = real[i][j] + fold(re[i] * re[j] + im[i] * im[j])
            for j in range(i + 1, 6):
                imag[i][j] = imag[i][j] + fold(im[i] * re[j] - re[i] * im[j])
    entry = 0
    for i in range(6):
        for j in range(i, 6):
            out_ref[0, entry : entry + 1, :] = jnp.sum(real[i][j], axis=0, keepdims=True)
            entry += 1
    for i in range(6):
        for j in range(i + 1, 6):
            out_ref[0, entry : entry + 1, :] = jnp.sum(imag[i][j], axis=0, keepdims=True)
            entry += 1


def element_spectra(own, oth, own_rim, oth_rim, weights, modulus, groups):
    rows, inner = own.shape
    rim = own_rim.shape[1]
    elems = weights.shape[2]
    width = 256
    per = elems // groups // width
    whole = lambda i: (0, 0)
    return pl.pallas_call(
        spectra_kernel,
        out_shape=jax.ShapeDtypeStruct((groups, 36, elems // groups), F32),
        grid=(elems // width,),
        in_specs=[
            pl.BlockSpec((rows, inner), whole),
            pl.BlockSpec((rows, inner), whole),
            pl.BlockSpec((rows, rim), whole),
            pl.BlockSpec((rows, rim), whole),
            pl.BlockSpec((3, inner + rim, width), lambda i: (0, 0, i)),
            pl.BlockSpec((1, width), lambda i: (0, i)),
        ],
        out_specs=pl.BlockSpec((1, 36, width), lambda i: (i // per, 0, i % per)),
        compiler_params=params(48),
        cost_estimate=pl.CostEstimate(
            flops=2 * 6 * rows * (inner + rim) * elems,
            bytes_accessed=6 * (inner + rim) * elems,
            transcendentals=0,
        ),
        name="element_spectra",
    )(own, oth, own_rim, oth_rim, weights, modulus)


def local(
    mode_shapes,
    load_nodal,
    mode_freq,
    damping,
    drive_freq,
    send_lists,
    connectivity,
    shape_grads,
    modulus,
):
    modes, comps, nodes = mode_shapes.shape
    cols = load_nodal.shape[2]
    bound = send_lists.shape[1]
    freqs = drive_freq.shape[0]
    parts = Z * XLO
    rows = cols // parts
    mesh_at = lax.axis_index("mesh")
    z_at = lax.axis_index("mode") // XLO
    core = (mesh_at % CORE).astype(jnp.int32)
    core_arg = core.reshape(1)
    shapes = jnp.transpose(mode_shapes, (1, 0, 2))

    mesh_data = jnp.concatenate(
        [
            connectivity.astype(F32),
            shape_grads.reshape(-1, shape_grads.shape[2]),
            modulus[None, :],
        ],
        axis=0,
    )
    near = [mesh_data] + [lax.ppermute(mesh_data, "mode", mode_perm(-j)) for j in range(1, Z)]
    mesh_all = jnp.concatenate(near, axis=1)

    pad = 2 * HALF - modes
    natural = jnp.pad(mode_freq, (0, pad), constant_values=1.0)[:, None]
    loss = jnp.pad(damping, (0, pad), constant_values=0.5)[:, None]
    natural = lax.dynamic_slice_in_dim(natural, core * HALF, HALF)
    loss = lax.dynamic_slice_in_dim(loss, core * HALF, HALF)
    forcing = jnp.repeat(drive_freq, cols // freqs)[None, :]
    gap = natural * natural - forcing * forcing
    damp = 2.0 * loss * natural * forcing
    size = gap * gap + damp * damp
    sign = jnp.where(jnp.arange(cols) % 2 == 0, 1.0, -1.0).astype(F32)[None, :]
    direct = gap / size
    cross = sign * (damp / size)

    mine, theirs = partial_loads(core_arg, shapes, load_nodal)
    got = lax.ppermute(theirs, "mesh", mesh_perm(0, 0, 1))
    chip = (mine + got.astype(F32)).astype(BF16)
    got = lax.ppermute(chip, "mesh", mesh_perm(0, 1, 0))
    pair = (chip.astype(F32) + got.astype(F32)).astype(BF16)
    ring = [pair] + [lax.ppermute(pair, "mesh", mesh_perm(dy)) for dy in range(1, Y)]
    resp_mine = half_response(ring, direct, cross)
    resp_theirs = lax.ppermute(resp_mine, "mesh", mesh_perm(0, 0, 1))

    spot = jnp.arange(cols)
    block, inside = spot // rows, spot % rows
    source = block * rows + 2 * (inside % (rows // 2)) + inside // (rows // 2)
    order = (source[:, None] == spot[None, :]).astype(BF16)

    terms, mark = partial_disp(core_arg, resp_mine, resp_theirs, order, shapes, parts)
    terms = lax.all_to_all(terms, "mode", 0, 0)

    weights = element_weights(mark, mesh_all[:8], mesh_all[8:32], nodes + 2 * bound)
    pick = (send_lists.reshape(1, -1) == jnp.arange(nodes)[:, None]).astype(BF16)

    own = jnp.sum(terms.astype(F32), axis=0).astype(BF16).reshape(comps * rows, nodes)
    oth = lax.ppermute(own, "mode", mode_perm(0, 1))
    rim = jnp.dot(own, pick, preferred_element_type=F32).astype(BF16)

    count = lax.axis_size("mesh")

    def beside(values, step, flip):
        perm = []
        for p in range(count):
            if 0 <= p + step < count:
                for z in range(Z):
                    for x in range(XLO):
                        perm.append(
                            (p * parts + mode_index(z, x), (p + step) * parts + mode_index(z, x ^ flip))
                        )
        return lax.ppermute(values, ("mesh", "mode"), perm)

    before, after = rim[:, bound:], rim[:, :bound]
    own_rim = jnp.concatenate([beside(before, 1, 0), beside(after, -1, 0)], axis=1)
    oth_rim = jnp.concatenate([beside(before, 1, 1), beside(after, -1, 1)], axis=1)

    spectra = element_spectra(own, oth, own_rim, oth_rim, weights, mesh_all[32:33], Z)
    back = [spectra[0]] + [lax.ppermute(spectra[j], "mode", mode_perm(j)) for j in range(1, Z)]
    back = jnp.stack(back)
    return jnp.take(back, (z_at - jnp.arange(Z)) % Z, axis=0)


def solution(mesh):
    in_specs = (
        P("mode", None, "mesh"),
        P(None, "mesh", None),
        P("mode"),
        P("mode"),
        P(),
        P(None, "mesh"),
        P(None, ("mesh", "mode")),
        P(None, None, ("mesh", "mode")),
        P(("mesh", "mode")),
    )
    out_specs = P(None, None, ("mesh", "mode"))
    return jax.shard_map(local, mesh=mesh, in_specs=in_specs, out_specs=out_specs, check_vma=False)
```

time: 754 us -> 293 us (0.39)
  waiting for transfers between devices: 534 us -> 129 us
  Pallas kernels: 0 us -> 99.4 us
  local copies, waits for them, and re-layouts: 110 us -> 18 us
  matrix products: 45.4 us -> 1.5 us
  other arithmetic: 42.3 us -> 6.19 us
  starting transfers between devices: 7.28 us -> 37.3 us
  between operations: 13.8 us -> 0.31 us
    psum x2 -> x0, waiting for transfers between devices: 521 us -> none  [the longest x1 379 us: local(): displacement = lax.psum(partial_value.astype(jnp.bfloat16), 'mode')]
    ppermute x2 -> x17, waiting for transfers between devices: 12.7 us -> 129 us  [the longest x3 102 us: local(): lax.ppermute(mesh_data, 'mode', mode_perm(-j))]
    pallas_call x0 -> x5, Pallas kernels: none -> 99.4 us  [the longest x1 54.6 us: element_weights(): pl.pallas_call(weights_kernel, out_shape=jax.ShapeDtypeStruct((3, nodes,...]
    gather x3 -> x1, local copies, waits for them, and re-layouts: 51.7 us -> 0.57 us  [local(): return jnp.take(back, (z_at - jnp.arange(Z)) % Z, axis=0)]
    dot_general x3 -> x1, matrix products: 45.4 us -> 1.5 us  [local(): rim = jnp.dot(own, pick, preferred_element_type=F32).astype(BF16)]
    ppermute x2 -> x17, starting transfers between devices: 7.05 us -> 31.2 us  [the longest x4 14.1 us: beside(): return lax.ppermute(values, ('mesh', 'mode'), perm)]
    concatenate x1 -> x0, local copies, waits for them, and re-layouts: 21.6 us -> none  [local(): jnp.concatenate([displacement, extended[:, 0], extended[:, 3]], axis=1)]
    psum x1 -> x0, local copies, waits for them, and re-layouts: 19.3 us -> none  [local(): displacement = lax.psum(partial_value.astype(jnp.bfloat16), 'mode')]
  transfers between devices with their start and end apart: 4 -> 18, of which waited for: 4 -> 12; matrix products, arithmetic and copies ran while one was open for 0% -> 1% of each run, Pallas kernels for 0% -> 19%
where the time goes in v1:
time: 293 us; the launch traced here: 292 us
  waiting for transfers between devices  129 us (44%)
  Pallas kernels  99.4 us (34%)
  starting transfers between devices  37.3 us (13%)
  local copies, waits for them, and re-layouts  18 us (6%)
  other arithmetic  6.19 us (2%)
    ppermute x3, waiting for transfers between devices, local(): lax.ppermute(mesh_data, 'mode', mode_perm(-j))  102 us
    pallas_call x1, Pallas kernels, element_weights(): pl.pallas_call(weights_kernel, out_shape=jax.ShapeDtypeStruct((3, nodes,...  54.6 us
    pallas_call x1, Pallas kernels, element_spectra(): pl.pallas_call(spectra_kernel, out_shape=jax.ShapeDtypeStruct((groups, 36...  25.4 us
    unnamed x23, local copies, waits for them, and re-layouts  16.4 us
    ppermute x4, starting transfers between devices, beside(): return lax.ppermute(values, ('mesh', 'mode'), perm)  14.1 us
    ppermute x3, waiting for transfers between devices, local(): lax.ppermute(pair, 'mesh', mesh_perm(dy))  11.3 us
    pallas_call x1, Pallas kernels, partial_loads(): pl.pallas_call(loads_kernel, out_shape=(jax.ShapeDtypeStruct((HALF, cols)...  9.88 us
    pallas_call x1, Pallas kernels, partial_disp(): pl.pallas_call(disp_kernel, out_shape=(jax.ShapeDtypeStruct((parts, comps...  9.2 us
  transfers between devices with their start and end apart: 18, of which 12 were waited for; matrix products, arithmetic and copies ran while one was open for 1% of the time, Pallas kernels for 19%

profile of v1, /device:TPU:1, one launch (start us, length us, event | category | flops | bytes accessed | tf_op | source)
XLA Modules:
  0.0 292.0 jit_solution(10217892008250016255)
XLA Ops:
  0.0 4.5 %copy-done = bf16[500,3,4096]{2,0,1:T(8,128)(2,1)S(1)} copy-done((bf16[500,3,4096]{2,0,1:T(8,128)(2,1)S(1)}, bf16[500,3,4096]{2,0,1:T(8,128)(2,1)}, u32[]{:S(2)}) %copy-start) | copy-done | bytes 12288024
  4.5 3.7 %copy-done.2 = bf16[3,4096,384]{2,1,0:T(8,128)(2,1)S(1)} copy-done((bf16[3,4096,384]{2,1,0:T(8,128)(2,1)S(1)}, bf16[3,4096,384]{2,1,0:T(8,128)(2,1)}, u32[]{:S(2)}) %copy-start.2) | copy-done | bytes 9437208
  8.2 9.9 %modal_loads.1 = (f32[256,384]{1,0:T(8,128)S(1)}, bf16[256,384]{1,0:T(8,128)(2,1)S(1)}) custom-call(s32[1]{0:T(128)} %bitcast.core_ref, bf16[3,500,4096]{2,1,0:T(8,128)(2,1)S(1)} %bitcast.19, bf16[3,4096,384]{2,1,0:T(8,128)(2,1)S(1)} %copy-done.2), custom_call_target="tpu_custom_call" | custom-call | flops 4718592000 | bytes 21725184 | tf_op jit(solution)/shard_map/modal_loads/pallas_call | solution.py:66
  20.7 2.9 collective-permute-start.1
  23.7 4.7 %collective-permute-done.1 = bf16[256,384]{1,0:T(8,128)(2,1)S(1)} collective-permute-done((bf16[256,384]{1,0:T(8,128)(2,1)S(1)}, bf16[256,384]{1,0:T(8,128)(2,1)S(1)}, u32[]{:S(2)}, u32[]{:S(2)}) %collective-permute-start.1) | collective-permute-done | bytes 196640 | tf_op jit(solution)/shard_map/ppermute | solution.py:353
  28.5 2.9 collective-permute-start.4
  32.6 3.7 %collective-permute-done.4.d_ref = bf16[256,384]{1,0:T(8,128)(2,1)S(1)} collective-permute-done((bf16[256,384]{1,0:T(8,128)(2,1)S(1)}, bf16[256,384]{1,0:T(8,128)(2,1)S(1)}, u32[]{:S(2)}, u32[]{:S(2)}) %collective-permute-start.4) | collective-permute-done | bytes 196640 | tf_op jit(solution)/shard_map/ppermute | solution.py:355
  36.3 1.6 collective-permute-done.3.c_ref
  37.8 6.0 %collective-permute-done.2.b_ref = bf16[256,384]{1,0:T(8,128)(2,1)S(1)} collective-permute-done((bf16[256,384]{1,0:T(8,128)(2,1)S(1)}, bf16[256,384]{1,0:T(8,128)(2,1)S(1)}, u32[]{:S(2)}, u32[]{:S(2)}) %collective-permute-start.2) | collective-permute-done | bytes 196640 | tf_op jit(solution)/shard_map/ppermute | solution.py:355
  45.9 4.5 %copy-done.1 = bf16[500,3,4096]{2,0,1:T(8,128)(2,1)S(1)} copy-done((bf16[500,3,4096]{2,0,1:T(8,128)(2,1)S(1)}, bf16[500,3,4096]{2,0,1:T(8,128)(2,1)}, u32[]{:S(2)}) %copy-start.1) | copy-done | bytes 12288024
  50.4 9.2 %mode_displacement.1 = (bf16[8,3,48,4096]{3,2,1,0:T(8,128)(2,1)S(1)}, f32[8,128]{1,0:T(8,128)S(1)}) custom-call(s32[1]{0:T(128)} %bitcast.core_ref, bf16[256,384]{1,0:T(8,128)(2,1)S(1)} %modal_response.1.mine_ref, bf16[256,384]{1,0:T(8,128)(2,1)S(1)} %collective-permute-done.5.theirs_ref, bf16[384,384]{1,0:T(8,128)(2,1)S(1)} %fusion.3.order_ref, ...), custom_call_target="tpu_custom_call" | custom-call | flops 4718592000 | bytes 21725184 | tf_op jit(solution)/shard_map/mode_displacement/pallas_call | solution.py:140
  59.6 3.6 %copy-done.3 = bf16[8,3,48,4096]{3,2,1,0:T(8,128)(2,1)} copy-done((bf16[8,3,48,4096]{3,2,1,0:T(8,128)(2,1)}, bf16[8,3,48,4096]{3,2,1,0:T(8,128)(2,1)S(1)}, u32[]{:S(2)}) %copy-start.3) | copy-done | bytes 9437208
  63.2 6.1 %all-to-all-start = ((bf16[8,3,48,4096]{3,2,1,0:T(8,128)(2,1)}), bf16[8,3,48,4096]{3,2,1,0:T(8,128)(2,1)}, u32[]{:S(2)}, u32[]{:S(2)}) async-start(bf16[8,3,48,4096]{3,2,1,0:T(8,128)(2,1)} %copy-done.3), calls=%async_computation | async-start | bytes 18874368 | tf_op jit(solution)/shard_map/all_to_all | solution.py:365
  70.9 2.6 collective-permute-start.12
  74.5 101.8 %collective-permute-done.13 = f32[33,512]{1,0:T(8,128)S(1)} collective-permute-done((f32[33,512]{1,0:T(8,128)S(1)}, f32[33,512]{1,0:T(8,128)S(1)}, u32[]{:S(2)}, u32[]{:S(2)}) %collective-permute-start.13) | collective-permute-done | bytes 67616 | tf_op jit(solution)/shard_map/ppermute | solution.py:334
  177.0 5.4 %reduce_sum.12 = bf16[3,48,4096]{2,1,0:T(8,128)(2,1)S(1)} reduce(bf16[8,3,48,4096]{3,2,1,0:T(8,128)(2,1)} %all-to-all-done, bf16[]{:T(256)} %constant.114.clone.1), dimensions={0}, to_apply=%region_0.1 | reduce | flops 4128768 | bytes 10616834 | tf_op jit(solution)/shard_map/reduce_sum | solution.py:370
  185.3 5.6 %collective-permute-start.9 = (bf16[144,256]{1,0:T(8,128)(2,1)S(1)}, bf16[144,256]{1,0:T(8,128)(2,1)S(1)}, u32[]{:S(2)}, u32[]{:S(2)}) collective-permute-start(bf16[144,256]{1,0:T(8,128)(2,1)S(1)} %get-tuple-element.17), channel_id=1, source_target_pairs={{0,9},{1,8},{2,11},{3,10},{4,13},{5,12},{6,15},{7,14},{8,17},{9,16... | collective-permute-start | bytes 221192 | tf_op jit(solution)/shard_map/ppermute | solution.py:385
  190.9 1.9 collective-permute-start.10
  192.8 54.6 %element_weights.1.weights_ref = bf16[3,4608,2048]{2,1,0:T(8,128)(2,1)} custom-call(f32[8,128]{1,0:T(8,128)S(1)} %get-tuple-element.12.mark_ref, f32[8,2048]{1,0:T(8,128)S(1)} %pad_maximum_fusion.5.conn_ref, f32[24,2048]{1,0:T(8,128)S(1)} %slice.40.grads_ref), custom_call_target="tpu_custom_call" | custom-call | flops 9059696640 | bytes 56623104 | tf_op jit(solution)/shard_map/element_weights/pallas_call | solution.py:201
  247.4 4.5 %collective-permute-start.7 = (bf16[144,256]{1,0:T(8,128)(2,1)S(1)}, bf16[144,256]{1,0:T(8,128)(2,1)S(1)}, u32[]{:S(2)}, u32[]{:S(2)}) collective-permute-start(bf16[144,256]{1,0:T(8,128)(2,1)S(1)} %get-tuple-element.17), channel_id=1, source_target_pairs={{0,8},{1,9},{2,10},{3,11},{4,12},{5,13},{6,14},{7,15},{8,16},{9,17... | collective-permute-start | bytes 221192 | tf_op jit(solution)/shard_map/ppermute | solution.py:385
  251.9 2.1 collective-permute-start.8
  254.1 5.0 %collective-permute-done.8 = bf16[144,256]{1,0:T(8,128)(2,1)S(1)} collective-permute-done((bf16[144,256]{1,0:T(8,128)(2,1)S(1)}, bf16[144,256]{1,0:T(8,128)(2,1)S(1)}, u32[]{:S(2)}, u32[]{:S(2)}) %collective-permute-start.8) | collective-permute-done | bytes 73760 | tf_op jit(solution)/shard_map/ppermute | solution.py:385
  259.1 25.4 %element_spectra.1 = f32[4,36,512]{2,1,0:T(8,128)S(1)} custom-call(bf16[144,4096]{1,0:T(8,128)(2,1)S(1)} %bitcast.23, bf16[144,4096]{1,0:T(8,128)(2,1)S(1)} %collective-permute-done.6.oth_ref, bf16[144,512]{1,0:T(8,128)(2,1)S(1)} %pad_maximum_fusion.2.own_rim_ref, bf16[144,512]{1,0:T(8,128)(2,1)S(1)} %pad_maximum_fusion.3.oth_rim_ref, ...), custom_call_target="tpu_custom_call" | custom-call | flops 16307453952 | bytes 56623104 | tf_op jit(solution)/shard_map/element_spectra/pallas_call | solution.py:280
  287.9 1.6 collective-permute-done.15
  (69 shorter events, 17.9 us)
Async XLA Ops:
  8.2 11.4 %copy-start.10 = (f32[4]{0:T(128)S(1)}, f32[4]{0:T(128)}, u32[]{:S(2)}) copy-start(f32[4]{0:T(128)} %param.13) | copy-start | bytes 52
  8.2 15.4 %copy-start.7 = (f32[500]{0:T(512)S(1)}, f32[500]{0:T(512)}, u32[]{:S(2)}) copy-start(f32[500]{0:T(512)} %param.11) | copy-start | bytes 6004
  8.2 15.4 %copy-start.8 = (f32[500]{0:T(512)S(1)}, f32[500]{0:T(512)}, u32[]{:S(2)}) copy-start(f32[500]{0:T(512)} %param.12) | copy-start | bytes 6004
  18.1 2.6 collective-permute-start
  20.7 7.7 %collective-permute-start.1 = (bf16[256,384]{1,0:T(8,128)(2,1)S(1)}, bf16[256,384]{1,0:T(8,128)(2,1)S(1)}, u32[]{:S(2)}, u32[]{:S(2)}) collective-permute-start(bf16[256,384]{1,0:T(8,128)(2,1)S(1)} %add_convert_fusion.1), channel_id=1, source_target_pairs={{0,16},{8,24},{16,0},{24,8},{32,48},{40,56},{48,32},{56,40},{64,80... | collective-permute-start | bytes 589832 | tf_op jit(solution)/shard_map/ppermute | solution.py:353
  28.5 7.8 %collective-permute-start.4 = (bf16[256,384]{1,0:T(8,128)(2,1)S(1)}, bf16[256,384]{1,0:T(8,128)(2,1)S(1)}, u32[]{:S(2)}, u32[]{:S(2)}) collective-permute-start(bf16[256,384]{1,0:T(8,128)(2,1)S(1)} %add_convert_fusion.a_ref), channel_id=1, source_target_pairs={{0,96},{8,104},{16,112},{24,120},{32,0},{40,8},{48,16},{56,24},{64... | collective-permute-start | bytes 589832 | tf_op jit(solution)/shard_map/ppermute | solution.py:355
  31.3 6.5 %collective-permute-start.3 = (bf16[256,384]{1,0:T(8,128)(2,1)S(1)}, bf16[256,384]{1,0:T(8,128)(2,1)S(1)}, u32[]{:S(2)}, u32[]{:S(2)}) collective-permute-start(bf16[256,384]{1,0:T(8,128)(2,1)S(1)} %add_convert_fusion.a_ref), channel_id=1, source_target_pairs={{0,64},{8,72},{16,80},{24,88},{32,96},{40,104},{48,112},{56,120},{... | collective-permute-start | bytes 589832 | tf_op jit(solution)/shard_map/ppermute | solution.py:355
  31.7 12.2 %collective-permute-start.2 = (bf16[256,384]{1,0:T(8,128)(2,1)S(1)}, bf16[256,384]{1,0:T(8,128)(2,1)S(1)}, u32[]{:S(2)}, u32[]{:S(2)}) collective-permute-start(bf16[256,384]{1,0:T(8,128)(2,1)S(1)} %add_convert_fusion.a_ref), channel_id=1, source_target_pairs={{0,32},{8,40},{16,48},{24,56},{32,64},{40,72},{48,80},{56,88},{64,... | collective-permute-start | bytes 589832 | tf_op jit(solution)/shard_map/ppermute | solution.py:355
  44.2 1.6 collective-permute-start.5
  63.2 6.1 %copy-start.4 = (f32[3,8,512]{2,1,0:T(8,128)S(1)}, f32[3,8,512]{2,1,0:T(8,128)}, u32[]{:S(2)}) copy-start(f32[3,8,512]{2,1,0:T(8,128)} %param.16) | copy-start | bytes 147460
  63.2 6.1 %copy-start.5 = (f32[512]{0:T(512)S(1)}, f32[512]{0:T(512)}, u32[]{:S(2)}) copy-start(f32[512]{0:T(512)} %param.17) | copy-start | bytes 6148
  63.2 11.3 %copy-start.9 = (s32[2,256]{1,0:T(2,128)S(1)}, s32[2,256]{1,0:T(2,128)}, u32[]{:S(2)}) copy-start(s32[2,256]{1,0:T(2,128)} %param.14) | copy-start | bytes 6148
  63.2 113.8 %all-to-all-start = ((bf16[8,3,48,4096]{3,2,1,0:T(8,128)(2,1)}), bf16[8,3,48,4096]{3,2,1,0:T(8,128)(2,1)}, u32[]{:S(2)}, u32[]{:S(2)}) async-start(bf16[8,3,48,4096]{3,2,1,0:T(8,128)(2,1)} %copy-done.3), calls=%async_computation | async-start | bytes 18874368 | tf_op jit(solution)/shard_map/all_to_all | solution.py:365
  69.4 106.9 %collective-permute-start.13 = (f32[33,512]{1,0:T(8,128)S(1)}, f32[33,512]{1,0:T(8,128)S(1)}, u32[]{:S(2)}, u32[]{:S(2)}) collective-permute-start(f32[33,512]{1,0:T(8,128)S(1)} %pad_maximum_fusion.4), channel_id=1, source_target_pairs={{0,2},{1,3},{2,4},{3,5},{4,6},{5,7},{6,0},{7,1},{8,10},{9,11},{10,... | collective-permute-start | bytes 202760 | tf_op jit(solution)/shard_map/ppermute | solution.py:334
  70.9 106.1 %collective-permute-start.12 = (f32[33,512]{1,0:T(8,128)S(1)}, f32[33,512]{1,0:T(8,128)S(1)}, u32[]{:S(2)}, u32[]{:S(2)}) collective-permute-start(f32[33,512]{1,0:T(8,128)S(1)} %pad_maximum_fusion.4), channel_id=1, source_target_pairs={{0,4},{1,5},{2,6},{3,7},{4,0},{5,1},{6,2},{7,3},{8,12},{9,13},{10,... | collective-permute-start | bytes 202760 | tf_op jit(solution)/shard_map/ppermute | solution.py:334
  73.5 103.4 %collective-permute-start.11 = (f32[33,512]{1,0:T(8,128)S(1)}, f32[33,512]{1,0:T(8,128)S(1)}, u32[]{:S(2)}, u32[]{:S(2)}) collective-permute-start(f32[33,512]{1,0:T(8,128)S(1)} %pad_maximum_fusion.4), channel_id=1, source_target_pairs={{0,6},{1,7},{2,0},{3,1},{4,2},{5,3},{6,4},{7,5},{8,14},{9,15},{10,... | collective-permute-start | bytes 202760 | tf_op jit(solution)/shard_map/ppermute | solution.py:334
  182.5 76.6 %collective-permute-start.6 = (bf16[144,4096]{1,0:T(8,128)(2,1)S(1)}, bf16[144,4096]{1,0:T(8,128)(2,1)S(1)}, u32[]{:S(2)}, u32[]{:S(2)}) collective-permute-start(bf16[144,4096]{1,0:T(8,128)(2,1)S(1)} %bitcast.21), channel_id=1, source_target_pairs={{0,1},{1,0},{2,3},{3,2},{4,5},{5,4},{6,7},{7,6},{8,9},{9,8},{10,11... | collective-permute-start | bytes 3538952 | tf_op jit(solution)/shard_map/ppermute | solution.py:371
  185.3 68.7 %collective-permute-start.9 = (bf16[144,256]{1,0:T(8,128)(2,1)S(1)}, bf16[144,256]{1,0:T(8,128)(2,1)S(1)}, u32[]{:S(2)}, u32[]{:S(2)}) collective-permute-start(bf16[144,256]{1,0:T(8,128)(2,1)S(1)} %get-tuple-element.17), channel_id=1, source_target_pairs={{0,9},{1,8},{2,11},{3,10},{4,13},{5,12},{6,15},{7,14},{8,17},{9,16... | collective-permute-start | bytes 221192 | tf_op jit(solution)/shard_map/ppermute | solution.py:385
  190.9 63.1 %collective-permute-start.10 = (bf16[144,256]{1,0:T(8,128)(2,1)S(1)}, bf16[144,256]{1,0:T(8,128)(2,1)S(1)}, u32[]{:S(2)}, u32[]{:S(2)}) collective-permute-start(bf16[144,256]{1,0:T(8,128)(2,1)S(1)} %get-tuple-element.18), channel_id=1, source_target_pairs={{8,1},{9,0},{10,3},{11,2},{12,5},{13,4},{14,7},{15,6},{16,9},{17,8... | collective-permute-start | bytes 221192 | tf_op jit(solution)/shard_map/ppermute | solution.py:385
  247.4 6.7 %collective-permute-start.7 = (bf16[144,256]{1,0:T(8,128)(2,1)S(1)}, bf16[144,256]{1,0:T(8,128)(2,1)S(1)}, u32[]{:S(2)}, u32[]{:S(2)}) collective-permute-start(bf16[144,256]{1,0:T(8,128)(2,1)S(1)} %get-tuple-element.17), channel_id=1, source_target_pairs={{0,8},{1,9},{2,10},{3,11},{4,12},{5,13},{6,14},{7,15},{8,16},{9,17... | collective-permute-start | bytes 221192 | tf_op jit(solution)/shard_map/ppermute | solution.py:385
  251.9 7.2 %collective-permute-start.8 = (bf16[144,256]{1,0:T(8,128)(2,1)S(1)}, bf16[144,256]{1,0:T(8,128)(2,1)S(1)}, u32[]{:S(2)}, u32[]{:S(2)}) collective-permute-start(bf16[144,256]{1,0:T(8,128)(2,1)S(1)} %get-tuple-element.18), channel_id=1, source_target_pairs={{8,0},{9,1},{10,2},{11,3},{12,4},{13,5},{14,6},{15,7},{16,8},{17,9... | collective-permute-start | bytes 221192 | tf_op jit(solution)/shard_map/ppermute | solution.py:385
  284.6 3.4 %collective-permute-start.16 = (f32[36,512]{1,0:T(8,128)S(1)}, f32[36,512]{1,0:T(8,128)S(1)}, u32[]{:S(2)}, u32[]{:S(2)}) collective-permute-start(f32[36,512]{1,0:T(8,128)S(1)} %get-tuple-element.14), channel_id=1, source_target_pairs={{0,6},{1,7},{2,0},{3,1},{4,2},{5,3},{6,4},{7,5},{8,14},{9,15},{10,... | collective-permute-start | bytes 221192 | tf_op jit(solution)/shard_map/ppermute | solution.py:392
  284.6 4.9 %collective-permute-start.15 = (f32[36,512]{1,0:T(8,128)S(1)}, f32[36,512]{1,0:T(8,128)S(1)}, u32[]{:S(2)}, u32[]{:S(2)}) collective-permute-start(f32[36,512]{1,0:T(8,128)S(1)} %get-tuple-element.15), channel_id=1, source_target_pairs={{0,4},{1,5},{2,6},{3,7},{4,0},{5,1},{6,2},{7,3},{8,12},{9,13},{10,... | collective-permute-start | bytes 221192 | tf_op jit(solution)/shard_map/ppermute | solution.py:392
  285.9 4.5 %collective-permute-start.14 = (f32[36,512]{1,0:T(8,128)S(1)}, f32[36,512]{1,0:T(8,128)S(1)}, u32[]{:S(2)}, u32[]{:S(2)}) collective-permute-start(f32[36,512]{1,0:T(8,128)S(1)} %get-tuple-element.16), channel_id=1, source_target_pairs={{0,2},{1,3},{2,4},{3,5},{4,6},{5,7},{6,0},{7,1},{8,10},{9,11},{10,... | collective-permute-start | bytes 221192 | tf_op jit(solution)/shard_map/ppermute | solution.py:392
  (5 other events, 22.4 us)

commit v2 on v1

v2 whole, which is shorter than its diff:
```python
import functools

import jax
import jax.numpy as jnp
from jax import lax
from jax.experimental import pallas as pl
from jax.experimental.pallas import tpu as pltpu
from jax.sharding import PartitionSpec as P

POISSON = 0.3
F32 = jnp.float32
BF16 = jnp.bfloat16
MIB = 1024 * 1024
Z, XLO = 4, 2
Y, XHI, CORE = 4, 2, 2
HALF = 256
CHUNK = 1024
ANY = pl.BlockSpec(memory_space=pl.ANY)
SMEM = pl.BlockSpec(memory_space=pltpu.SMEM)


def params(mib):
    return pltpu.CompilerParams(vmem_limit_bytes=mib * MIB)


def cost(flops, moved):
    return pl.CostEstimate(flops=int(flops), bytes_accessed=int(moved), transcendentals=0)


def shaped(shape, kind):
    return jax.ShapeDtypeStruct(shape, kind)


def mode_index(z, x):
    return (z % Z) * XLO + x


def mesh_index(y, h, c):
    return ((y % Y) * XHI + h) * CORE + c


def mode_perm(dz, flip=0):
    return [(mode_index(z, x), mode_index(z + dz, x ^ flip)) for z in range(Z) for x in range(XLO)]


def mesh_perm(dy, flip_h=0, flip_c=0):
    return [
        (mesh_index(y, h, c), mesh_index(y + dy, h ^ flip_h, c ^ flip_c))
        for y in range(Y)
        for h in range(XHI)
        for c in range(CORE)
    ]


def loads_kernel(core_ref, shapes_ref, load_ref, mine_ref, theirs_ref, acc):
    step = pl.program_id(0)
    modes = shapes_ref.shape[1]

    @pl.when(step == 0)
    def _():
        acc[...] = jnp.zeros_like(acc)

    acc[:modes, :] += jnp.dot(shapes_ref[0], load_ref[0], preferred_element_type=F32)

    @pl.when(step == pl.num_programs(0) - 1)
    def _():
        core = core_ref[0]
        mine_ref[...] = acc[pl.ds(core * HALF, HALF), :]
        theirs_ref[...] = acc[pl.ds((1 - core) * HALF, HALF), :].astype(BF16)


def partial_loads(core, shapes, load):
    comps, modes, nodes = shapes.shape
    cols = load.shape[2]
    block = 2048
    per = nodes // block
    return pl.pallas_call(
        loads_kernel,
        out_shape=(shaped((HALF, cols), F32), shaped((HALF, cols), BF16)),
        grid=(comps * per,),
        in_specs=[
            SMEM,
            pl.BlockSpec((1, modes, block), lambda i: (i // per, 0, i % per)),
            pl.BlockSpec((1, block, cols), lambda i: (i // per, i % per, 0)),
        ],
        out_specs=(
            pl.BlockSpec((HALF, cols), lambda i: (0, 0)),
            pl.BlockSpec((HALF, cols), lambda i: (0, 0)),
        ),
        scratch_shapes=[pltpu.VMEM((2 * HALF, cols), F32)],
        compiler_params=params(56),
        cost_estimate=cost(2 * modes * comps * nodes * cols, 2 * comps * nodes * (modes + cols)),
        name="modal_loads",
    )(core, shapes, load)


def response_kernel(a_ref, b_ref, c_ref, d_ref, direct_ref, cross_ref, out_ref):
    total = (
        a_ref[...].astype(F32)
        + b_ref[...].astype(F32)
        + c_ref[...].astype(F32)
        + d_ref[...].astype(F32)
    )
    cols = total.shape[1]
    even = lax.broadcasted_iota(jnp.int32, total.shape, 1) % 2 == 0
    other = jnp.where(even, pltpu.roll(total, cols - 1, 1), pltpu.roll(total, 1, 1))
    out_ref[...] = (direct_ref[...] * total + cross_ref[...] * other).astype(BF16)


def half_response(parts, direct, cross):
    return pl.pallas_call(
        response_kernel,
        out_shape=shaped(direct.shape, BF16),
        compiler_params=params(32),
        cost_estimate=cost(direct.size * 8, direct.size * 18),
        name="modal_response",
    )(*parts, direct, cross)


def element_data_kernel(mark_ref, conn_ref, grads_ref, modulus_ref, out_ref):
    del mark_ref
    corners, width = conn_ref.shape
    conn = conn_ref[...].astype(F32)
    out_ref[:corners, :] = conn
    for d in range(3):
        total = jnp.zeros((corners, width), F32)
        for a in range(corners):
            total = total + jnp.where(conn == conn[a : a + 1, :], grads_ref[d, a : a + 1, :], 0.0)
        out_ref[(d + 1) * corners : (d + 2) * corners, :] = total
    out_ref[4 * corners :, :] = jnp.broadcast_to(modulus_ref[...], (corners, width))


def element_data(mark, conn, grads, modulus):
    corners, elems = conn.shape
    vmem = pl.BlockSpec(memory_space=pltpu.VMEM)
    return pl.pallas_call(
        element_data_kernel,
        out_shape=shaped((5 * corners, elems), F32),
        in_specs=[ANY, vmem, vmem, vmem],
        out_specs=vmem,
        compiler_params=params(32),
        cost_estimate=cost(1000, elems * 4 * 80),
        name="element_data",
    )(mark, conn, grads, modulus[None, :])


def split_ways(blocks, plus_ref, minus_ref, up_ref, down_ref, own_ref):
    half = up_ref.shape[-1]
    low = [b[..., :half] for b in blocks]
    high = [b[..., half:] for b in blocks]
    plus_ref[0, 0] = low[2]
    plus_ref[1, 0] = high[1]
    minus_ref[0, 0] = high[2]
    minus_ref[1, 0] = low[3]
    up_ref[0] = low[1]
    down_ref[0] = high[3]
    own_ref[0] = blocks[0]


def way_shapes(comps, rows, width):
    half = width // 2
    shapes = (
        (2, comps, rows, half),
        (2, comps, rows, half),
        (comps, rows, half),
        (comps, rows, half),
        (comps, rows, width),
    )
    specs = tuple(
        pl.BlockSpec((2, 1) + s[2:], lambda i: (0, i, 0, 0))
        if len(s) == 4
        else pl.BlockSpec((1,) + s[1:], lambda i: (i, 0, 0))
        for s in shapes
    )
    return tuple(shaped(s, BF16) for s in shapes), specs


def z_first_kernel(mark_ref, resp_ref, shapes_ref, *out_refs):
    del mark_ref
    value = jnp.dot(resp_ref[...], shapes_ref[0], preferred_element_type=F32).astype(BF16)
    rows = value.shape[0] // Z
    split_ways([value[j * rows : (j + 1) * rows, :] for j in range(Z)], *out_refs)


def z_first_terms(mark, resp, shapes, chunk):
    comps, modes, _ = shapes.shape
    cols = resp.shape[0]
    out_shape, out_specs = way_shapes(comps, cols // Z, CHUNK)
    return pl.pallas_call(
        z_first_kernel,
        out_shape=out_shape,
        grid=(comps,),
        in_specs=[
            ANY,
            pl.BlockSpec((cols, modes), lambda i: (0, 0)),
            pl.BlockSpec((1, modes, CHUNK), lambda i: (i, 0, chunk)),
        ],
        out_specs=out_specs,
        compiler_params=params(52),
        cost_estimate=cost(2 * modes * comps * CHUNK * cols, 2 * comps * CHUNK * (modes + cols)),
        name="z_first_terms",
    )(mark, resp, shapes)


def x_first_kernel(core_ref, mine_ref, theirs_ref, order_ref, shapes_ref, away_ref, keep_ref, turned_ref, resp):
    modes = shapes_ref.shape[1]

    @pl.when(pl.program_id(0) == 0)
    def _():
        core = core_ref[0]
        resp[pl.ds(core * HALF, HALF), :] = mine_ref[...]
        resp[pl.ds((1 - core) * HALF, HALF), :] = theirs_ref[...]
        turned = lax.dot_general(
            order_ref[...], resp[...], (((1,), (1,)), ((), ())), preferred_element_type=F32
        )
        turned_ref[...] = turned[:, :modes].astype(BF16)

    value = jnp.dot(turned_ref[...], shapes_ref[0], preferred_element_type=F32).astype(BF16)
    rows = value.shape[0] // (Z * XLO)
    for j in range(Z):
        keep_ref[j, 0] = value[(2 * j) * rows : (2 * j + 1) * rows, :]
        away_ref[j, 0] = value[(2 * j + 1) * rows : (2 * j + 2) * rows, :]


def x_first_terms(core, mine, theirs, order, shapes, chunk):
    comps, modes, _ = shapes.shape
    cols = mine.shape[1]
    rows = cols // (Z * XLO)
    part = pl.BlockSpec((Z, 1, rows, CHUNK), lambda i: (0, i, 0, 0))
    whole = lambda i: (0, 0)
    return pl.pallas_call(
        x_first_kernel,
        out_shape=(
            shaped((Z, comps, rows, CHUNK), BF16),
            shaped((Z, comps, rows, CHUNK), BF16),
            shaped((cols, modes), BF16),
        ),
        grid=(comps,),
        in_specs=[
            SMEM,
            pl.BlockSpec((HALF, cols), whole),
            pl.BlockSpec((HALF, cols), whole),
            pl.BlockSpec((cols, cols), whole),
            pl.BlockSpec((1, modes, CHUNK), lambda i: (i, 0, chunk)),
        ],
        out_specs=(part, part, pl.BlockSpec((cols, modes), whole)),
        scratch_shapes=[pltpu.VMEM((2 * HALF, cols), BF16)],
        compiler_params=params(52),
        cost_estimate=cost(2 * modes * comps * CHUNK * cols, 2 * comps * CHUNK * (modes + cols)),
        name="x_first_terms",
    )(core, mine, theirs, order, shapes)


def x_sum_kernel(keep_ref, got_ref, *out_refs):
    blocks = [(keep_ref[j, 0].astype(F32) + got_ref[j, 0].astype(F32)).astype(BF16) for j in range(Z)]
    split_ways(blocks, *out_refs)


def x_sum(keep, got):
    _, comps, rows, width = keep.shape
    out_shape, out_specs = way_shapes(comps, rows, width)
    part = pl.BlockSpec((Z, 1, rows, width), lambda i: (0, i, 0, 0))
    return pl.pallas_call(
        x_sum_kernel,
        out_shape=out_shape,
        grid=(comps,),
        in_specs=[part, part],
        out_specs=out_specs,
        compiler_params=params(32),
        cost_estimate=cost(keep.size, keep.size * 6),
        name="x_sum",
    )(keep, got)


def pass_on_kernel(up_ref, down_ref, plus_ref, minus_ref, up_out, down_out):
    up_out[...] = (up_ref[...].astype(F32) + plus_ref[0].astype(F32)).astype(BF16)
    down_out[...] = (down_ref[...].astype(F32) + minus_ref[0].astype(F32)).astype(BF16)


def pass_on(up, down, plus, minus):
    comps, rows, half = up.shape
    one = pl.BlockSpec((1, rows, half), lambda i: (i, 0, 0))
    first = pl.BlockSpec((1, 1, rows, half), lambda i: (0, i, 0, 0))
    return pl.pallas_call(
        pass_on_kernel,
        out_shape=(shaped(up.shape, BF16), shaped(up.shape, BF16)),
        grid=(comps,),
        in_specs=[one, one, first, first],
        out_specs=(one, one),
        compiler_params=params(32),
        cost_estimate=cost(2 * up.size, up.size * 12),
        name="pass_on",
    )(up, down, plus, minus)


def ring_sum_kernel(own_ref, plus_ref, minus_ref, up_ref, down_ref, out_ref):
    half = up_ref.shape[2]
    low = own_ref[0, :, :half].astype(F32) + minus_ref[0, 0].astype(F32) + up_ref[0].astype(F32)
    high = own_ref[0, :, half:].astype(F32) + plus_ref[0, 0].astype(F32) + down_ref[0].astype(F32)
    out_ref[0, :, :half] = low.astype(BF16)
    out_ref[0, :, half:] = high.astype(BF16)


def ring_sum(own, plus, minus, up, down):
    comps, rows, width = own.shape
    one = lambda n: pl.BlockSpec((1, rows, n), lambda i: (i, 0, 0))
    second = pl.BlockSpec((1, 1, rows, width // 2), lambda i: (1, i, 0, 0))
    return pl.pallas_call(
        ring_sum_kernel,
        out_shape=shaped(own.shape, BF16),
        grid=(comps,),
        in_specs=[one(width), second, second, one(width // 2), one(width // 2)],
        out_specs=one(width),
        compiler_params=params(32),
        cost_estimate=cost(2 * own.size, own.size * 8),
        name="ring_sum",
    )(own, plus, minus, up, down)


def gather_rows_kernel(first, lists_ref, own_ref, got_ref, rim_in_ref, out_ref, rim_ref):
    rows = own_ref.shape[1]
    width = own_ref.shape[2]
    if rows == out_ref.shape[1]:
        half = rows // 2
        own = own_ref[0].astype(F32)
        got = got_ref[0].astype(F32)
        out_ref[0, :half, :] = (own[:half] + got[half:]).astype(BF16)
        out_ref[0, half:, :] = (own[half:] + got[:half]).astype(BF16)
    else:
        out_ref[0, :rows, :] = own_ref[0]
        out_ref[0, rows:, :] = got_ref[0]
    node = lax.broadcasted_iota(jnp.int32, (width, lists_ref.shape[1]), 0)
    pick = jnp.where(node == lists_ref[...] - first, 1.0, 0.0).astype(BF16)
    rim = jnp.dot(out_ref[0], pick, preferred_element_type=F32)
    if rim_in_ref is not None:
        rim = rim + rim_in_ref[0].astype(F32)
    rim_ref[0] = rim.astype(BF16)


def gather_rows(lists, own, got, rim, chunk):
    comps, rows, width = own.shape
    full = rows if rim is not None else 2 * rows
    count = lists.shape[1]
    one = lambda r, n: pl.BlockSpec((1, r, n), lambda i: (i, 0, 0))
    kernel = functools.partial(gather_rows_kernel, chunk * width)
    if rim is None:
        kernel = lambda l, a, b, o, r: gather_rows_kernel(chunk * width, l, a, b, None, o, r)
    specs = [pl.BlockSpec((1, count), lambda i: (0, 0)), one(rows, width), one(rows, width)]
    args = [lists, own, got]
    if rim is not None:
        specs.append(one(full, count))
        args.append(rim)
    return pl.pallas_call(
        kernel,
        out_shape=(shaped((comps, full, width), BF16), shaped((comps, full, count), BF16)),
        grid=(comps,),
        in_specs=specs,
        out_specs=(one(full, width), one(full, count)),
        compiler_params=params(32),
        cost_estimate=cost(2 * comps * full * width * count, comps * full * width * 6),
        name="gather_rows",
    )(*args)


NODE_BLOCK = 256
ROWS = 16
LANES = 128


def write_weights(first, conn_ref, grads_ref, out_ref, nodes, start, width):
    corners = conn_ref.shape[0]
    base = lax.broadcasted_iota(jnp.int32, (ROWS, LANES), 0).astype(F32).astype(BF16)
    zero = jnp.zeros((ROWS, LANES), BF16)
    for piece in range(width // LANES):
        cut = pl.ds(start + piece * LANES, LANES)
        grads = grads_ref[:, cut].astype(BF16)
        grad = [jnp.broadcast_to(grads[i : i + 1, :], (ROWS, LANES)) for i in range(3 * corners)]
        for part in range(nodes // NODE_BLOCK):
            keys = (conn_ref[:, cut] - (first + part * NODE_BLOCK)).astype(BF16)
            key = [jnp.broadcast_to(keys[a : a + 1, :], (ROWS, LANES)) for a in range(corners)]
            for row in range(NODE_BLOCK // ROWS):
                node = base + BF16(row * ROWS)
                sums = [zero] * 3
                for a in range(corners):
                    hit = node == key[a]
                    for d in range(3):
                        sums[d] = jnp.where(hit, grad[d * corners + a], sums[d])
                for d in range(3):
                    out_ref[d, pl.ds(part * NODE_BLOCK + row * ROWS, ROWS), pl.ds(piece * LANES, LANES)] = sums[d]


def weights_kernel(first, mark_ref, conn_ref, grads_ref, out_ref):
    del mark_ref
    _, nodes, width = out_ref.shape
    start = first + (pl.program_id(1) * nodes).astype(F32)
    write_weights(start, conn_ref, grads_ref, out_ref, nodes, 0, width)


def element_weights(mark, data, first, nodes):
    elems = data.shape[1]
    width = 512
    block = 512
    return pl.pallas_call(
        functools.partial(weights_kernel, first),
        out_shape=shaped((3, nodes, elems), BF16),
        grid=(elems // width, nodes // block),
        in_specs=[
            ANY,
            pl.BlockSpec((8, width), lambda j, i: (0, j)),
            pl.BlockSpec((24, width), lambda j, i: (0, j)),
        ],
        out_specs=pl.BlockSpec((3, block, width), lambda j, i: (0, i, j)),
        compiler_params=params(32),
        cost_estimate=cost(nodes * elems * 1500, 6 * nodes * elems),
        name="element_weights",
    )(mark, data[:8], data[8:32])


def build_multiply_kernel(first, values_ref, conn_ref, grads_ref, *refs):
    acc_ref, out_ref, weights = refs if len(refs) == 3 else (None,) + refs
    width = out_ref.shape[2]
    nodes = weights.shape[2]
    comps, rows, _ = values_ref.shape
    values = values_ref[...].reshape(comps * rows, nodes)
    piece = weights.shape[3]
    for at in range(width // piece):
        slot = at % weights.shape[0]
        cut = pl.ds(at * piece, piece)
        write_weights(first, conn_ref, grads_ref, weights.at[slot], nodes, at * piece, piece)
        for d in range(3):
            term = jnp.dot(values, weights[slot, d], preferred_element_type=F32)
            if acc_ref is not None:
                term = term + acc_ref[d, :, cut]
            out_ref[d, :, cut] = term


def build_multiply(values, data, acc, first):
    comps, rows, nodes = values.shape
    elems = data.shape[1]
    width = 512
    total = comps * rows
    block = pl.BlockSpec((3, total, width), lambda j: (0, 0, j))
    specs = [
        pl.BlockSpec((comps, rows, nodes), lambda j: (0, 0, 0)),
        pl.BlockSpec((8, width), lambda j: (0, j)),
        pl.BlockSpec((24, width), lambda j: (0, j)),
    ]
    args = [values, data[:8], data[8:32]]
    if acc is not None:
        specs.append(block)
        args.append(acc)
    return pl.pallas_call(
        functools.partial(build_multiply_kernel, float(first)),
        out_shape=shaped((3, total, elems), F32),
        grid=(elems // width,),
        in_specs=specs,
        out_specs=block,
        scratch_shapes=[pltpu.VMEM((2, 3, nodes, 256), BF16)],
        input_output_aliases={} if acc is None else {3: 0},
        compiler_params=params(40),
        cost_estimate=cost(nodes * elems * 1500, 24 * total * elems),
        name="build_multiply",
    )(*args)


def multiply_kernel(values_ref, weights_ref, acc_ref, out_ref):
    comps, rows, nodes = values_ref.shape
    values = values_ref[...].reshape(comps * rows, nodes)
    for d in range(3):
        out_ref[d] = acc_ref[d] + jnp.dot(values, weights_ref[d], preferred_element_type=F32)


def multiply(values, weights, acc):
    comps, rows, nodes = values.shape
    elems = weights.shape[2]
    width = 512
    block = pl.BlockSpec((3, comps * rows, width), lambda j: (0, 0, j))
    return pl.pallas_call(
        multiply_kernel,
        out_shape=shaped(acc.shape, F32),
        grid=(elems // width,),
        in_specs=[
            pl.BlockSpec((comps, rows, nodes), lambda j: (0, 0, 0)),
            pl.BlockSpec((3, nodes, width), lambda j: (0, 0, j)),
            block,
        ],
        out_specs=block,
        input_output_aliases={2: 0},
        compiler_params=params(40),
        cost_estimate=cost(6 * comps * rows * nodes * elems, 6 * nodes * elems),
        name="multiply",
    )(values, weights, acc)


def spectra_kernel(before_ref, after_ref, weights_ref, acc_ref, modulus_ref, out_ref):
    comps, rows, rim = before_ref.shape
    width = out_ref.shape[2]
    half = rows // 4
    before = before_ref[...].reshape(comps * rows, rim)
    after = after_ref[...].reshape(comps * rows, rim)
    modulus = modulus_ref[:1, :]
    lame = modulus * (POISSON / ((1.0 + POISSON) * (1.0 - 2.0 * POISSON)))
    shear = modulus * (1.0 / (2.0 * (1.0 + POISSON)))
    grads = []
    for d in range(3):
        grads.append(
            acc_ref[d]
            + jnp.dot(before, weights_ref[d, :rim, :], preferred_element_type=F32)
            + jnp.dot(after, weights_ref[d, rim:, :], preferred_element_type=F32)
        )
    real = [[None] * 6 for _ in range(6)]
    imag = [[None] * 6 for _ in range(6)]

    def add(store, i, j, value):
        store[i][j] = value if store[i][j] is None else store[i][j] + value

    def stress(top):
        def at(c, d):
            return grads[d][c * rows + top : c * rows + top + 8, :]

        volume = lame * (at(0, 0) + at(1, 1) + at(2, 2))
        twice = 2.0 * shear
        return [
            volume + twice * at(0, 0),
            volume + twice * at(1, 1),
            volume + twice * at(2, 2),
            shear * (at(1, 2) + at(2, 1)),
            shear * (at(2, 0) + at(0, 2)),
            shear * (at(0, 1) + at(1, 0)),
        ]

    for side in range(2):
        for part in range(half // 8):
            re = stress(side * 2 * half + part * 8)
            im = stress(side * 2 * half + half + part * 8)
            for i in range(6):
                for j in range(i, 6):
                    add(real, i, j, re[i] * re[j] + im[i] * im[j])
                for j in range(i + 1, 6):
                    add(imag, i, j, im[i] * re[j] - re[i] * im[j])
    entry = 0
    for i in range(6):
        for j in range(i, 6):
            out_ref[0, entry : entry + 1, :] = jnp.sum(real[i][j], axis=0, keepdims=True)
            entry += 1
    for i in range(6):
        for j in range(i + 1, 6):
            out_ref[0, entry : entry + 1, :] = jnp.sum(imag[i][j], axis=0, keepdims=True)
            entry += 1


def element_spectra(before, after, weights, acc, modulus):
    comps, rows, rim = before.shape
    elems = weights.shape[2]
    width = 256
    per = elems // Z // width
    whole = lambda i: (0, 0, 0)
    return pl.pallas_call(
        spectra_kernel,
        out_shape=shaped((Z, 36, elems // Z), F32),
        grid=(elems // width,),
        in_specs=[
            pl.BlockSpec((comps, rows, rim), whole),
            pl.BlockSpec((comps, rows, rim), whole),
            pl.BlockSpec((3, 2 * rim, width), lambda i: (0, 0, i)),
            pl.BlockSpec((3, comps * rows, width), lambda i: (0, 0, i)),
            pl.BlockSpec((8, width), lambda i: (0, i)),
        ],
        out_specs=pl.BlockSpec((1, 36, width), lambda i: (i // per, 0, i % per)),
        compiler_params=params(40),
        cost_estimate=cost(12 * comps * rows * rim * elems, 24 * comps * rows * elems),
        name="element_spectra",
    )(before, after, weights, acc, modulus)


def local(
    mode_shapes,
    load_nodal,
    mode_freq,
    damping,
    drive_freq,
    send_lists,
    connectivity,
    shape_grads,
    modulus,
):
    modes, _, nodes = mode_shapes.shape
    cols = load_nodal.shape[2]
    bound = send_lists.shape[1]
    freqs = drive_freq.shape[0]
    rows = cols // (Z * XLO)
    mode_at = lax.axis_index("mode")
    z_at, x_at = mode_at // XLO, mode_at % XLO
    core = (lax.axis_index("mesh") % CORE).astype(jnp.int32)
    core_arg = core.reshape(1)
    shapes = jnp.transpose(mode_shapes, (1, 0, 2))
    lists = send_lists.reshape(1, -1)

    pad = 2 * HALF - modes
    natural = jnp.pad(mode_freq, (0, pad), constant_values=1.0)[:, None]
    loss = jnp.pad(damping, (0, pad), constant_values=0.5)[:, None]
    natural = lax.dynamic_slice_in_dim(natural, core * HALF, HALF)
    loss = lax.dynamic_slice_in_dim(loss, core * HALF, HALF)
    forcing = jnp.repeat(drive_freq, cols // freqs)[None, :]
    gap = natural * natural - forcing * forcing
    damp = 2.0 * loss * natural * forcing
    size = gap * gap + damp * damp
    sign = jnp.where(jnp.arange(cols) % 2 == 0, 1.0, -1.0).astype(F32)[None, :]
    direct = gap / size
    cross = sign * (damp / size)

    spot = jnp.arange(cols)
    block, inside = spot // rows, spot % rows
    block = mode_index(z_at + block // XLO, x_at ^ (block % XLO))
    source = block * rows + 2 * (inside % (rows // 2)) + inside // (rows // 2)
    order = (source[:, None] == spot[None, :]).astype(BF16)

    mine, theirs = partial_loads(core_arg, shapes, load_nodal)
    got = lax.ppermute(theirs, "mesh", mesh_perm(0, 0, 1))
    chip = (mine + got.astype(F32)).astype(BF16)
    got = lax.ppermute(chip, "mesh", mesh_perm(0, 1, 0))
    pair = (chip.astype(F32) + got.astype(F32)).astype(BF16)
    ring = [pair] + [lax.ppermute(pair, "mesh", mesh_perm(dy)) for dy in range(1, Y)]

    data = element_data(theirs, connectivity, shape_grads, modulus)
    data = jnp.concatenate(
        [data] + [lax.ppermute(data, "mode", mode_perm(-j)) for j in range(1, Z)], axis=1
    )
    rim_weights = element_weights(pair, data, float(nodes), 2 * bound)

    resp_mine = half_response(ring, direct, cross)
    resp_theirs = lax.ppermute(resp_mine, "mesh", mesh_perm(0, 0, 1))

    chunks = nodes // CHUNK
    up_perm, down_perm, side_perm = mode_perm(1), mode_perm(-1), mode_perm(0, 1)
    away, keep, resp = x_first_terms(core_arg, resp_mine, resp_theirs, order, shapes, 0)
    got = lax.ppermute(away, "mode", side_perm)

    def first_hop(ways):
        return lax.ppermute(ways[0], "mode", up_perm), lax.ppermute(ways[1], "mode", down_perm)

    def second_hop(ways, plus, minus):
        up, down = pass_on(ways[2], ways[3], plus, minus)
        return up, lax.ppermute(up, "mode", up_perm), lax.ppermute(down, "mode", down_perm)

    ways_1 = z_first_terms(resp, resp, shapes, 1)
    plus_1, minus_1 = first_hop(ways_1)
    ways_2 = z_first_terms(ways_1[2], resp, shapes, 2)
    plus_2, minus_2 = first_hop(ways_2)
    last_weights = element_weights(ways_2[2], data, float((chunks - 1) * CHUNK), CHUNK)
    sent_1, up_1, down_1 = second_hop(ways_1, plus_1, minus_1)
    ways_0 = x_sum(keep, got)
    plus_0, minus_0 = first_hop(ways_0)
    ways_3 = z_first_terms(sent_1, resp, shapes, 3)
    own_1 = ring_sum(ways_1[4], plus_1, minus_1, up_1, down_1)
    side_1 = lax.ppermute(own_1, "mode", side_perm)
    _, up_2, down_2 = second_hop(ways_2, plus_2, minus_2)
    plus_3, minus_3 = first_hop(ways_3)
    own_2 = ring_sum(ways_2[4], plus_2, minus_2, up_2, down_2)
    side_2 = lax.ppermute(own_2, "mode", side_perm)
    _, up_0, down_0 = second_hop(ways_0, plus_0, minus_0)
    own_0 = ring_sum(ways_0[4], plus_0, minus_0, up_0, down_0)
    side_0 = lax.ppermute(own_0, "mode", side_perm)
    _, up_3, down_3 = second_hop(ways_3, plus_3, minus_3)
    own_3 = ring_sum(ways_3[4], plus_3, minus_3, up_3, down_3)
    side_3 = lax.ppermute(own_3, "mode", side_perm)

    values_0, rim = gather_rows(lists, own_0, side_0, None, 0)
    values_1, rim = gather_rows(lists, own_1, side_1, rim, 1)
    values_2, rim = gather_rows(lists, own_2, side_2, rim, 2)
    acc = build_multiply(values_1, data, None, CHUNK)
    acc = build_multiply(values_2, data, acc, 2 * CHUNK)
    acc = build_multiply(values_0, data, acc, 0)
    values_3, rim = gather_rows(lists, own_3, side_3, rim, 3)

    count = lax.axis_size("mesh")
    before = lax.ppermute(rim[..., bound:], "mesh", [(p, p + 1) for p in range(count - 1)])
    after = lax.ppermute(rim[..., :bound], "mesh", [(p + 1, p) for p in range(count - 1)])
    acc = multiply(values_3, last_weights, acc)
    spectra = element_spectra(before, after, rim_weights, acc, data[32:40])
    back = [spectra[0]] + [lax.ppermute(spectra[j], "mode", mode_perm(j)) for j in range(1, Z)]
    back = jnp.stack(back)
    return jnp.take(back, (z_at - jnp.arange(Z)) % Z, axis=0)


def solution(mesh):
    in_specs = (
        P("mode", None, "mesh"),
        P(None, "mesh", None),
        P("mode"),
        P("mode"),
        P(),
        P(None, "mesh"),
        P(None, ("mesh", "mode")),
        P(None, None, ("mesh", "mode")),
        P(("mesh", "mode")),
    )
    out_specs = P(None, None, ("mesh", "mode"))
    return jax.shard_map(local, mesh=mesh, in_specs=in_specs, out_specs=out_specs, check_vma=False)
```

time: 293 us -> 211 us (0.72)
  waiting for transfers between devices: 129 us -> 50.7 us
  starting transfers between devices: 37.3 us -> 54.7 us
  local copies, waits for them, and re-layouts: 18 us -> 6.3 us
  other arithmetic: 6.19 us -> 1.7 us
  Pallas kernels: 99.4 us -> 95.8 us
    ppermute x8 -> x26, waiting for transfers between devices: 107 us -> 35.3 us  [the longest x4 17.8 us: first_hop(): lax.ppermute(ways[0], 'mode', up_perm)]
    ppermute x8 -> x26, starting transfers between devices: 20.5 us -> 39 us  [the longest x1 11.7 us: local(): lax.ppermute(rim[..., bound:], 'mesh', [(p, p + 1) for p in range(count -...]
    unnamed x23 -> x27, local copies, waits for them, and re-layouts: 16.4 us -> 4.61 us
    all_to_all x1 -> x0, starting transfers between devices: 6.1 us -> none  [local(): terms = lax.all_to_all(terms, 'mode', 0, 0)]
    reduce_sum x1 -> x0, other arithmetic: 5.45 us -> none  [local(): jnp.sum(terms.astype(F32), axis=0).astype(BF16).reshape(comps * rows, nodes)]
    ppermute x3, waiting for transfers between devices: 11.3 us -> 6.68 us  [local(): lax.ppermute(pair, 'mesh', mesh_perm(dy))]
    pallas_call x5 -> x27, Pallas kernels: 99.4 us -> 95.8 us  [the longest x3 32 us: build_multiply(): pl.pallas_call(functools.partial(build_multiply_kernel, float(first)), ou...]
  transfers between devices with their start and end apart: 18 -> 35, of which waited for: 12 -> 17; matrix products, arithmetic and copies ran while one was open for 1% -> 0% of each run, Pallas kernels for 19% -> 33%
where the time goes in v2:
time: 211 us; the launch traced here: 210 us
  Pallas kernels  95.8 us (45%)
  starting transfers between devices  54.7 us (26%)
  waiting for transfers between devices  50.7 us (24%)
  local copies, waits for them, and re-layouts  6.3 us (3%)
    pallas_call x3, Pallas kernels, build_multiply(): pl.pallas_call(functools.partial(build_multiply_kernel, float(first)), ou...  32 us
    ppermute x4, waiting for transfers between devices, first_hop(): lax.ppermute(ways[0], 'mode', up_perm)  17.8 us
    pallas_call x3, Pallas kernels, z_first_terms(): pl.pallas_call(z_first_kernel, out_shape=out_shape, grid=(comps,), in_spe...  13.6 us
    pallas_call x1, Pallas kernels, partial_loads(): pl.pallas_call(loads_kernel, out_shape=(shaped((HALF, cols), F32), shaped...  12.5 us
    ppermute x3, waiting for transfers between devices, local(): lax.ppermute(data, 'mode', mode_perm(-j))  11.7 us
    ppermute x1, starting transfers between devices, local(): lax.ppermute(rim[..., bound:], 'mesh', [(p, p + 1) for p in range(count -...  11.7 us
    pallas_call x2, Pallas kernels, element_weights(): pl.pallas_call(functools.partial(weights_kernel, first), out_shape=shaped...  10.1 us
    pallas_call x1, Pallas kernels, element_spectra(): pl.pallas_call(spectra_kernel, out_shape=shaped((Z, 36, elems // Z), F32)...  7.71 us
  transfers between devices with their start and end apart: 35, of which 17 were waited for; matrix products, arithmetic and copies ran while one was open for 0% of the time, Pallas kernels for 33%

profile of v2, /device:TPU:1, one launch (start us, length us, event | category | flops | bytes accessed | tf_op | source)
XLA Modules:
  0.0 209.6 jit_solution(10648587518652154604)
XLA Ops:
  0.0 12.5 %modal_loads.1 = (f32[256,384]{1,0:T(8,128)}, bf16[256,384]{1,0:T(8,128)(2,1)}) custom-call(s32[1]{0:T(128)} %bitcast.core_ref, bf16[3,500,4096]{2,1,0:T(8,128)(2,1)} %bitcast.22, bf16[3,4096,384]{2,1,0:T(8,128)(2,1)} %load_ref.1), custom_call_target="tpu_custom_call" | custom-call | flops 4718592000 | bytes 21725184 | tf_op jit(solution)/shard_map/modal_loads/pallas_call | solution.py:77
  16.2 2.9 %collective-permute-start.1 = (bf16[256,384]{1,0:T(8,128)(2,1)S(1)}, bf16[256,384]{1,0:T(8,128)(2,1)S(1)}, u32[]{:S(2)}, u32[]{:S(2)}) collective-permute-start(bf16[256,384]{1,0:T(8,128)(2,1)S(1)} %add_convert_fusion.1), channel_id=1, source_target_pairs={{0,16},{8,24},{16,0},{24,8},{32,48},{40,56},{48,32},{56,40},{64,80... | collective-permute-start | bytes 589832 | tf_op jit(solution)/shard_map/ppermute | solution.py:621
  19.3 4.7 %collective-permute-done.1 = bf16[256,384]{1,0:T(8,128)(2,1)S(1)} collective-permute-done((bf16[256,384]{1,0:T(8,128)(2,1)S(1)}, bf16[256,384]{1,0:T(8,128)(2,1)S(1)}, u32[]{:S(2)}, u32[]{:S(2)}) %collective-permute-start.1) | collective-permute-done | bytes 196640 | tf_op jit(solution)/shard_map/ppermute | solution.py:621
  30.7 5.2 %collective-permute-done.3.c_ref = bf16[256,384]{1,0:T(8,128)(2,1)S(1)} collective-permute-done((bf16[256,384]{1,0:T(8,128)(2,1)S(1)}, bf16[256,384]{1,0:T(8,128)(2,1)S(1)}, u32[]{:S(2)}, u32[]{:S(2)}) %collective-permute-start.3) | collective-permute-done | bytes 196640 | tf_op jit(solution)/shard_map/ppermute | solution.py:623
  39.6 5.3 %x_first_terms.1 = (bf16[4,3,48,1024]{3,2,1,0:T(8,128)(2,1)}, bf16[4,3,48,1024]{3,2,1,0:T(8,128)(2,1)}, bf16[384,500]{1,0:T(8,128)(2,1)S(1)}) custom-call(s32[1]{0:T(128)} %bitcast.core_ref, bf16[256,384]{1,0:T(8,128)(2,1)S(1)} %modal_response.1.mine_ref, bf16[256,384]{1,0:T(8,128)(2,1)S(1)} %collective-permute-done.5.theirs_ref, ...), custom_call_target="tpu_custom_call" | custom-call | flops 1179648000 | bytes 5431296 | tf_op jit(solution)/shard_map/x_first_terms/pallas_call | solution.py:231
  46.1 4.5 %z_first_terms.3 = (bf16[2,3,96,512]{3,2,1,0:T(8,128)(2,1)S(1)}, bf16[2,3,96,512]{3,2,1,0:T(8,128)(2,1)}, bf16[3,96,512]{2,1,0:T(8,128)(2,1)S(1)}, bf16[3,96,512]{2,1,0:T(8,128)(2,1)S(1)}, bf16[3,96,1024]{2,1,0:T(8,128)(2,1)}) custom-call(bf16[384,500]{1,0:T(8,128)(2,1)S(1)} %get-tuple-element.48.mark_ref.resp_ref, ...), custom_call_target="tpu_custom_call" | custom-call | flops 1179648000 | bytes 5431296 | tf_op jit(solution)/shard_map/z_first_terms/pallas_call | solution.py:189
  54.5 4.6 %z_first_terms.5 = (bf16[2,3,96,512]{3,2,1,0:T(8,128)(2,1)S(1)}, bf16[2,3,96,512]{3,2,1,0:T(8,128)(2,1)}, bf16[3,96,512]{2,1,0:T(8,128)(2,1)S(1)}, bf16[3,96,512]{2,1,0:T(8,128)(2,1)S(1)}, bf16[3,96,1024]{2,1,0:T(8,128)(2,1)}) custom-call(bf16[3,96,512]{2,1,0:T(8,128)(2,1)S(1)} %get-tuple-element.49.up_ref.mark_ref, ...), custom_call_target="tpu_custom_call" | custom-call | flops 1179648000 | bytes 5431296 | tf_op jit(solution)/shard_map/z_first_terms/pallas_call | solution.py:189
  59.1 2.7 %collective-permute-start.14 = (bf16[2,3,96,512]{3,2,1,0:T(8,128)(2,1)}, bf16[2,3,96,512]{3,2,1,0:T(8,128)(2,1)S(1)}, u32[]{:S(2)}, u32[]{:S(2)}) collective-permute-start(bf16[2,3,96,512]{3,2,1,0:T(8,128)(2,1)} %get-tuple-element.63), channel_id=1, source_target_pairs={{0,6},{1,7},{2,0},{3,1},{4,2},{5,3},{6,4},{7,5},{8,14},{9,15},{10,... | collective-permute-start | bytes 1769480 | tf_op jit(solution)/shard_map/ppermute | solution.py:640
  61.9 5.6 %collective-permute-done.6.plus_ref = bf16[2,3,96,512]{3,2,1,0:T(8,128)(2,1)S(1)} collective-permute-done((bf16[2,3,96,512]{3,2,1,0:T(8,128)(2,1)S(1)}, bf16[2,3,96,512]{3,2,1,0:T(8,128)(2,1)S(1)}, u32[]{:S(2)}, u32[]{:S(2)}) %collective-permute-start.6) | collective-permute-done | bytes 589856 | tf_op jit(solution)/shard_map/ppermute | solution.py:640
  74.5 5.6 %collective-permute-done.13.plus_ref = bf16[2,3,96,512]{3,2,1,0:T(8,128)(2,1)S(1)} collective-permute-done((bf16[2,3,96,512]{3,2,1,0:T(8,128)(2,1)S(1)}, bf16[2,3,96,512]{3,2,1,0:T(8,128)(2,1)S(1)}, u32[]{:S(2)}, u32[]{:S(2)}) %collective-permute-start.13) | collective-permute-done | bytes 589856 | tf_op jit(solution)/shard_map/ppermute | solution.py:640
  82.6 5.4 %collective-permute-done.29 = f32[40,512]{1,0:T(8,128)S(1)} collective-permute-done((f32[40,512]{1,0:T(8,128)S(1)}, f32[40,512]{1,0:T(8,128)S(1)}, u32[]{:S(2)}, u32[]{:S(2)}) %collective-permute-start.29) | collective-permute-done | bytes 81952 | tf_op jit(solution)/shard_map/ppermute | solution.py:627
  88.8 6.3 %collective-permute-done.30 = f32[40,512]{1,0:T(8,128)S(1)} collective-permute-done((f32[40,512]{1,0:T(8,128)S(1)}, f32[40,512]{1,0:T(8,128)S(1)}, u32[]{:S(2)}, u32[]{:S(2)}) %collective-permute-start.30) | collective-permute-done | bytes 81952 | tf_op jit(solution)/shard_map/ppermute | solution.py:627
  95.1 4.5 %z_first_terms.4 = (bf16[2,3,96,512]{3,2,1,0:T(8,128)(2,1)S(1)}, bf16[2,3,96,512]{3,2,1,0:T(8,128)(2,1)}, bf16[3,96,512]{2,1,0:T(8,128)(2,1)S(1)}, bf16[3,96,512]{2,1,0:T(8,128)(2,1)S(1)}, bf16[3,96,1024]{2,1,0:T(8,128)(2,1)}) custom-call(bf16[3,96,512]{2,1,0:T(8,128)(2,1)S(1)} %get-tuple-element.53.mark_ref, ...), custom_call_target="tpu_custom_call" | custom-call | flops 1179648000 | bytes 5431296 | tf_op jit(solution)/shard_map/z_first_terms/pallas_call | solution.py:189
  109.2 3.3 %element_weights.2.weights_ref = bf16[3,512,2048]{2,1,0:T(8,128)(2,1)S(1)} custom-call(bf16[256,384]{1,0:T(8,128)(2,1)S(1)} %add_convert_fusion.a_ref.mark_ref, f32[8,2048]{1,0:T(8,128)S(1)} %get-tuple-element.92.conn_ref, f32[24,2048]{1,0:T(8,128)S(1)} %slice.46.grads_ref), custom_call_target="tpu_custom_call" | custom-call | flops 1572864000 | bytes 6291456 | tf_op jit(solution)/shard_map/element_weights/pallas_call | solution.py:403
  112.8 6.5 %collective-permute-done.8.plus_ref = bf16[2,3,96,512]{3,2,1,0:T(8,128)(2,1)S(1)} collective-permute-done((bf16[2,3,96,512]{3,2,1,0:T(8,128)(2,1)S(1)}, bf16[2,3,96,512]{3,2,1,0:T(8,128)(2,1)S(1)}, u32[]{:S(2)}, u32[]{:S(2)}) %collective-permute-start.8) | collective-permute-done | bytes 589856 | tf_op jit(solution)/shard_map/ppermute | solution.py:640
  119.9 2.6 %collective-permute-done.24.up_ref = bf16[3,48,512]{2,1,0:T(8,128)(2,1)S(1)} collective-permute-done((bf16[3,48,512]{2,1,0:T(8,128)(2,1)S(1)}, bf16[3,48,512]{2,1,0:T(8,128)(2,1)S(1)}, u32[]{:S(2)}, u32[]{:S(2)}) %collective-permute-start.24) | collective-permute-done | bytes 147488 | tf_op jit(solution)/shard_map/ppermute | solution.py:644
  124.0 6.7 %element_weights.3.weights_ref = bf16[3,1024,2048]{2,1,0:T(8,128)(2,1)S(1)} custom-call(bf16[3,96,512]{2,1,0:T(8,128)(2,1)S(1)} %get-tuple-element.64.up_ref.mark_ref, f32[8,2048]{1,0:T(8,128)S(1)} %get-tuple-element.92.conn_ref, f32[24,2048]{1,0:T(8,128)S(1)} %slice.46.grads_ref), custom_call_target="tpu_custom_call" | custom-call | flops 3145728000 | bytes 12582912 | tf_op jit(solution)/shard_map/element_weights/pallas_call | solution.py:403
  130.7 4.6 %copy-done = bf16[3,1024,2048]{2,1,0:T(8,128)(2,1)} copy-done((bf16[3,1024,2048]{2,1,0:T(8,128)(2,1)}, bf16[3,1024,2048]{2,1,0:T(8,128)(2,1)S(1)}, u32[]{:S(2)}) %copy-start) | copy-done | bytes 12582936
  138.5 10.1 %build_multiply.3.refs_0_ = f32[3,288,2048]{2,1,0:T(8,128)S(1)} custom-call(bf16[3,96,1024]{2,1,0:T(8,128)(2,1)S(1)} %get-tuple-element.86.values_ref, f32[8,2048]{1,0:T(8,128)S(1)} %get-tuple-element.92.conn_ref, f32[24,2048]{1,0:T(8,128)S(1)} %slice.46.grads_ref), custom_call_target="tpu_custom_call" | custom-call | flops 3145728000 | bytes 14155776 | tf_op jit(solution)/shard_map/build_multiply/pallas_call | solution.py:452
  149.8 11.0 %build_multiply.4.refs_0_ = f32[3,288,2048]{2,1,0:T(8,128)S(1)} custom-call(bf16[3,96,1024]{2,1,0:T(8,128)(2,1)S(1)} %get-tuple-element.85.values_ref, f32[8,2048]{1,0:T(8,128)S(1)} %get-tuple-element.92.conn_ref, f32[24,2048]{1,0:T(8,128)S(1)} %slice.46.grads_ref, f32[3,288,2048]{2,1,0:T(8,128)S(1)} %build_multiply.3.refs_0_), custom_call_target="tpu_custom_call", output_to_operand_aliasing={{}: (3, {})} | custom-call | flops 3145728000 | bytes 14155776 | tf_op jit(solution)/shard_map/build_multiply/pallas_call | solution.py:452
  160.7 11.0 %build_multiply.5.acc_ref = f32[3,288,2048]{2,1,0:T(8,128)S(1)} custom-call(bf16[3,96,1024]{2,1,0:T(8,128)(2,1)S(1)} %get-tuple-element.84.values_ref, f32[8,2048]{1,0:T(8,128)S(1)} %get-tuple-element.92.conn_ref, f32[24,2048]{1,0:T(8,128)S(1)} %slice.46.grads_ref, f32[3,288,2048]{2,1,0:T(8,128)S(1)} %build_multiply.4.refs_0_), custom_call_target="tpu_custom_call", output_to_operand_aliasing={{}: (3, {})} | custom-call | flops 3145728000 | bytes 14155776 | tf_op jit(solution)/shard_map/build_multiply/pallas_call | solution.py:452
  172.9 11.7 %collective-permute-start.27 = (bf16[3,96,256]{2,1,0:T(8,128)(2,1)S(1)}, bf16[3,96,256]{2,1,0:T(8,128)(2,1)S(1)}, u32[]{:S(2)}, u32[]{:S(2)}) collective-permute-start(bf16[3,96,256]{2,1,0:T(8,128)(2,1)S(1)} %get-tuple-element.94), channel_id=1, source_target_pairs={{0,8},{8,16},{16,24},{24,32},{32,40},{40,48},{48,56},{56,64},{64,7... | collective-permute-start | bytes 442376 | tf_op jit(solution)/shard_map/ppermute | solution.py:677
  186.6 7.7 %multiply.1.acc_ref = f32[3,288,2048]{2,1,0:T(8,128)S(1)} custom-call(bf16[3,96,1024]{2,1,0:T(8,128)(2,1)S(1)} %get-tuple-element.83.values_ref, bf16[3,1024,2048]{2,1,0:T(8,128)(2,1)} %copy-done, f32[3,288,2048]{2,1,0:T(8,128)S(1)} %build_multiply.5.acc_ref), custom_call_target="tpu_custom_call", output_to_operand_aliasing={{}: (2, {})} | custom-call | flops 3623878656 | bytes 12582912 | tf_op jit(solution)/shard_map/multiply/pallas_call | solution.py:478
  194.3 7.7 %element_spectra.1 = f32[4,36,512]{2,1,0:T(8,128)S(1)} custom-call(bf16[3,96,256]{2,1,0:T(8,128)(2,1)S(1)} %collective-permute-done.27.before_ref, bf16[3,96,256]{2,1,0:T(8,128)(2,1)S(1)} %collective-permute-done.28.after_ref, bf16[3,512,2048]{2,1,0:T(8,128)(2,1)S(1)} %element_weights.2.weights_ref, f32[3,288,2048]{2,1,0:T(8,128)S(1)} %multiply.1.acc_ref, ...), custom_call_target="tpu_custom_call" | custom-call | flops 1811939328 | bytes 14155776 | tf_op jit(solution)/shard_map/element_spectra/pallas_call | solution.py:558
  (122 shorter events, 56.6 us)
Async XLA Ops:
  25.4 10.6 %collective-permute-start.3 = (bf16[256,384]{1,0:T(8,128)(2,1)S(1)}, bf16[256,384]{1,0:T(8,128)(2,1)S(1)}, u32[]{:S(2)}, u32[]{:S(2)}) collective-permute-start(bf16[256,384]{1,0:T(8,128)(2,1)S(1)} %add_convert_fusion.a_ref.mark_ref), channel_id=1, source_target_pairs={{0,64},{8,72},{16,80},{24,88},{32,96},{40,104},{48,112},{56,120},{... | collective-permute-start | bytes 589832 | tf_op jit(solution)/shard_map/ppermute | solution.py:623
  44.8 27.4 %collective-permute-start.21 = (bf16[4,3,48,1024]{3,2,1,0:T(8,128)(2,1)}, bf16[4,3,48,1024]{3,2,1,0:T(8,128)(2,1)S(1)}, u32[]{:S(2)}, u32[]{:S(2)}) collective-permute-start(bf16[4,3,48,1024]{3,2,1,0:T(8,128)(2,1)} %get-tuple-element.71), channel_id=1, source_target_pairs={{0,1},{1,0},{2,3},{3,2},{4,5},{5,4},{6,7},{7,6},{8,9},{9,8},{10,11... | collective-permute-start | bytes 3538952 | tf_op jit(solution)/shard_map/ppermute | solution.py:637
  50.6 16.9 %collective-permute-start.6 = (bf16[2,3,96,512]{3,2,1,0:T(8,128)(2,1)S(1)}, bf16[2,3,96,512]{3,2,1,0:T(8,128)(2,1)S(1)}, u32[]{:S(2)}, u32[]{:S(2)}) collective-permute-start(bf16[2,3,96,512]{3,2,1,0:T(8,128)(2,1)S(1)} %get-tuple-element.51), channel_id=1, source_target_pairs={{0,2},{1,3},{2,4},{3,5},{4,6},{5,7},{6,0},{7,1},{8,10},{9,11},{10,... | collective-permute-start | bytes 1769480 | tf_op jit(solution)/shard_map/ppermute | solution.py:640
  52.3 15.2 %collective-permute-start.7 = (bf16[2,3,96,512]{3,2,1,0:T(8,128)(2,1)}, bf16[2,3,96,512]{3,2,1,0:T(8,128)(2,1)S(1)}, u32[]{:S(2)}, u32[]{:S(2)}) collective-permute-start(bf16[2,3,96,512]{3,2,1,0:T(8,128)(2,1)} %get-tuple-element.52), channel_id=1, source_target_pairs={{0,6},{1,7},{2,0},{3,1},{4,2},{5,3},{6,4},{7,5},{8,14},{9,15},{10,... | collective-permute-start | bytes 1769480 | tf_op jit(solution)/shard_map/ppermute | solution.py:640
  59.1 21.1 %collective-permute-start.13 = (bf16[2,3,96,512]{3,2,1,0:T(8,128)(2,1)S(1)}, bf16[2,3,96,512]{3,2,1,0:T(8,128)(2,1)S(1)}, u32[]{:S(2)}, u32[]{:S(2)}) collective-permute-start(bf16[2,3,96,512]{3,2,1,0:T(8,128)(2,1)S(1)} %get-tuple-element.62), channel_id=1, source_target_pairs={{0,2},{1,3},{2,4},{3,5},{4,6},{5,7},{6,0},{7,1},{8,10},{9,11},{10,... | collective-permute-start | bytes 1769480 | tf_op jit(solution)/shard_map/ppermute | solution.py:640
  59.1 22.2 %collective-permute-start.14 = (bf16[2,3,96,512]{3,2,1,0:T(8,128)(2,1)}, bf16[2,3,96,512]{3,2,1,0:T(8,128)(2,1)S(1)}, u32[]{:S(2)}, u32[]{:S(2)}) collective-permute-start(bf16[2,3,96,512]{3,2,1,0:T(8,128)(2,1)} %get-tuple-element.63), channel_id=1, source_target_pairs={{0,6},{1,7},{2,0},{3,1},{4,2},{5,3},{6,4},{7,5},{8,14},{9,15},{10,... | collective-permute-start | bytes 1769480 | tf_op jit(solution)/shard_map/ppermute | solution.py:640
  67.7 33.5 %collective-permute-start.18 = (bf16[3,96,512]{2,1,0:T(8,128)(2,1)S(1)}, bf16[3,96,512]{2,1,0:T(8,128)(2,1)S(1)}, u32[]{:S(2)}, u32[]{:S(2)}) collective-permute-start(bf16[3,96,512]{2,1,0:T(8,128)(2,1)S(1)} %get-tuple-element.53.mark_ref), channel_id=1, source_target_pairs={{0,2},{1,3},{2,4},{3,5},{4,6},{5,7},{6,0},{7,1},{8,10},{9,11},{10,... | collective-permute-start | bytes 884744 | tf_op jit(solution)/shard_map/ppermute | solution.py:644
  68.3 34.1 %collective-permute-start.19 = (bf16[3,96,512]{2,1,0:T(8,128)(2,1)S(1)}, bf16[3,96,512]{2,1,0:T(8,128)(2,1)S(1)}, u32[]{:S(2)}, u32[]{:S(2)}) collective-permute-start(bf16[3,96,512]{2,1,0:T(8,128)(2,1)S(1)} %get-tuple-element.69), channel_id=1, source_target_pairs={{0,6},{1,7},{2,0},{3,1},{4,2},{5,3},{6,4},{7,5},{8,14},{9,15},{10,... | collective-permute-start | bytes 884744 | tf_op jit(solution)/shard_map/ppermute | solution.py:644
  72.8 29.8 %collective-permute-start.22 = (bf16[2,3,48,512]{3,2,1,0:T(8,128)(2,1)S(1)}, bf16[2,3,48,512]{3,2,1,0:T(8,128)(2,1)S(1)}, u32[]{:S(2)}, u32[]{:S(2)}) collective-permute-start(bf16[2,3,48,512]{3,2,1,0:T(8,128)(2,1)S(1)} %get-tuple-element.73), channel_id=1, source_target_pairs={{0,2},{1,3},{2,4},{3,5},{4,6},{5,7},{6,0},{7,1},{8,10},{9,11},{10,... | collective-permute-start | bytes 884744 | tf_op jit(solution)/shard_map/ppermute | solution.py:640
  81.3 13.8 %collective-permute-start.30 = (f32[40,512]{1,0:T(8,128)S(1)}, f32[40,512]{1,0:T(8,128)S(1)}, u32[]{:S(2)}, u32[]{:S(2)}) collective-permute-start(f32[40,512]{1,0:T(8,128)S(1)} %element_data.1), channel_id=1, source_target_pairs={{0,4},{1,5},{2,6},{3,7},{4,0},{5,1},{6,2},{7,3},{8,12},{9,13},{10,... | collective-permute-start | bytes 245768 | tf_op jit(solution)/shard_map/ppermute | solution.py:627
  87.9 11.7 %collective-permute-start.31 = (f32[40,512]{1,0:T(8,128)S(1)}, f32[40,512]{1,0:T(8,128)S(1)}, u32[]{:S(2)}, u32[]{:S(2)}) collective-permute-start(f32[40,512]{1,0:T(8,128)S(1)} %element_data.1), channel_id=1, source_target_pairs={{0,2},{1,3},{2,4},{3,5},{4,6},{5,7},{6,0},{7,1},{8,10},{9,11},{10,... | collective-permute-start | bytes 245768 | tf_op jit(solution)/shard_map/ppermute | solution.py:627
  95.1 10.3 %collective-permute-start.23 = (bf16[2,3,48,512]{3,2,1,0:T(8,128)(2,1)S(1)}, bf16[2,3,48,512]{3,2,1,0:T(8,128)(2,1)S(1)}, u32[]{:S(2)}, u32[]{:S(2)}) collective-permute-start(bf16[2,3,48,512]{3,2,1,0:T(8,128)(2,1)S(1)} %get-tuple-element.74), channel_id=1, source_target_pairs={{0,6},{1,7},{2,0},{3,1},{4,2},{5,3},{6,4},{7,5},{8,14},{9,15},{10,... | collective-permute-start | bytes 884744 | tf_op jit(solution)/shard_map/ppermute | solution.py:640
  102.4 17.0 %collective-permute-start.8 = (bf16[2,3,96,512]{3,2,1,0:T(8,128)(2,1)S(1)}, bf16[2,3,96,512]{3,2,1,0:T(8,128)(2,1)S(1)}, u32[]{:S(2)}, u32[]{:S(2)}) collective-permute-start(bf16[2,3,96,512]{3,2,1,0:T(8,128)(2,1)S(1)} %get-tuple-element.55), channel_id=1, source_target_pairs={{0,2},{1,3},{2,4},{3,5},{4,6},{5,7},{6,0},{7,1},{8,10},{9,11},{10,... | collective-permute-start | bytes 1769480 | tf_op jit(solution)/shard_map/ppermute | solution.py:640
  102.6 17.0 %collective-permute-start.9 = (bf16[2,3,96,512]{3,2,1,0:T(8,128)(2,1)}, bf16[2,3,96,512]{3,2,1,0:T(8,128)(2,1)S(1)}, u32[]{:S(2)}, u32[]{:S(2)}) collective-permute-start(bf16[2,3,96,512]{3,2,1,0:T(8,128)(2,1)} %get-tuple-element.56), channel_id=1, source_target_pairs={{0,6},{1,7},{2,0},{3,1},{4,2},{5,3},{6,4},{7,5},{8,14},{9,15},{10,... | collective-permute-start | bytes 1769480 | tf_op jit(solution)/shard_map/ppermute | solution.py:640
  105.4 31.9 %collective-permute-start.20 = (bf16[3,96,1024]{2,1,0:T(8,128)(2,1)S(1)}, bf16[3,96,1024]{2,1,0:T(8,128)(2,1)S(1)}, u32[]{:S(2)}, u32[]{:S(2)}) collective-permute-start(bf16[3,96,1024]{2,1,0:T(8,128)(2,1)S(1)} %ring_sum.6.own_ref), channel_id=1, source_target_pairs={{0,1},{1,0},{2,3},{3,2},{4,5},{5,4},{6,7},{7,6},{8,9},{9,8},{10,11... | collective-permute-start | bytes 1769480 | tf_op jit(solution)/shard_map/ppermute | solution.py:656
  106.5 16.0 %collective-permute-start.24 = (bf16[3,48,512]{2,1,0:T(8,128)(2,1)S(1)}, bf16[3,48,512]{2,1,0:T(8,128)(2,1)S(1)}, u32[]{:S(2)}, u32[]{:S(2)}) collective-permute-start(bf16[3,48,512]{2,1,0:T(8,128)(2,1)S(1)} %get-tuple-element.77), channel_id=1, source_target_pairs={{0,2},{1,3},{2,4},{3,5},{4,6},{5,7},{6,0},{7,1},{8,10},{9,11},{10,... | collective-permute-start | bytes 442376 | tf_op jit(solution)/shard_map/ppermute | solution.py:644
  107.3 15.4 %collective-permute-start.25 = (bf16[3,48,512]{2,1,0:T(8,128)(2,1)S(1)}, bf16[3,48,512]{2,1,0:T(8,128)(2,1)S(1)}, u32[]{:S(2)}, u32[]{:S(2)}) collective-permute-start(bf16[3,48,512]{2,1,0:T(8,128)(2,1)S(1)} %get-tuple-element.78), channel_id=1, source_target_pairs={{0,6},{1,7},{2,0},{3,1},{4,2},{5,3},{6,4},{7,5},{8,14},{9,15},{10,... | collective-permute-start | bytes 442376 | tf_op jit(solution)/shard_map/ppermute | solution.py:644
  119.3 29.2 %collective-permute-start.17 = (bf16[3,96,1024]{2,1,0:T(8,128)(2,1)S(1)}, bf16[3,96,1024]{2,1,0:T(8,128)(2,1)S(1)}, u32[]{:S(2)}, u32[]{:S(2)}) collective-permute-start(bf16[3,96,1024]{2,1,0:T(8,128)(2,1)S(1)} %ring_sum.5.own_ref), channel_id=1, source_target_pairs={{0,1},{1,0},{2,3},{3,2},{4,5},{5,4},{6,7},{7,6},{8,9},{9,8},{10,11... | collective-permute-start | bytes 1769480 | tf_op jit(solution)/shard_map/ppermute | solution.py:660
  119.8 15.5 %collective-permute-start.10 = (bf16[3,96,512]{2,1,0:T(8,128)(2,1)S(1)}, bf16[3,96,512]{2,1,0:T(8,128)(2,1)S(1)}, u32[]{:S(2)}, u32[]{:S(2)}) collective-permute-start(bf16[3,96,512]{2,1,0:T(8,128)(2,1)S(1)} %get-tuple-element.59), channel_id=1, source_target_pairs={{0,2},{1,3},{2,4},{3,5},{4,6},{5,7},{6,0},{7,1},{8,10},{9,11},{10,... | collective-permute-start | bytes 884744 | tf_op jit(solution)/shard_map/ppermute | solution.py:644
  122.5 12.8 %collective-permute-start.11 = (bf16[3,96,512]{2,1,0:T(8,128)(2,1)S(1)}, bf16[3,96,512]{2,1,0:T(8,128)(2,1)S(1)}, u32[]{:S(2)}, u32[]{:S(2)}) collective-permute-start(bf16[3,96,512]{2,1,0:T(8,128)(2,1)S(1)} %get-tuple-element.60), channel_id=1, source_target_pairs={{0,6},{1,7},{2,0},{3,1},{4,2},{5,3},{6,4},{7,5},{8,14},{9,15},{10,... | collective-permute-start | bytes 884744 | tf_op jit(solution)/shard_map/ppermute | solution.py:644
  122.9 13.4 %collective-permute-start.26 = (bf16[3,48,1024]{2,1,0:T(8,128)(2,1)S(1)}, bf16[3,48,1024]{2,1,0:T(8,128)(2,1)S(1)}, u32[]{:S(2)}, u32[]{:S(2)}) collective-permute-start(bf16[3,48,1024]{2,1,0:T(8,128)(2,1)S(1)} %ring_sum.7.a), channel_id=1, source_target_pairs={{0,1},{1,0},{2,3},{3,2},{4,5},{5,4},{6,7},{7,6},{8,9},{9,8},{10,11... | collective-permute-start | bytes 884744 | tf_op jit(solution)/shard_map/ppermute | solution.py:663
  135.6 36.1 %collective-permute-start.12 = (bf16[3,96,1024]{2,1,0:T(8,128)(2,1)S(1)}, bf16[3,96,1024]{2,1,0:T(8,128)(2,1)S(1)}, u32[]{:S(2)}, u32[]{:S(2)}) collective-permute-start(bf16[3,96,1024]{2,1,0:T(8,128)(2,1)S(1)} %ring_sum.4.own_ref), channel_id=1, source_target_pairs={{0,1},{1,0},{2,3},{3,2},{4,5},{5,4},{6,7},{7,6},{8,9},{9,8},{10,11... | collective-permute-start | bytes 1769480 | tf_op jit(solution)/shard_map/ppermute | solution.py:666
  172.9 21.3 %collective-permute-start.27 = (bf16[3,96,256]{2,1,0:T(8,128)(2,1)S(1)}, bf16[3,96,256]{2,1,0:T(8,128)(2,1)S(1)}, u32[]{:S(2)}, u32[]{:S(2)}) collective-permute-start(bf16[3,96,256]{2,1,0:T(8,128)(2,1)S(1)} %get-tuple-element.94), channel_id=1, source_target_pairs={{0,8},{8,16},{16,24},{24,32},{32,40},{40,48},{48,56},{56,64},{64,7... | collective-permute-start | bytes 442376 | tf_op jit(solution)/shard_map/ppermute | solution.py:677
  184.6 9.6 %collective-permute-start.28 = (bf16[3,96,256]{2,1,0:T(8,128)(2,1)S(1)}, bf16[3,96,256]{2,1,0:T(8,128)(2,1)S(1)}, u32[]{:S(2)}, u32[]{:S(2)}) collective-permute-start(bf16[3,96,256]{2,1,0:T(8,128)(2,1)S(1)} %get-tuple-element.93), channel_id=1, source_target_pairs={{8,0},{16,8},{24,16},{32,24},{40,32},{48,40},{56,48},{64,56},{72,6... | collective-permute-start | bytes 442376 | tf_op jit(solution)/shard_map/ppermute | solution.py:678
  (24 other events, 242.6 us)

commit v3 on v2

v3 whole, which is shorter than its diff:
```python
import functools

import jax
import jax.numpy as jnp
from jax import lax
from jax.experimental import pallas as pl
from jax.experimental.pallas import tpu as pltpu
from jax.sharding import PartitionSpec as P

POISSON = 0.3
F32 = jnp.float32
BF16 = jnp.bfloat16
MIB = 1024 * 1024
Z, XLO = 4, 2
Y, XHI, CORE = 4, 2, 2
HALF = 256
ANY = pl.BlockSpec(memory_space=pl.ANY)
VMEM = pl.BlockSpec(memory_space=pltpu.VMEM)
SMEM = pl.BlockSpec(memory_space=pltpu.SMEM)


def params(mib):
    return pltpu.CompilerParams(vmem_limit_bytes=mib * MIB)


def cost(flops, moved):
    return pl.CostEstimate(flops=int(flops), bytes_accessed=int(moved), transcendentals=0)


def shaped(shape, kind):
    return jax.ShapeDtypeStruct(shape, kind)


def mode_index(z, x):
    return (z % Z) * XLO + x


def mesh_index(y, h, c):
    return ((y % Y) * XHI + h) * CORE + c


def mode_perm(dz, flip=0):
    return [(mode_index(z, x), mode_index(z + dz, x ^ flip)) for z in range(Z) for x in range(XLO)]


def mesh_perm(dy, flip_h=0, flip_c=0):
    return [
        (mesh_index(y, h, c), mesh_index(y + dy, h ^ flip_h, c ^ flip_c))
        for y in range(Y)
        for h in range(XHI)
        for c in range(CORE)
    ]


def loads_kernel(cuts, core_ref, shapes_ref, load_ref, mine_ref, theirs_ref, shapes, load, acc, shape_sems, load_sems):
    modes = shapes.shape[1]

    def copies(i):
        c, at, width = cuts[i]
        cut = pl.ds(at, width)
        return (
            pltpu.make_async_copy(shapes_ref.at[c, :, cut], shapes.at[c, :, cut], shape_sems.at[i]),
            pltpu.make_async_copy(load_ref.at[c, cut, :], load.at[c, cut, :], load_sems.at[i]),
        )

    for i in range(len(cuts)):
        for copy in copies(i):
            copy.start()
    acc[modes:, :] = jnp.zeros((acc.shape[0] - modes, acc.shape[1]), F32)
    for i, (c, at, width) in enumerate(cuts):
        for copy in copies(i):
            copy.wait()
        cut = pl.ds(at, width)
        term = jnp.dot(shapes[c, :, cut], load[c, cut, :], preferred_element_type=F32)
        acc[:modes, :] = term if i == 0 else acc[:modes, :] + term
    core = core_ref[0]
    mine_ref[...] = acc[pl.ds(core * HALF, HALF), :]
    theirs_ref[...] = acc[pl.ds((1 - core) * HALF, HALF), :].astype(BF16)


def partial_loads(core, shapes, load):
    comps, modes, nodes = shapes.shape
    cols = load.shape[2]
    block = 1024
    cuts = [(c, at, block) for c in range(comps) for at in range(0, nodes, block)]
    vmem = pl.BlockSpec(memory_space=pltpu.VMEM)
    return pl.pallas_call(
        functools.partial(loads_kernel, cuts),
        out_shape=(shaped((HALF, cols), F32), shaped((HALF, cols), BF16)),
        in_specs=[SMEM, ANY, ANY],
        out_specs=(vmem, vmem),
        scratch_shapes=[
            pltpu.VMEM(shapes.shape, BF16),
            pltpu.VMEM(load.shape, BF16),
            pltpu.VMEM((2 * HALF, cols), F32),
            pltpu.SemaphoreType.DMA((len(cuts),)),
            pltpu.SemaphoreType.DMA((len(cuts),)),
        ],
        compiler_params=params(56),
        cost_estimate=cost(2 * modes * comps * nodes * cols, 2 * comps * nodes * (modes + cols)),
        name="modal_loads",
    )(core, shapes, load)


def response_kernel(mark_ref, a_ref, b_ref, c_ref, d_ref, direct_ref, cross_ref, out_ref):
    del mark_ref
    total = (
        a_ref[...].astype(F32)
        + b_ref[...].astype(F32)
        + c_ref[...].astype(F32)
        + d_ref[...].astype(F32)
    )
    cols = total.shape[1]
    even = lax.broadcasted_iota(jnp.int32, total.shape, 1) % 2 == 0
    other = jnp.where(even, pltpu.roll(total, cols - 1, 1), pltpu.roll(total, 1, 1))
    out_ref[...] = (direct_ref[...] * total + cross_ref[...] * other).astype(BF16)


def half_response(mark, parts, direct, cross):
    vmem = pl.BlockSpec(memory_space=pltpu.VMEM)
    return pl.pallas_call(
        response_kernel,
        out_shape=shaped(direct.shape, BF16),
        in_specs=[ANY] + [vmem] * 6,
        out_specs=vmem,
        compiler_params=params(16),
        cost_estimate=cost(direct.size * 8, direct.size * 18),
        name="modal_response",
    )(mark, *parts, direct, cross)


def element_data_kernel(mark_ref, conn_ref, grads_ref, modulus_ref, out_ref):
    del mark_ref
    corners, width = conn_ref.shape
    conn = conn_ref[...].astype(F32)
    out_ref[:corners, :] = conn
    for d in range(3):
        total = jnp.zeros((corners, width), F32)
        for a in range(corners):
            total = total + jnp.where(conn == conn[a : a + 1, :], grads_ref[d, a : a + 1, :], 0.0)
        out_ref[(d + 1) * corners : (d + 2) * corners, :] = total
    out_ref[4 * corners :, :] = jnp.broadcast_to(modulus_ref[...], (corners, width))


def element_data(mark, conn, grads, modulus):
    corners, elems = conn.shape
    vmem = pl.BlockSpec(memory_space=pltpu.VMEM)
    return pl.pallas_call(
        element_data_kernel,
        out_shape=shaped((5 * corners, elems), F32),
        in_specs=[ANY, vmem, vmem, vmem],
        out_specs=vmem,
        compiler_params=params(16),
        cost_estimate=cost(1000, elems * 4 * 80),
        name="element_data",
    )(mark, conn, grads, modulus[None, :])


def split_ways(blocks, plus_ref, minus_ref, up_ref, down_ref, own_ref):
    half = up_ref.shape[-1]
    low = [b[..., :half] for b in blocks]
    high = [b[..., half:] for b in blocks]
    plus_ref[0, 0] = low[2]
    plus_ref[1, 0] = high[1]
    minus_ref[0, 0] = high[2]
    minus_ref[1, 0] = low[3]
    up_ref[0] = low[1]
    down_ref[0] = high[3]
    own_ref[0] = blocks[0]


def way_shapes(comps, rows, width):
    half = width // 2
    shapes = (
        (2, comps, rows, half),
        (2, comps, rows, half),
        (comps, rows, half),
        (comps, rows, half),
        (comps, rows, width),
    )
    specs = tuple(
        pl.BlockSpec((2, 1) + s[2:], lambda i: (0, i, 0, 0))
        if len(s) == 4
        else pl.BlockSpec((1,) + s[1:], lambda i: (i, 0, 0))
        for s in shapes
    )
    return tuple(shaped(s, BF16) for s in shapes), specs


def fetch_shapes(first, shapes_ref, held, sems):
    step = pl.program_id(0)
    cut = pl.ds(first, held.shape[2])

    @pl.when(step == 0)
    def _():
        for c in range(held.shape[0]):
            pltpu.make_async_copy(shapes_ref.at[c, :, cut], held.at[c], sems.at[c]).start()

    pltpu.make_async_copy(shapes_ref.at[step, :, cut], held.at[step], sems.at[step]).wait()
    return held[step]


def fetch_scratch(shapes, width):
    comps, modes, _ = shapes.shape
    return [pltpu.VMEM((comps, modes, width), BF16), pltpu.SemaphoreType.DMA((comps,))]


def z_first_kernel(first, mark_ref, resp_ref, shapes_ref, *refs):
    del mark_ref
    out_refs, (held, sems) = refs[:5], refs[5:]
    part = fetch_shapes(first, shapes_ref, held, sems)
    value = jnp.dot(resp_ref[...], part, preferred_element_type=F32).astype(BF16)
    rows = value.shape[0] // Z
    split_ways([value[j * rows : (j + 1) * rows, :] for j in range(Z)], *out_refs)


def z_first_terms(mark, resp, shapes, chunk):
    first, width = chunk
    comps, modes, _ = shapes.shape
    cols = resp.shape[0]
    out_shape, out_specs = way_shapes(comps, cols // Z, width)
    return pl.pallas_call(
        functools.partial(z_first_kernel, first),
        out_shape=out_shape,
        grid=(comps,),
        in_specs=[ANY, pl.BlockSpec((cols, modes), lambda i: (0, 0)), ANY],
        out_specs=out_specs,
        scratch_shapes=fetch_scratch(shapes, width),
        compiler_params=params(24),
        cost_estimate=cost(2 * modes * comps * width * cols, 2 * comps * width * (modes + cols)),
        name="z_first_terms",
    )(mark, resp, shapes)


def x_first_kernel(
    first, core_ref, mine_ref, theirs_ref, order_ref, shapes_ref, away_ref, keep_ref, turned_ref, resp, held, sems
):
    modes = shapes_ref.shape[1]
    part = fetch_shapes(first, shapes_ref, held, sems)

    @pl.when(pl.program_id(0) == 0)
    def _():
        core = core_ref[0]
        resp[pl.ds(core * HALF, HALF), :] = mine_ref[...]
        resp[pl.ds((1 - core) * HALF, HALF), :] = theirs_ref[...]
        turned = lax.dot_general(
            order_ref[...], resp[...], (((1,), (1,)), ((), ())), preferred_element_type=F32
        )
        turned_ref[...] = turned[:, :modes].astype(BF16)

    value = jnp.dot(turned_ref[...], part, preferred_element_type=F32).astype(BF16)
    rows = value.shape[0] // (Z * XLO)
    for j in range(Z):
        keep_ref[j, 0] = value[(2 * j) * rows : (2 * j + 1) * rows, :]
        away_ref[j, 0] = value[(2 * j + 1) * rows : (2 * j + 2) * rows, :]


def x_first_terms(core, mine, theirs, order, shapes, chunk):
    first, width = chunk
    comps, modes, _ = shapes.shape
    cols = mine.shape[1]
    rows = cols // (Z * XLO)
    part = pl.BlockSpec((Z, 1, rows, width), lambda i: (0, i, 0, 0))
    whole = lambda i: (0, 0)
    return pl.pallas_call(
        functools.partial(x_first_kernel, first),
        out_shape=(
            shaped((Z, comps, rows, width), BF16),
            shaped((Z, comps, rows, width), BF16),
            shaped((cols, modes), BF16),
        ),
        grid=(comps,),
        in_specs=[
            SMEM,
            pl.BlockSpec((HALF, cols), whole),
            pl.BlockSpec((HALF, cols), whole),
            pl.BlockSpec((cols, cols), whole),
            ANY,
        ],
        out_specs=(part, part, pl.BlockSpec((cols, modes), whole)),
        scratch_shapes=[pltpu.VMEM((2 * HALF, cols), BF16)] + fetch_scratch(shapes, width),
        compiler_params=params(24),
        cost_estimate=cost(2 * modes * comps * width * cols, 2 * comps * width * (modes + cols)),
        name="x_first_terms",
    )(core, mine, theirs, order, shapes)


def x_sum_kernel(mark_ref, keep_ref, got_ref, *out_refs):
    del mark_ref
    blocks = [(keep_ref[j, 0].astype(F32) + got_ref[j, 0].astype(F32)).astype(BF16) for j in range(Z)]
    split_ways(blocks, *out_refs)


def x_sum(mark, keep, got):
    _, comps, rows, width = keep.shape
    out_shape, out_specs = way_shapes(comps, rows, width)
    part = pl.BlockSpec((Z, 1, rows, width), lambda i: (0, i, 0, 0))
    return pl.pallas_call(
        x_sum_kernel,
        out_shape=out_shape,
        grid=(comps,),
        in_specs=[ANY, part, part],
        out_specs=out_specs,
        compiler_params=params(16),
        cost_estimate=cost(keep.size, keep.size * 6),
        name="x_sum",
    )(mark, keep, got)


def pass_on_kernel(mark_ref, up_ref, down_ref, plus_ref, minus_ref, up_out, down_out):
    del mark_ref
    up_out[...] = (up_ref[...].astype(F32) + plus_ref[0].astype(F32)).astype(BF16)
    down_out[...] = (down_ref[...].astype(F32) + minus_ref[0].astype(F32)).astype(BF16)


def pass_on(mark, up, down, plus, minus):
    comps, rows, half = up.shape
    one = pl.BlockSpec((1, rows, half), lambda i: (i, 0, 0))
    first = pl.BlockSpec((1, 1, rows, half), lambda i: (0, i, 0, 0))
    return pl.pallas_call(
        pass_on_kernel,
        out_shape=(shaped(up.shape, BF16), shaped(up.shape, BF16)),
        grid=(comps,),
        in_specs=[ANY, one, one, first, first],
        out_specs=(one, one),
        compiler_params=params(16),
        cost_estimate=cost(2 * up.size, up.size * 12),
        name="pass_on",
    )(mark, up, down, plus, minus)


def ring_sum_kernel(mark_ref, own_ref, plus_ref, minus_ref, up_ref, down_ref, out_ref):
    del mark_ref
    half = up_ref.shape[2]
    low = own_ref[0, :, :half].astype(F32) + minus_ref[0, 0].astype(F32) + up_ref[0].astype(F32)
    high = own_ref[0, :, half:].astype(F32) + plus_ref[0, 0].astype(F32) + down_ref[0].astype(F32)
    out_ref[0, :, :half] = low.astype(BF16)
    out_ref[0, :, half:] = high.astype(BF16)


def ring_sum(mark, own, plus, minus, up, down):
    comps, rows, width = own.shape
    one = lambda n: pl.BlockSpec((1, rows, n), lambda i: (i, 0, 0))
    second = pl.BlockSpec((1, 1, rows, width // 2), lambda i: (1, i, 0, 0))
    return pl.pallas_call(
        ring_sum_kernel,
        out_shape=shaped(own.shape, BF16),
        grid=(comps,),
        in_specs=[ANY, one(width), second, second, one(width // 2), one(width // 2)],
        out_specs=one(width),
        compiler_params=params(16),
        cost_estimate=cost(2 * own.size, own.size * 8),
        name="ring_sum",
    )(mark, own, plus, minus, up, down)


def gather_rows_kernel(first, mark_ref, lists_ref, own_ref, got_ref, *refs):
    del mark_ref
    rim_in_ref, out_ref, rim_ref = refs if len(refs) == 3 else (None,) + refs
    rows = own_ref.shape[1]
    width = own_ref.shape[2]
    if rows == out_ref.shape[1]:
        half = rows // 2
        own = own_ref[0].astype(F32)
        got = got_ref[0].astype(F32)
        out_ref[0, :half, :] = (own[:half] + got[half:]).astype(BF16)
        out_ref[0, half:, :] = (own[half:] + got[:half]).astype(BF16)
    else:
        out_ref[0, :rows, :] = own_ref[0]
        out_ref[0, rows:, :] = got_ref[0]
    node = lax.broadcasted_iota(jnp.int32, (width, lists_ref.shape[1]), 0)
    pick = jnp.where(node == lists_ref[...] - first, 1.0, 0.0).astype(BF16)
    rim = jnp.dot(out_ref[0], pick, preferred_element_type=F32)
    if rim_in_ref is not None:
        rim = rim + rim_in_ref[0].astype(F32)
    rim_ref[0] = rim.astype(BF16)


def gather_rows(mark, lists, own, got, rim, first, full):
    comps, rows, width = own.shape
    count = lists.shape[1]
    one = lambda r, n: pl.BlockSpec((1, r, n), lambda i: (i, 0, 0))
    specs = [ANY, pl.BlockSpec((1, count), lambda i: (0, 0)), one(rows, width), one(rows, width)]
    args = [mark, lists, own, got]
    if rim is not None:
        specs.append(one(full, count))
        args.append(rim)
    return pl.pallas_call(
        functools.partial(gather_rows_kernel, first),
        out_shape=(shaped((comps, full, width), BF16), shaped((comps, full, count), BF16)),
        grid=(comps,),
        in_specs=specs,
        out_specs=(one(full, width), one(full, count)),
        compiler_params=params(16),
        cost_estimate=cost(2 * comps * full * width * count, comps * full * width * 6),
        name="gather_rows",
    )(*args)


NODE_BLOCK = 256
ROWS = 16
LANES = 128


def weights_kernel(first, mark_ref, conn_ref, grads_ref, out_ref):
    del mark_ref
    corners, elems = conn_ref.shape
    nodes = out_ref.shape[1]
    base = lax.broadcasted_iota(jnp.int32, (ROWS, LANES), 0).astype(F32).astype(BF16)
    zero = jnp.zeros((ROWS, LANES), BF16)

    def piece(step, carry):
        cut = pl.ds(pl.multiple_of(step * LANES, LANES), LANES)
        grads = grads_ref[:, cut].astype(BF16)
        grad = [jnp.broadcast_to(grads[i : i + 1, :], (ROWS, LANES)) for i in range(3 * corners)]
        for at in range(0, nodes, NODE_BLOCK):
            keys = (conn_ref[:, cut] - (first + at)).astype(BF16)
            key = [jnp.broadcast_to(keys[a : a + 1, :], (ROWS, LANES)) for a in range(corners)]
            for row in range(0, NODE_BLOCK, ROWS):
                node = base + BF16(row)
                sums = [zero] * 3
                for a in range(corners):
                    hit = node == key[a]
                    for d in range(3):
                        sums[d] = jnp.where(hit, grad[d * corners + a], sums[d])
                for d in range(3):
                    out_ref[d, pl.ds(at + row, ROWS), cut] = sums[d]
        return carry

    lax.fori_loop(0, elems // LANES, piece, 0)


def element_weights(mark, data, first, count):
    elems = data.shape[1]
    return pl.pallas_call(
        functools.partial(weights_kernel, float(first)),
        out_shape=shaped((3, count, elems), BF16),
        in_specs=[ANY, VMEM, VMEM],
        out_specs=VMEM,
        compiler_params=params(8),
        cost_estimate=cost(count * elems * 1500, 6 * count * elems),
        name="element_weights",
    )(mark, data[:8], data[8:32])


def multiply_kernel(pieces, mark_ref, values_ref, *refs):
    del mark_ref
    weights_refs, rest = refs[:pieces], refs[pieces:]
    acc_ref, out_ref = rest if len(rest) == 2 else (None,) + rest
    comps, rows, nodes = values_ref.shape
    values = values_ref[...].reshape(comps * rows, nodes)

    def piece(step, carry):
        cut = pl.ds(pl.multiple_of(step * WIDE, WIDE), WIDE)
        for d in range(3):
            total = None if acc_ref is None else acc_ref[d, :, cut]
            at = 0
            for ref in weights_refs:
                count = ref.shape[1]
                term = jnp.dot(values[:, at : at + count], ref[d, :, cut], preferred_element_type=F32)
                total = term if total is None else total + term
                at += count
            out_ref[d, :, cut] = total
        return carry

    lax.fori_loop(0, out_ref.shape[2] // WIDE, piece, 0)


WIDE = 256


def multiply(mark, values, weights, acc):
    comps, rows, nodes = values.shape
    elems = weights[0].shape[2]
    total = comps * rows
    args = [mark, values] + list(weights) + ([] if acc is None else [acc])
    return pl.pallas_call(
        functools.partial(multiply_kernel, len(weights)),
        out_shape=shaped((3, total, elems), F32),
        in_specs=[ANY] + [VMEM] * (len(args) - 1),
        out_specs=VMEM,
        input_output_aliases={} if acc is None else {len(args) - 1: 0},
        compiler_params=params(8),
        cost_estimate=cost(6 * total * nodes * elems, 6 * nodes * elems),
        name="multiply",
    )(*args)


def spectra_kernel(before_ref, after_ref, weights_ref, acc_ref, modulus_ref, out_ref, grads):
    comps, rows, rim = before_ref.shape
    half = rows // 4
    groups, _, count = out_ref.shape
    per = count // WIDE
    before = before_ref[...].reshape(comps * rows, rim)
    after = after_ref[...].reshape(comps * rows, rim)

    def finish(group, place, lanes_at, modulus):
        lame = modulus * (POISSON / ((1.0 + POISSON) * (1.0 - 2.0 * POISSON)))
        shear = modulus * (1.0 / (2.0 * (1.0 + POISSON)))
        twice = 2.0 * shear
        lanes = pl.ds(lanes_at, LANES)

        def stress(top):
            def at(c, d):
                return grads[d, c * rows + top : c * rows + top + 8, lanes]

            volume = lame * (at(0, 0) + at(1, 1) + at(2, 2))
            return [
                volume + twice * at(0, 0),
                volume + twice * at(1, 1),
                volume + twice * at(2, 2),
                shear * (at(1, 2) + at(2, 1)),
                shear * (at(2, 0) + at(0, 2)),
                shear * (at(0, 1) + at(1, 0)),
            ]

        pairs = [(i, j, 0) for i in range(6) for j in range(i, 6)]
        pairs += [(i, j, 1) for i in range(6) for j in range(i + 1, 6)]
        totals = [None] * len(pairs)
        for top in [s * 2 * half + p for s in range(2) for p in range(0, half, 8)]:
            re = stress(top)
            im = stress(top + half)
            for n, (i, j, turned) in enumerate(pairs):
                if turned:
                    term = im[i] * re[j] - re[i] * im[j]
                else:
                    term = re[i] * re[j] + im[i] * im[j]
                totals[n] = term if totals[n] is None else totals[n] + term
        for n in range(len(pairs)):
            out_ref[group, pl.ds(n, 1), pl.ds(place, LANES)] = jnp.sum(totals[n], axis=0, keepdims=True)

    def piece(step, carry):
        cut = pl.ds(pl.multiple_of(step * WIDE, WIDE), WIDE)
        for d in range(3):
            grads[d] = (
                acc_ref[d, :, cut]
                + jnp.dot(before, weights_ref[d, :rim, cut], preferred_element_type=F32)
                + jnp.dot(after, weights_ref[d, rim:, cut], preferred_element_type=F32)
            )
        group = step // per
        start = (step % per) * WIDE
        for at in range(0, WIDE, LANES):
            here = pl.ds(pl.multiple_of(step * WIDE + at, LANES), LANES)
            finish(group, pl.multiple_of(start + at, LANES), at, modulus_ref[:1, here])
        return carry

    lax.fori_loop(0, groups * per, piece, 0)


def element_spectra(before, after, weights, acc, modulus):
    comps, rows, rim = before.shape
    elems = weights.shape[2]
    return pl.pallas_call(
        spectra_kernel,
        out_shape=shaped((Z, 36, elems // Z), F32),
        in_specs=[VMEM] * 5,
        out_specs=VMEM,
        scratch_shapes=[pltpu.VMEM((3, comps * rows, WIDE), F32)],
        compiler_params=params(8),
        cost_estimate=cost(12 * comps * rows * rim * elems, 24 * comps * rows * elems),
        name="element_spectra",
    )(before, after, weights, acc, modulus)


def collect_kernel(place_ref, a_ref, b_ref, c_ref, d_ref, out_ref):
    for j, ref in enumerate((a_ref, b_ref, c_ref, d_ref)):
        out_ref[pl.ds((place_ref[0] + Z - j) % Z, 1)] = ref[...][None]


def collect(place, blocks):
    return pl.pallas_call(
        collect_kernel,
        out_shape=shaped((Z,) + blocks[0].shape, F32),
        in_specs=[SMEM] + [VMEM] * Z,
        out_specs=VMEM,
        compiler_params=params(8),
        cost_estimate=cost(1, 8 * Z * blocks[0].size),
        name="collect",
    )(place, *blocks)


def local(
    mode_shapes,
    load_nodal,
    mode_freq,
    damping,
    drive_freq,
    send_lists,
    connectivity,
    shape_grads,
    modulus,
):
    modes, _, nodes = mode_shapes.shape
    cols = load_nodal.shape[2]
    bound = send_lists.shape[1]
    freqs = drive_freq.shape[0]
    rows = cols // (Z * XLO)
    mode_at = lax.axis_index("mode")
    z_at, x_at = mode_at // XLO, mode_at % XLO
    core = (lax.axis_index("mesh") % CORE).astype(jnp.int32)
    core_arg = core.reshape(1)
    shapes = jnp.transpose(mode_shapes, (1, 0, 2))
    lists = send_lists.reshape(1, -1)

    pad = 2 * HALF - modes
    natural = jnp.pad(mode_freq, (0, pad), constant_values=1.0)[:, None]
    loss = jnp.pad(damping, (0, pad), constant_values=0.5)[:, None]
    natural = lax.dynamic_slice_in_dim(natural, core * HALF, HALF)
    loss = lax.dynamic_slice_in_dim(loss, core * HALF, HALF)
    forcing = jnp.repeat(drive_freq, cols // freqs)[None, :]
    gap = natural * natural - forcing * forcing
    damp = 2.0 * loss * natural * forcing
    size = gap * gap + damp * damp
    sign = jnp.where(jnp.arange(cols) % 2 == 0, 1.0, -1.0).astype(F32)[None, :]
    direct = gap / size
    cross = sign * (damp / size)

    spot = jnp.arange(cols)
    block, inside = spot // rows, spot % rows
    block = mode_index(z_at + block // XLO, x_at ^ (block % XLO))
    source = block * rows + 2 * (inside % (rows // 2)) + inside // (rows // 2)
    order = (source[:, None] == spot[None, :]).astype(BF16)

    mine, theirs = partial_loads(core_arg, shapes, load_nodal)
    got = lax.ppermute(theirs, "mesh", mesh_perm(0, 0, 1))
    chip = (mine + got.astype(F32)).astype(BF16)
    got = lax.ppermute(chip, "mesh", mesh_perm(0, 1, 0))
    pair = (chip.astype(F32) + got.astype(F32)).astype(BF16)
    ring = [pair] + [lax.ppermute(pair, "mesh", mesh_perm(dy)) for dy in range(1, Y)]

    data = element_data(theirs, connectivity, shape_grads, modulus)
    data = jnp.concatenate(
        [data] + [lax.ppermute(data, "mode", mode_perm(-j)) for j in range(1, Z)], axis=1
    )
    up_perm, down_perm, side_perm = mode_perm(1), mode_perm(-1), mode_perm(0, 1)
    up = lambda v: lax.ppermute(v, "mode", up_perm)
    down = lambda v: lax.ppermute(v, "mode", down_perm)
    side = lambda v: lax.ppermute(v, "mode", side_perm)
    full = 2 * rows

    w_1, w_0, w_2, w_3 = nodes * 5 // 16, nodes * 4 // 16, nodes * 5 // 16, nodes * 2 // 16
    c_1, c_0 = (0, w_1), (w_1, w_0)
    c_2, c_3 = (w_1 + w_0, w_2), (w_1 + w_0 + w_2, w_3)

    part = 2 * NODE_BLOCK
    early = w_2 - part
    build = lambda mark, first, count: element_weights(mark, data, first, count)
    weights_1 = [build(pair, 0, part)]
    resp_mine = half_response(weights_1[0], ring, direct, cross)
    resp_theirs = lax.ppermute(resp_mine, "mesh", mesh_perm(0, 0, 1))
    away, keep, resp = x_first_terms(core_arg, resp_mine, resp_theirs, order, shapes, c_0)
    got_0 = side(away)
    ways_1 = z_first_terms(keep, resp, shapes, c_1)
    plus_1, minus_1 = up(ways_1[0]), down(ways_1[1])
    ways_2 = z_first_terms(ways_1[2], resp, shapes, c_2)
    plus_2, minus_2 = up(ways_2[0]), down(ways_2[1])
    weights_1.append(build(ways_2[2], part, w_1 - part))
    on_1 = pass_on(weights_1[1], ways_1[2], ways_1[3], plus_1, minus_1)
    up_1, down_1 = up(on_1[0]), down(on_1[1])
    ways_3 = z_first_terms(on_1[0], resp, shapes, c_3)
    weights_0 = [build(ways_3[2], c_0[0], part)]
    ways_0 = x_sum(weights_0[0], keep, got_0)
    plus_0, minus_0 = up(ways_0[0]), down(ways_0[1])
    weights_0.append(build(ways_0[2], c_0[0] + part, w_0 - part))
    on_2 = pass_on(weights_0[1], ways_2[2], ways_2[3], plus_2, minus_2)
    up_2, down_2 = up(on_2[0]), down(on_2[1])
    plus_3, minus_3 = up(ways_3[0]), down(ways_3[1])
    weights_2 = [build(on_2[0], c_2[0], early)]
    own_1 = ring_sum(weights_2[0], ways_1[4], plus_1, minus_1, up_1, down_1)
    side_1 = side(own_1)
    on_0 = pass_on(own_1, ways_0[2], ways_0[3], plus_0, minus_0)
    up_0, down_0 = up(on_0[0]), down(on_0[1])
    own_2 = ring_sum(on_0[0], ways_2[4], plus_2, minus_2, up_2, down_2)
    side_2 = side(own_2)
    values_1, rim = gather_rows(own_2, lists, own_1, side_1, None, c_1[0], full)
    acc = multiply(rim, values_1, weights_1, None)
    on_3 = pass_on(acc, ways_3[2], ways_3[3], plus_3, minus_3)
    up_3, down_3 = up(on_3[0]), down(on_3[1])
    own_0 = ring_sum(on_3[0], ways_0[4], plus_0, minus_0, up_0, down_0)
    side_0 = side(own_0)
    weights_2.append(build(own_0, c_2[0] + early, w_2 - early))
    own_3 = ring_sum(weights_2[1], ways_3[4], plus_3, minus_3, up_3, down_3)
    side_3 = side(own_3)
    values_2, rim = gather_rows(own_3, lists, own_2, side_2, rim, c_2[0], full)
    acc = multiply(rim, values_2, weights_2, acc)
    weights_3 = [build(acc, nodes - w_3, w_3)]
    values_0, rim = gather_rows(weights_3[0], lists, own_0, side_0, rim, c_0[0], full)
    acc = multiply(rim, values_0, weights_0, acc)
    rim_weights = build(acc, nodes, 2 * bound)
    values_3, rim = gather_rows(rim_weights, lists, own_3, side_3, rim, c_3[0], full)

    count = lax.axis_size("mesh")
    before = lax.ppermute(rim[..., bound:], "mesh", [(p, p + 1) for p in range(count - 1)])
    after = lax.ppermute(rim[..., :bound], "mesh", [(p + 1, p) for p in range(count - 1)])
    acc = multiply(rim, values_3, weights_3, acc)
    spectra = element_spectra(before, after, rim_weights, acc, data[32:40])
    back = [spectra[0]] + [lax.ppermute(spectra[j], "mode", mode_perm(j)) for j in range(1, Z)]
    return collect(z_at.astype(jnp.int32).reshape(1), back)


def solution(mesh):
    in_specs = (
        P("mode", None, "mesh"),
        P(None, "mesh", None),
        P("mode"),
        P("mode"),
        P(),
        P(None, "mesh"),
        P(None, ("mesh", "mode")),
        P(None, None, ("mesh", "mode")),
        P(("mesh", "mode")),
    )
    out_specs = P(None, None, ("mesh", "mode"))
    return jax.shard_map(local, mesh=mesh, in_specs=in_specs, out_specs=out_specs, check_vma=False)
```

time: 211 us -> 196 us (0.929)
  Pallas kernels: 95.8 us -> 81.6 us
  waiting for transfers between devices: 50.7 us -> 42.7 us
  local copies, waits for them, and re-layouts: 6.3 us -> 11 us
  starting transfers between devices: 54.7 us -> 57.3 us
    pallas_call x16 -> x23, Pallas kernels: 85.9 us -> 73.3 us  [the longest x8 25.9 us: element_weights(): pl.pallas_call(functools.partial(weights_kernel, float(first)), out_shape...]
    ppermute x3, waiting for transfers between devices: 11.7 us -> 0.01 us  [local(): lax.ppermute(data, 'mode', mode_perm(-j))]
    unnamed x27 -> x37, local copies, waits for them, and re-layouts: 4.61 us -> 9.85 us
    ppermute x21, starting transfers between devices: 22.4 us -> 25.7 us  [the longest x8 19.1 us: local(): down = lambda v: lax.ppermute(v, 'mode', down_perm)]
    ppermute x21, waiting for transfers between devices: 23.6 us -> 26.8 us  [the longest x8 20.4 us: local(): up = lambda v: lax.ppermute(v, 'mode', up_perm)]
    ppermute x3, waiting for transfers between devices: 6.68 us -> 3.95 us  [local(): lax.ppermute(pair, 'mesh', mesh_perm(dy))]
    ppermute x3, starting transfers between devices: 3.06 us -> 5.35 us  [local(): lax.ppermute(data, 'mode', mode_perm(-j))]
  transfers between devices with their start and end apart: 35 -> 35, of which waited for: 17 -> 12; matrix products, arithmetic and copies ran while one was open for 0% -> 1% of each run, Pallas kernels for 33% -> 31%
where the time goes in v3:
time: 196 us; the launch traced here: 195 us
  Pallas kernels  81.6 us (42%)
  starting transfers between devices  57.3 us (29%)
  waiting for transfers between devices  42.7 us (22%)
  local copies, waits for them, and re-layouts  11 us (6%)
    pallas_call x8, Pallas kernels, element_weights(): pl.pallas_call(functools.partial(weights_kernel, float(first)), out_shape...  25.9 us
    pallas_call x4, Pallas kernels, multiply(): pl.pallas_call(functools.partial(multiply_kernel, len(weights)), out_shap...  22.2 us
    ppermute x8, waiting for transfers between devices, local(): up = lambda v: lax.ppermute(v, 'mode', up_perm)  20.4 us
    ppermute x8, starting transfers between devices, local(): down = lambda v: lax.ppermute(v, 'mode', down_perm)  19.1 us
    pallas_call x1, Pallas kernels, partial_loads(): pl.pallas_call(functools.partial(loads_kernel, cuts), out_shape=(shaped((...  11.1 us
    unnamed x37, local copies, waits for them, and re-layouts  9.85 us
    ppermute x1, starting transfers between devices, local(): lax.ppermute(rim[..., bound:], 'mesh', [(p, p + 1) for p in range(count -...  9.83 us
    ppermute x8, waiting for transfers between devices, local(): down = lambda v: lax.ppermute(v, 'mode', down_perm)  6.44 us
  transfers between devices with their start and end apart: 35, of which 12 were waited for; matrix products, arithmetic and copies ran while one was open for 1% of the time, Pallas kernels for 31%

profile of v3, /device:TPU:1, one launch (start us, length us, event | category | flops | bytes accessed | tf_op | source)
XLA Modules:
  0.0 194.9 jit_solution(925268251886523502)
XLA Ops:
  0.0 11.1 %modal_loads.1 = (f32[256,384]{1,0:T(8,128)}, bf16[256,384]{1,0:T(8,128)(2,1)}) custom-call(s32[1]{0:T(128)} %bitcast.1.core_ref, bf16[3,500,4096]{2,1,0:T(8,128)(2,1)} %bitcast.15, bf16[3,4096,384]{2,1,0:T(8,128)(2,1)} %load_ref.1), custom_call_target="tpu_custom_call" | custom-call | flops 4718592000 | bytes 21725184 | tf_op jit(solution)/shard_map/modal_loads/pallas_call | solution.py:87
  11.3 4.6 %collective-permute-start.2 = (f32[40,512]{1,0:T(8,128)S(1)}, f32[40,512]{1,0:T(8,128)S(1)}, u32[]{:S(2)}, u32[]{:S(2)}) collective-permute-start(f32[40,512]{1,0:T(8,128)S(1)} %element_data.1), channel_id=1, source_target_pairs={{0,6},{1,7},{2,0},{3,1},{4,2},{5,3},{6,4},{7,5},{8,14},{9,15},{10,... | collective-permute-start | bytes 245768 | tf_op jit(solution)/shard_map/ppermute | solution.py:633
  23.3 4.8 %collective-permute-done.1 = bf16[256,384]{1,0:T(8,128)(2,1)S(1)} collective-permute-done((bf16[256,384]{1,0:T(8,128)(2,1)S(1)}, bf16[256,384]{1,0:T(8,128)(2,1)S(1)}, u32[]{:S(2)}, u32[]{:S(2)}) %collective-permute-start.1) | collective-permute-done | bytes 196640 | tf_op jit(solution)/shard_map/ppermute | solution.py:627
  33.3 2.9 %element_weights.8.mark_ref.refs_0_ = bf16[3,512,2048]{2,1,0:T(8,128)(2,1)S(1)} custom-call(bf16[256,384]{1,0:T(8,128)(2,1)S(1)} %add_convert_fusion.mark_ref.a_ref, f32[8,2048]{1,0:T(8,128)S(1)} %get-tuple-element.92.conn_ref, f32[24,2048]{1,0:T(8,128)S(1)} %slice.50.grads_ref), custom_call_target="tpu_custom_call" | custom-call | flops 1572864000 | bytes 6291456 | tf_op jit(solution)/shard_map/element_weights/pallas_call | solution.py:435
  36.2 3.9 %collective-permute-done.6.c_ref = bf16[256,384]{1,0:T(8,128)(2,1)S(1)} collective-permute-done((bf16[256,384]{1,0:T(8,128)(2,1)S(1)}, bf16[256,384]{1,0:T(8,128)(2,1)S(1)}, u32[]{:S(2)}, u32[]{:S(2)}) %collective-permute-start.6) | collective-permute-done | bytes 196640 | tf_op jit(solution)/shard_map/ppermute | solution.py:629
  46.2 2.8 %x_first_terms.1 = (bf16[4,3,48,1024]{3,2,1,0:T(8,128)(2,1)S(1)}, bf16[4,3,48,1024]{3,2,1,0:T(8,128)(2,1)S(1)}, bf16[384,500]{1,0:T(8,128)(2,1)S(1)}) custom-call(s32[1]{0:T(128)} %bitcast.1.core_ref, bf16[256,384]{1,0:T(8,128)(2,1)S(1)} %modal_response.1.mine_ref, bf16[256,384]{1,0:T(8,128)(2,1)S(1)} %collective-permute-done.8.theirs_ref, ...), custom_call_target="tpu_custom_call" | custom-call | flops 1179648000 | bytes 5431296 | tf_op jit(solution)/shard_map/x_first_terms/pallas_call | solution.py:265
  60.5 4.3 %element_weights.9.mark_ref.refs_1_ = bf16[3,768,2048]{2,1,0:T(8,128)(2,1)S(1)} custom-call(bf16[3,96,640]{2,1,0:T(8,128)(2,1)S(1)} %get-tuple-element.51.mark_ref.up_ref, f32[8,2048]{1,0:T(8,128)S(1)} %get-tuple-element.92.conn_ref, f32[24,2048]{1,0:T(8,128)S(1)} %slice.50.grads_ref), custom_call_target="tpu_custom_call" | custom-call | flops 2359296000 | bytes 9437184 | tf_op jit(solution)/shard_map/element_weights/pallas_call | solution.py:435
  64.8 6.4 %collective-permute-done.10.minus_ref = bf16[2,3,96,640]{3,2,1,0:T(8,128)(2,1)S(1)} collective-permute-done((bf16[2,3,96,640]{3,2,1,0:T(8,128)(2,1)S(1)}, bf16[2,3,96,640]{3,2,1,0:T(8,128)(2,1)S(1)}, u32[]{:S(2)}, u32[]{:S(2)}) %collective-permute-start.10) | collective-permute-done | bytes 737312 | tf_op jit(solution)/shard_map/ppermute | solution.py:637
  77.3 2.9 %element_weights.10.mark_ref.refs_0_ = bf16[3,512,2048]{2,1,0:T(8,128)(2,1)S(1)} custom-call(bf16[3,96,256]{2,1,0:T(8,128)(2,1)S(1)} %get-tuple-element.56.mark_ref.up_ref, f32[8,2048]{1,0:T(8,128)S(1)} %get-tuple-element.92.conn_ref, f32[24,2048]{1,0:T(8,128)S(1)} %slice.50.grads_ref), custom_call_target="tpu_custom_call" | custom-call | flops 1572864000 | bytes 6291456 | tf_op jit(solution)/shard_map/element_weights/pallas_call | solution.py:435
  80.8 2.9 %element_weights.11.mark_ref.refs_1_ = bf16[3,512,2048]{2,1,0:T(8,128)(2,1)S(1)} custom-call(bf16[3,48,512]{2,1,0:T(8,128)(2,1)S(1)} %get-tuple-element.58.mark_ref.up_ref, f32[8,2048]{1,0:T(8,128)S(1)} %get-tuple-element.92.conn_ref, f32[24,2048]{1,0:T(8,128)S(1)} %slice.50.grads_ref), custom_call_target="tpu_custom_call" | custom-call | flops 1572864000 | bytes 6291456 | tf_op jit(solution)/shard_map/element_weights/pallas_call | solution.py:435
  83.7 5.1 %collective-permute-done.12.plus_ref = bf16[2,3,96,640]{3,2,1,0:T(8,128)(2,1)S(1)} collective-permute-done((bf16[2,3,96,640]{3,2,1,0:T(8,128)(2,1)S(1)}, bf16[2,3,96,640]{3,2,1,0:T(8,128)(2,1)S(1)}, u32[]{:S(2)}, u32[]{:S(2)}) %collective-permute-start.12) | collective-permute-done | bytes 737312 | tf_op jit(solution)/shard_map/ppermute | solution.py:636
  89.0 4.3 %element_weights.12.mark_ref.refs_0_ = bf16[3,768,2048]{2,1,0:T(8,128)(2,1)S(1)} custom-call(bf16[3,96,640]{2,1,0:T(8,128)(2,1)S(1)} %get-tuple-element.62.mark_ref, f32[8,2048]{1,0:T(8,128)S(1)} %get-tuple-element.92.conn_ref, f32[24,2048]{1,0:T(8,128)S(1)} %slice.50.grads_ref), custom_call_target="tpu_custom_call" | custom-call | flops 2359296000 | bytes 9437184 | tf_op jit(solution)/shard_map/element_weights/pallas_call | solution.py:435
  93.3 3.4 %collective-permute-done.14.up_ref = bf16[3,96,640]{2,1,0:T(8,128)(2,1)S(1)} collective-permute-done((bf16[3,96,640]{2,1,0:T(8,128)(2,1)S(1)}, bf16[3,96,640]{2,1,0:T(8,128)(2,1)S(1)}, u32[]{:S(2)}, u32[]{:S(2)}) %collective-permute-start.14) | collective-permute-done | bytes 368672 | tf_op jit(solution)/shard_map/ppermute | solution.py:636
  102.7 10.1 %collective-permute-done.16.plus_ref = bf16[2,3,48,512]{3,2,1,0:T(8,128)(2,1)S(1)} collective-permute-done((bf16[2,3,48,512]{3,2,1,0:T(8,128)(2,1)S(1)}, bf16[2,3,48,512]{3,2,1,0:T(8,128)(2,1)S(1)}, u32[]{:S(2)}, u32[]{:S(2)}) %collective-permute-start.16) | collective-permute-done | bytes 294944 | tf_op jit(solution)/shard_map/ppermute | solution.py:636
  124.1 6.2 %multiply.4.mark_ref.refs_2_ = f32[3,288,2048]{2,1,0:T(8,128)S(1)} custom-call(bf16[3,96,512]{2,1,0:T(8,128)(2,1)S(1)} %get-tuple-element.71.mark_ref.refs_0_, bf16[3,96,1280]{2,1,0:T(8,128)(2,1)S(1)} %get-tuple-element.72.values_ref, bf16[3,512,2048]{2,1,0:T(8,128)(2,1)S(1)} %copy-done.4, bf16[3,768,2048]{2,1,0:T(8,128)(2,1)S(1)} %element_weights.9.mark_ref.refs_1_), custom_call_target="tpu_custom_call" | custom-call | flops 4529848320 | bytes 15728640 | tf_op jit(solution)/shard_map/multiply/pallas_call | solution.py:477
  133.7 2.9 %element_weights.13.mark_ref.refs_1_ = bf16[3,512,2048]{2,1,0:T(8,128)(2,1)S(1)} custom-call(bf16[3,48,1024]{2,1,0:T(8,128)(2,1)S(1)} %ring_sum.6.mark_ref.own_ref, f32[8,2048]{1,0:T(8,128)S(1)} %get-tuple-element.92.conn_ref, f32[24,2048]{1,0:T(8,128)S(1)} %slice.50.grads_ref), custom_call_target="tpu_custom_call" | custom-call | flops 1572864000 | bytes 6291456 | tf_op jit(solution)/shard_map/element_weights/pallas_call | solution.py:435
  140.5 3.4 %copy-done.6 = bf16[3,512,2048]{2,1,0:T(8,128)(2,1)S(1)} copy-done((bf16[3,512,2048]{2,1,0:T(8,128)(2,1)S(1)}, bf16[3,512,2048]{2,1,0:T(8,128)(2,1)}, u32[]{:S(2)}) %copy-start.6) | copy-done | bytes 6291480
  143.9 6.6 %multiply.5.mark_ref.refs_2_ = f32[3,288,2048]{2,1,0:T(8,128)S(1)} custom-call(bf16[3,96,512]{2,1,0:T(8,128)(2,1)S(1)} %get-tuple-element.81.mark_ref.refs_0_, bf16[3,96,1280]{2,1,0:T(8,128)(2,1)S(1)} %get-tuple-element.82.values_ref, bf16[3,768,2048]{2,1,0:T(8,128)(2,1)S(1)} %element_weights.12.mark_ref.refs_0_, ...), custom_call_target="tpu_custom_call", output_to_operand_aliasing={{}: (4, {})} | custom-call | flops 4529848320 | bytes 15728640 | tf_op jit(solution)/shard_map/multiply/pallas_call | solution.py:477
  150.5 2.9 %element_weights.14.mark_ref.refs_0_ = bf16[3,512,2048]{2,1,0:T(8,128)(2,1)S(1)} custom-call(f32[3,288,2048]{2,1,0:T(8,128)S(1)} %multiply.5.mark_ref.refs_2_, f32[8,2048]{1,0:T(8,128)S(1)} %get-tuple-element.92.conn_ref, f32[24,2048]{1,0:T(8,128)S(1)} %slice.50.grads_ref), custom_call_target="tpu_custom_call" | custom-call | flops 1572864000 | bytes 6291456 | tf_op jit(solution)/shard_map/element_weights/pallas_call | solution.py:435
  154.5 5.7 %multiply.6.mark_ref.refs_1_ = f32[3,288,2048]{2,1,0:T(8,128)S(1)} custom-call(bf16[3,96,512]{2,1,0:T(8,128)(2,1)S(1)} %get-tuple-element.83.mark_ref.refs_0_, bf16[3,96,1024]{2,1,0:T(8,128)(2,1)S(1)} %get-tuple-element.84.values_ref, bf16[3,512,2048]{2,1,0:T(8,128)(2,1)S(1)} %bitcast.21, ...), custom_call_target="tpu_custom_call", output_to_operand_aliasing={{}: (4, {})} | custom-call | flops 3623878656 | bytes 12582912 | tf_op jit(solution)/shard_map/multiply/pallas_call | solution.py:477
  160.2 2.9 %element_weights.15.mark_ref.weights_ref = bf16[3,512,2048]{2,1,0:T(8,128)(2,1)S(1)} custom-call(f32[3,288,2048]{2,1,0:T(8,128)S(1)} %multiply.6.mark_ref.refs_1_, f32[8,2048]{1,0:T(8,128)S(1)} %get-tuple-element.92.conn_ref, f32[24,2048]{1,0:T(8,128)S(1)} %slice.50.grads_ref), custom_call_target="tpu_custom_call" | custom-call | flops 1572864000 | bytes 6291456 | tf_op jit(solution)/shard_map/element_weights/pallas_call | solution.py:435
  164.0 9.8 %collective-permute-start.30 = (bf16[3,96,256]{2,1,0:T(8,128)(2,1)S(1)}, bf16[3,96,256]{2,1,0:T(8,128)(2,1)S(1)}, u32[]{:S(2)}, u32[]{:S(2)}) collective-permute-start(bf16[3,96,256]{2,1,0:T(8,128)(2,1)S(1)} %get-tuple-element.94), channel_id=1, source_target_pairs={{0,8},{8,16},{16,24},{24,32},{32,40},{40,48},{48,56},{56,64},{64,7... | collective-permute-start | bytes 442376 | tf_op jit(solution)/shard_map/ppermute | solution.py:693
  176.0 3.7 %multiply.7.acc_ref = f32[3,288,2048]{2,1,0:T(8,128)S(1)} custom-call(bf16[3,96,512]{2,1,0:T(8,128)(2,1)S(1)} %get-tuple-element.85.mark_ref, bf16[3,96,512]{2,1,0:T(8,128)(2,1)S(1)} %get-tuple-element.86.values_ref, bf16[3,512,2048]{2,1,0:T(8,128)(2,1)S(1)} %element_weights.14.mark_ref.refs_0_, ...), custom_call_target="tpu_custom_call", output_to_operand_aliasing={{}: (3, {})} | custom-call | flops 1811939328 | bytes 6291456 | tf_op jit(solution)/shard_map/multiply/pallas_call | solution.py:477
  181.8 6.1 %element_spectra.1 = f32[4,36,512]{2,1,0:T(8,128)S(1)} custom-call(bf16[3,96,256]{2,1,0:T(8,128)(2,1)S(1)} %collective-permute-done.30.before_ref, bf16[3,96,256]{2,1,0:T(8,128)(2,1)S(1)} %collective-permute-done.31.after_ref, bf16[3,512,2048]{2,1,0:T(8,128)(2,1)S(1)} %element_weights.15.mark_ref.weights_ref, f32[3,288,2048]{2,1,0:T(8,128)S(1)} %multiply.7.acc_ref, ...), custom_call_target="tpu_custom_call" | custom-call | flops 1811939328 | bytes 14155776 | tf_op jit(solution)/shard_map/element_spectra/pallas_call | solution.py:553
  (135 shorter events, 74.4 us)
Async XLA Ops:
  11.3 12.0 %collective-permute-start.2 = (f32[40,512]{1,0:T(8,128)S(1)}, f32[40,512]{1,0:T(8,128)S(1)}, u32[]{:S(2)}, u32[]{:S(2)}) collective-permute-start(f32[40,512]{1,0:T(8,128)S(1)} %element_data.1), channel_id=1, source_target_pairs={{0,6},{1,7},{2,0},{3,1},{4,2},{5,3},{6,4},{7,5},{8,14},{9,15},{10,... | collective-permute-start | bytes 245768 | tf_op jit(solution)/shard_map/ppermute | solution.py:633
  28.2 8.0 %collective-permute-start.5 = (bf16[256,384]{1,0:T(8,128)(2,1)S(1)}, bf16[256,384]{1,0:T(8,128)(2,1)S(1)}, u32[]{:S(2)}, u32[]{:S(2)}) collective-permute-start(bf16[256,384]{1,0:T(8,128)(2,1)S(1)} %add_convert_fusion.mark_ref.a_ref), channel_id=1, source_target_pairs={{0,32},{8,40},{16,48},{24,56},{32,64},{40,72},{48,80},{56,88},{64,... | collective-permute-start | bytes 589832 | tf_op jit(solution)/shard_map/ppermute | solution.py:629
  29.6 10.6 %collective-permute-start.6 = (bf16[256,384]{1,0:T(8,128)(2,1)S(1)}, bf16[256,384]{1,0:T(8,128)(2,1)S(1)}, u32[]{:S(2)}, u32[]{:S(2)}) collective-permute-start(bf16[256,384]{1,0:T(8,128)(2,1)S(1)} %add_convert_fusion.mark_ref.a_ref), channel_id=1, source_target_pairs={{0,64},{8,72},{16,80},{24,88},{32,96},{40,104},{48,112},{56,120},{... | collective-permute-start | bytes 589832 | tf_op jit(solution)/shard_map/ppermute | solution.py:629
  49.1 31.1 %collective-permute-start.11 = (bf16[4,3,48,1024]{3,2,1,0:T(8,128)(2,1)S(1)}, bf16[4,3,48,1024]{3,2,1,0:T(8,128)(2,1)S(1)}, u32[]{:S(2)}, u32[]{:S(2)}) collective-permute-start(bf16[4,3,48,1024]{3,2,1,0:T(8,128)(2,1)S(1)} %get-tuple-element.57), channel_id=1, source_target_pairs={{0,1},{1,0},{2,3},{3,2},{4,5},{5,4},{6,7},{7,6},{8,9},{9,8},{10,11... | collective-permute-start | bytes 3538952 | tf_op jit(solution)/shard_map/ppermute | solution.py:638
  52.9 18.3 %collective-permute-start.10 = (bf16[2,3,96,640]{3,2,1,0:T(8,128)(2,1)S(1)}, bf16[2,3,96,640]{3,2,1,0:T(8,128)(2,1)S(1)}, u32[]{:S(2)}, u32[]{:S(2)}) collective-permute-start(bf16[2,3,96,640]{3,2,1,0:T(8,128)(2,1)S(1)} %get-tuple-element.54), channel_id=1, source_target_pairs={{0,6},{1,7},{2,0},{3,1},{4,2},{5,3},{6,4},{7,5},{8,14},{9,15},{10,... | collective-permute-start | bytes 2211848 | tf_op jit(solution)/shard_map/ppermute | solution.py:637
  54.7 18.3 %collective-permute-start.9 = (bf16[2,3,96,640]{3,2,1,0:T(8,128)(2,1)S(1)}, bf16[2,3,96,640]{3,2,1,0:T(8,128)(2,1)S(1)}, u32[]{:S(2)}, u32[]{:S(2)}) collective-permute-start(bf16[2,3,96,640]{3,2,1,0:T(8,128)(2,1)S(1)} %get-tuple-element.53), channel_id=1, source_target_pairs={{0,2},{1,3},{2,4},{3,5},{4,6},{5,7},{6,0},{7,1},{8,10},{9,11},{10,... | collective-permute-start | bytes 2211848 | tf_op jit(solution)/shard_map/ppermute | solution.py:636
  57.6 31.2 %collective-permute-start.12 = (bf16[2,3,96,640]{3,2,1,0:T(8,128)(2,1)S(1)}, bf16[2,3,96,640]{3,2,1,0:T(8,128)(2,1)S(1)}, u32[]{:S(2)}, u32[]{:S(2)}) collective-permute-start(bf16[2,3,96,640]{3,2,1,0:T(8,128)(2,1)S(1)} %get-tuple-element.60), channel_id=1, source_target_pairs={{0,2},{1,3},{2,4},{3,5},{4,6},{5,7},{6,0},{7,1},{8,10},{9,11},{10,... | collective-permute-start | bytes 2211848 | tf_op jit(solution)/shard_map/ppermute | solution.py:636
  59.2 29.6 %collective-permute-start.13 = (bf16[2,3,96,640]{3,2,1,0:T(8,128)(2,1)S(1)}, bf16[2,3,96,640]{3,2,1,0:T(8,128)(2,1)S(1)}, u32[]{:S(2)}, u32[]{:S(2)}) collective-permute-start(bf16[2,3,96,640]{3,2,1,0:T(8,128)(2,1)S(1)} %get-tuple-element.61), channel_id=1, source_target_pairs={{0,6},{1,7},{2,0},{3,1},{4,2},{5,3},{6,4},{7,5},{8,14},{9,15},{10,... | collective-permute-start | bytes 2211848 | tf_op jit(solution)/shard_map/ppermute | solution.py:637
  73.2 23.5 %collective-permute-start.14 = (bf16[3,96,640]{2,1,0:T(8,128)(2,1)S(1)}, bf16[3,96,640]{2,1,0:T(8,128)(2,1)S(1)}, u32[]{:S(2)}, u32[]{:S(2)}) collective-permute-start(bf16[3,96,640]{2,1,0:T(8,128)(2,1)S(1)} %get-tuple-element.55.mark_ref), channel_id=1, source_target_pairs={{0,2},{1,3},{2,4},{3,5},{4,6},{5,7},{6,0},{7,1},{8,10},{9,11},{10,... | collective-permute-start | bytes 1105928 | tf_op jit(solution)/shard_map/ppermute | solution.py:636
  73.3 23.4 %collective-permute-start.15 = (bf16[3,96,640]{2,1,0:T(8,128)(2,1)S(1)}, bf16[3,96,640]{2,1,0:T(8,128)(2,1)S(1)}, u32[]{:S(2)}, u32[]{:S(2)}) collective-permute-start(bf16[3,96,640]{2,1,0:T(8,128)(2,1)S(1)} %get-tuple-element.64), channel_id=1, source_target_pairs={{0,6},{1,7},{2,0},{3,1},{4,2},{5,3},{6,4},{7,5},{8,14},{9,15},{10,... | collective-permute-start | bytes 1105928 | tf_op jit(solution)/shard_map/ppermute | solution.py:637
  97.0 20.3 %collective-permute-start.20 = (bf16[3,96,1280]{2,1,0:T(8,128)(2,1)S(1)}, bf16[3,96,1280]{2,1,0:T(8,128)(2,1)S(1)}, u32[]{:S(2)}, u32[]{:S(2)}) collective-permute-start(bf16[3,96,1280]{2,1,0:T(8,128)(2,1)S(1)} %ring_sum.4.mark_ref.own_ref), channel_id=1, source_target_pairs={{0,1},{1,0},{2,3},{3,2},{4,5},{5,4},{6,7},{7,6},{8,9},{9,8},{10,11... | collective-permute-start | bytes 2211848 | tf_op jit(solution)/shard_map/ppermute | solution.py:638
  97.3 15.6 %collective-permute-start.18 = (bf16[3,96,640]{2,1,0:T(8,128)(2,1)S(1)}, bf16[3,96,640]{2,1,0:T(8,128)(2,1)S(1)}, u32[]{:S(2)}, u32[]{:S(2)}) collective-permute-start(bf16[3,96,640]{2,1,0:T(8,128)(2,1)S(1)} %get-tuple-element.62.mark_ref), channel_id=1, source_target_pairs={{0,2},{1,3},{2,4},{3,5},{4,6},{5,7},{6,0},{7,1},{8,10},{9,11},{10,... | collective-permute-start | bytes 1105928 | tf_op jit(solution)/shard_map/ppermute | solution.py:636
  97.3 15.6 %collective-permute-start.19 = (bf16[3,96,640]{2,1,0:T(8,128)(2,1)S(1)}, bf16[3,96,640]{2,1,0:T(8,128)(2,1)S(1)}, u32[]{:S(2)}, u32[]{:S(2)}) collective-permute-start(bf16[3,96,640]{2,1,0:T(8,128)(2,1)S(1)} %get-tuple-element.70), channel_id=1, source_target_pairs={{0,6},{1,7},{2,0},{3,1},{4,2},{5,3},{6,4},{7,5},{8,14},{9,15},{10,... | collective-permute-start | bytes 1105928 | tf_op jit(solution)/shard_map/ppermute | solution.py:637
  100.0 12.8 %collective-permute-start.16 = (bf16[2,3,48,512]{3,2,1,0:T(8,128)(2,1)S(1)}, bf16[2,3,48,512]{3,2,1,0:T(8,128)(2,1)S(1)}, u32[]{:S(2)}, u32[]{:S(2)}) collective-permute-start(bf16[2,3,48,512]{3,2,1,0:T(8,128)(2,1)S(1)} %get-tuple-element.66), channel_id=1, source_target_pairs={{0,2},{1,3},{2,4},{3,5},{4,6},{5,7},{6,0},{7,1},{8,10},{9,11},{10,... | collective-permute-start | bytes 884744 | tf_op jit(solution)/shard_map/ppermute | solution.py:636
  100.0 12.8 %collective-permute-start.17 = (bf16[2,3,48,512]{3,2,1,0:T(8,128)(2,1)S(1)}, bf16[2,3,48,512]{3,2,1,0:T(8,128)(2,1)S(1)}, u32[]{:S(2)}, u32[]{:S(2)}) collective-permute-start(bf16[2,3,48,512]{3,2,1,0:T(8,128)(2,1)S(1)} %get-tuple-element.67), channel_id=1, source_target_pairs={{0,6},{1,7},{2,0},{3,1},{4,2},{5,3},{6,4},{7,5},{8,14},{9,15},{10,... | collective-permute-start | bytes 884744 | tf_op jit(solution)/shard_map/ppermute | solution.py:637
  113.3 25.8 %collective-permute-start.27 = (bf16[3,96,1280]{2,1,0:T(8,128)(2,1)S(1)}, bf16[3,96,1280]{2,1,0:T(8,128)(2,1)S(1)}, u32[]{:S(2)}, u32[]{:S(2)}) collective-permute-start(bf16[3,96,1280]{2,1,0:T(8,128)(2,1)S(1)} %ring_sum.5.mark_ref.own_ref), channel_id=1, source_target_pairs={{0,1},{1,0},{2,3},{3,2},{4,5},{5,4},{6,7},{7,6},{8,9},{9,8},{10,11... | collective-permute-start | bytes 2211848 | tf_op jit(solution)/shard_map/ppermute | solution.py:638
  114.6 15.7 %collective-permute-start.21 = (bf16[2,3,96,256]{3,2,1,0:T(8,128)(2,1)S(1)}, bf16[2,3,96,256]{3,2,1,0:T(8,128)(2,1)S(1)}, u32[]{:S(2)}, u32[]{:S(2)}) collective-permute-start(bf16[2,3,96,256]{3,2,1,0:T(8,128)(2,1)S(1)} %get-tuple-element.74), channel_id=1, source_target_pairs={{0,2},{1,3},{2,4},{3,5},{4,6},{5,7},{6,0},{7,1},{8,10},{9,11},{10,... | collective-permute-start | bytes 884744 | tf_op jit(solution)/shard_map/ppermute | solution.py:636
  114.6 15.7 %collective-permute-start.22 = (bf16[2,3,96,256]{3,2,1,0:T(8,128)(2,1)S(1)}, bf16[2,3,96,256]{3,2,1,0:T(8,128)(2,1)S(1)}, u32[]{:S(2)}, u32[]{:S(2)}) collective-permute-start(bf16[2,3,96,256]{3,2,1,0:T(8,128)(2,1)S(1)} %get-tuple-element.75), channel_id=1, source_target_pairs={{0,6},{1,7},{2,0},{3,1},{4,2},{5,3},{6,4},{7,5},{8,14},{9,15},{10,... | collective-permute-start | bytes 884744 | tf_op jit(solution)/shard_map/ppermute | solution.py:637
  117.3 15.9 %collective-permute-start.23 = (bf16[3,48,512]{2,1,0:T(8,128)(2,1)S(1)}, bf16[3,48,512]{2,1,0:T(8,128)(2,1)S(1)}, u32[]{:S(2)}, u32[]{:S(2)}) collective-permute-start(bf16[3,48,512]{2,1,0:T(8,128)(2,1)S(1)} %get-tuple-element.68.mark_ref), channel_id=1, source_target_pairs={{0,2},{1,3},{2,4},{3,5},{4,6},{5,7},{6,0},{7,1},{8,10},{9,11},{10,... | collective-permute-start | bytes 442376 | tf_op jit(solution)/shard_map/ppermute | solution.py:636
  117.3 15.9 %collective-permute-start.24 = (bf16[3,48,512]{2,1,0:T(8,128)(2,1)S(1)}, bf16[3,48,512]{2,1,0:T(8,128)(2,1)S(1)}, u32[]{:S(2)}, u32[]{:S(2)}) collective-permute-start(bf16[3,48,512]{2,1,0:T(8,128)(2,1)S(1)} %get-tuple-element.78), channel_id=1, source_target_pairs={{0,6},{1,7},{2,0},{3,1},{4,2},{5,3},{6,4},{7,5},{8,14},{9,15},{10,... | collective-permute-start | bytes 442376 | tf_op jit(solution)/shard_map/ppermute | solution.py:637
  133.3 20.1 %collective-permute-start.28 = (bf16[3,48,1024]{2,1,0:T(8,128)(2,1)S(1)}, bf16[3,48,1024]{2,1,0:T(8,128)(2,1)S(1)}, u32[]{:S(2)}, u32[]{:S(2)}) collective-permute-start(bf16[3,48,1024]{2,1,0:T(8,128)(2,1)S(1)} %ring_sum.6.mark_ref.own_ref), channel_id=1, source_target_pairs={{0,1},{1,0},{2,3},{3,2},{4,5},{5,4},{6,7},{7,6},{8,9},{9,8},{10,11... | collective-permute-start | bytes 884744 | tf_op jit(solution)/shard_map/ppermute | solution.py:638
  136.8 26.3 %collective-permute-start.29 = (bf16[3,96,512]{2,1,0:T(8,128)(2,1)S(1)}, bf16[3,96,512]{2,1,0:T(8,128)(2,1)S(1)}, u32[]{:S(2)}, u32[]{:S(2)}) collective-permute-start(bf16[3,96,512]{2,1,0:T(8,128)(2,1)S(1)} %ring_sum.7.mark_ref.own_ref), channel_id=1, source_target_pairs={{0,1},{1,0},{2,3},{3,2},{4,5},{5,4},{6,7},{7,6},{8,9},{9,8},{10,11... | collective-permute-start | bytes 884744 | tf_op jit(solution)/shard_map/ppermute | solution.py:638
  164.0 15.7 %collective-permute-start.30 = (bf16[3,96,256]{2,1,0:T(8,128)(2,1)S(1)}, bf16[3,96,256]{2,1,0:T(8,128)(2,1)S(1)}, u32[]{:S(2)}, u32[]{:S(2)}) collective-permute-start(bf16[3,96,256]{2,1,0:T(8,128)(2,1)S(1)} %get-tuple-element.94), channel_id=1, source_target_pairs={{0,8},{8,16},{16,24},{24,32},{32,40},{40,48},{48,56},{56,64},{64,7... | collective-permute-start | bytes 442376 | tf_op jit(solution)/shard_map/ppermute | solution.py:693
  173.8 8.0 %collective-permute-start.31 = (bf16[3,96,256]{2,1,0:T(8,128)(2,1)S(1)}, bf16[3,96,256]{2,1,0:T(8,128)(2,1)S(1)}, u32[]{:S(2)}, u32[]{:S(2)}) collective-permute-start(bf16[3,96,256]{2,1,0:T(8,128)(2,1)S(1)} %get-tuple-element.93), channel_id=1, source_target_pairs={{8,0},{16,8},{24,16},{32,24},{40,32},{48,40},{56,48},{64,56},{72,6... | collective-permute-start | bytes 442376 | tf_op jit(solution)/shard_map/ppermute | solution.py:694
  (29 other events, 258.9 us)

commit v4 on v3

--- a/solution.py
+++ b/solution.py
@@ -16,6 +16,7 @@
 HALF = 256
 ANY = pl.BlockSpec(memory_space=pl.ANY)
 VMEM = pl.BlockSpec(memory_space=pltpu.VMEM)
+HBM = pl.BlockSpec(memory_space=pltpu.HBM)
 SMEM = pl.BlockSpec(memory_space=pltpu.SMEM)
 
 
@@ -23,8 +24,8 @@
     return pltpu.CompilerParams(vmem_limit_bytes=mib * MIB)
 
 
-def cost(flops, moved):
-    return pl.CostEstimate(flops=int(flops), bytes_accessed=int(moved), transcendentals=0)
+def cost(flops=1, moved=1):
+    return pl.CostEstimate(flops=flops, bytes_accessed=moved, transcendentals=0)
 
 
 def shaped(shape, kind):
@@ -87,7 +88,7 @@
     return pl.pallas_call(
         functools.partial(loads_kernel, cuts),
         out_shape=(shaped((HALF, cols), F32), shaped((HALF, cols), BF16)),
-        in_specs=[SMEM, ANY, ANY],
+        in_specs=[SMEM, HBM, HBM],
         out_specs=(vmem, vmem),
         scratch_shapes=[
             pltpu.VMEM(shapes.shape, BF16),
@@ -97,7 +98,7 @@
             pltpu.SemaphoreType.DMA((len(cuts),)),
         ],
         compiler_params=params(56),
-        cost_estimate=cost(2 * modes * comps * nodes * cols, 2 * comps * nodes * (modes + cols)),
+        cost_estimate=cost(),
         name="modal_loads",
     )(core, shapes, load)
 
@@ -123,8 +124,8 @@
         out_shape=shaped(direct.shape, BF16),
         in_specs=[ANY] + [vmem] * 6,
         out_specs=vmem,
-        compiler_params=params(16),
-        cost_estimate=cost(direct.size * 8, direct.size * 18),
+        compiler_params=params(8),
+        cost_estimate=cost(),
         name="modal_response",
     )(mark, *parts, direct, cross)
 
@@ -150,8 +151,8 @@
         out_shape=shaped((5 * corners, elems), F32),
         in_specs=[ANY, vmem, vmem, vmem],
         out_specs=vmem,
-        compiler_params=params(16),
-        cost_estimate=cost(1000, elems * 4 * 80),
+        compiler_params=params(8),
+        cost_estimate=cost(),
         name="element_data",
     )(mark, conn, grads, modulus[None, :])
 
@@ -214,7 +215,7 @@
     split_ways([value[j * rows : (j + 1) * rows, :] for j in range(Z)], *out_refs)
 
 
-def z_first_terms(mark, resp, shapes, chunk):
+def z_first_terms(mark, resp, shapes, chunk, mib):
     first, width = chunk
     comps, modes, _ = shapes.shape
     cols = resp.shape[0]
@@ -223,11 +224,11 @@
         functools.partial(z_first_kernel, first),
         out_shape=out_shape,
         grid=(comps,),
-        in_specs=[ANY, pl.BlockSpec((cols, modes), lambda i: (0, 0)), ANY],
+        in_specs=[ANY, pl.BlockSpec((cols, modes), lambda i: (0, 0)), HBM],
         out_specs=out_specs,
         scratch_shapes=fetch_scratch(shapes, width),
-        compiler_params=params(24),
-        cost_estimate=cost(2 * modes * comps * width * cols, 2 * comps * width * (modes + cols)),
+        compiler_params=params(mib),
+        cost_estimate=cost(),
         name="z_first_terms",
     )(mark, resp, shapes)
 
@@ -255,7 +256,7 @@
         away_ref[j, 0] = value[(2 * j + 1) * rows : (2 * j + 2) * rows, :]
 
 
-def x_first_terms(core, mine, theirs, order, shapes, chunk):
+def x_first_terms(core, mine, theirs, order, shapes, chunk, mib):
     first, width = chunk
     comps, modes, _ = shapes.shape
     cols = mine.shape[1]
@@ -275,12 +276,12 @@
             pl.BlockSpec((HALF, cols), whole),
             pl.BlockSpec((HALF, cols), whole),
             pl.BlockSpec((cols, cols), whole),
-            ANY,
+            HBM,
         ],
         out_specs=(part, part, pl.BlockSpec((cols, modes), whole)),
         scratch_shapes=[pltpu.VMEM((2 * HALF, cols), BF16)] + fetch_scratch(shapes, width),
-        compiler_params=params(24),
-        cost_estimate=cost(2 * modes * comps * width * cols, 2 * comps * width * (modes + cols)),
+        compiler_params=params(mib),
+        cost_estimate=cost(),
         name="x_first_terms",
     )(core, mine, theirs, order, shapes)
 
@@ -301,8 +302,8 @@
         grid=(comps,),
         in_specs=[ANY, part, part],
         out_specs=out_specs,
-        compiler_params=params(16),
-        cost_estimate=cost(keep.size, keep.size * 6),
+        compiler_params=params(8),
+        cost_estimate=cost(),
         name="x_sum",
     )(mark, keep, got)
 
@@ -323,8 +324,8 @@
         grid=(comps,),
         in_specs=[ANY, one, one, first, first],
         out_specs=(one, one),
-        compiler_params=params(16),
-        cost_estimate=cost(2 * up.size, up.size * 12),
+        compiler_params=params(8),
+        cost_estimate=cost(),
         name="pass_on",
     )(mark, up, down, plus, minus)
 
@@ -348,10 +349,37 @@
         grid=(comps,),
         in_specs=[ANY, one(width), second, second, one(width // 2), one(width // 2)],
         out_specs=one(width),
-        compiler_params=params(16),
-        cost_estimate=cost(2 * own.size, own.size * 8),
+        compiler_params=params(8),
+        cost_estimate=cost(),
         name="ring_sum",
     )(mark, own, plus, minus, up, down)
+
+
+def half_sum_kernel(mark_ref, after_ref, own_ref, direct_ref, passed_ref, out_ref):
+    del mark_ref, after_ref
+    total = own_ref[...].astype(F32) + direct_ref[0].astype(F32) + passed_ref[...].astype(F32)
+    out_ref[...] = total.astype(BF16)
+
+
+def half_sum(mark, after, side, own, direct, passed):
+    comps, rows, half = passed.shape
+    one = pl.BlockSpec((1, rows, half), lambda i: (i, 0, 0))
+    return pl.pallas_call(
+        half_sum_kernel,
+        out_shape=shaped(passed.shape, BF16),
+        grid=(comps,),
+        in_specs=[
+            ANY,
+            ANY,
+            pl.BlockSpec((1, rows, half), lambda i: (i, 0, side)),
+            pl.BlockSpec((1, 1, rows, half), lambda i: (1, i, 0, 0)),
+            one,
+        ],
+        out_specs=one,
+        compiler_params=params(8),
+        cost_estimate=cost(),
+        name="half_sum",
+    )(mark, after, own, direct, passed)
 
 
 def gather_rows_kernel(first, mark_ref, lists_ref, own_ref, got_ref, *refs):
@@ -391,43 +419,101 @@
         grid=(comps,),
         in_specs=specs,
         out_specs=(one(full, width), one(full, count)),
-        compiler_params=params(16),
-        cost_estimate=cost(2 * comps * full * width * count, comps * full * width * 6),
+        compiler_params=params(8),
+        cost_estimate=cost(),
         name="gather_rows",
     )(*args)
 
 
 NODE_BLOCK = 256
+WIDE = 256
 ROWS = 16
 LANES = 128
 
 
-def weights_kernel(first, mark_ref, conn_ref, grads_ref, out_ref):
-    del mark_ref
-    corners, elems = conn_ref.shape
-    nodes = out_ref.shape[1]
+def build_tiles(first, nodes, conn, grads, store):
+    corners = conn.shape[0]
     base = lax.broadcasted_iota(jnp.int32, (ROWS, LANES), 0).astype(F32).astype(BF16)
     zero = jnp.zeros((ROWS, LANES), BF16)
+    grads = grads.astype(BF16)
+    grad = [jnp.broadcast_to(grads[i : i + 1, :], (ROWS, LANES)) for i in range(3 * corners)]
+    for at in range(0, nodes, NODE_BLOCK):
+        keys = (conn - (first + at)).astype(BF16)
+        key = [jnp.broadcast_to(keys[a : a + 1, :], (ROWS, LANES)) for a in range(corners)]
+        for row in range(0, NODE_BLOCK, ROWS):
+            node = base + BF16(row)
+            sums = [zero] * 3
+            for a in range(corners):
+                hit = node == key[a]
+                for d in range(3):
+                    sums[d] = jnp.where(hit, grad[d * corners + a], sums[d])
+            for d in range(3):
+                store(d, at + row, sums[d])
+
+
+def weights_kernel(first, mark_ref, conn_ref, grads_ref, out_ref):
+    del mark_ref
 
     def piece(step, carry):
         cut = pl.ds(pl.multiple_of(step * LANES, LANES), LANES)
-        grads = grads_ref[:, cut].astype(BF16)
-        grad = [jnp.broadcast_to(grads[i : i + 1, :], (ROWS, LANES)) for i in range(3 * corners)]
-        for at in range(0, nodes, NODE_BLOCK):
-            keys = (conn_ref[:, cut] - (first + at)).astype(BF16)
-            key = [jnp.broadcast_to(keys[a : a + 1, :], (ROWS, LANES)) for a in range(corners)]
-            for row in range(0, NODE_BLOCK, ROWS):
-                node = base + BF16(row)
-                sums = [zero] * 3
-                for a in range(corners):
-                    hit = node == key[a]
-                    for d in range(3):
-                        sums[d] = jnp.where(hit, grad[d * corners + a], sums[d])
-                for d in range(3):
-                    out_ref[d, pl.ds(at + row, ROWS), cut] = sums[d]
+
+        def store(d, row, value):
+            out_ref[d, pl.ds(row, ROWS), cut] = value
+
+        build_tiles(first, out_ref.shape[1], conn_ref[:, cut], grads_ref[:, cut], store)
         return carry
 
-    lax.fori_loop(0, elems // LANES, piece, 0)
+    lax.fori_loop(0, conn_ref.shape[1] // LANES, piece, 0)
+
+
+def all_weights_kernel(mark_ref, conn_ref, grads_ref, out_ref, made, sems):
+    del mark_ref
+    blocks, _, nodes, _ = out_ref.shape
+    _, _, count, wide = made.shape
+    parts = nodes // count
+
+    def copy(step, slot):
+        rows = pl.ds(pl.multiple_of((step % parts) * count, count), count)
+        return pltpu.make_async_copy(made.at[slot], out_ref.at[step // parts, :, rows, :], sems.at[slot])
+
+    def pair(twice, carry):
+        for slot in range(2):
+            step = twice * 2 + slot
+
+            @pl.when(twice > 0)
+            def _():
+                copy(step - 2, slot).wait()
+
+            first = ((step % parts) * count).astype(F32)
+            for lane in range(0, wide, LANES):
+                cut = pl.ds(pl.multiple_of((step // parts) * wide + lane, LANES), LANES)
+
+                def store(d, row, value):
+                    made[slot, d, pl.ds(row, ROWS), pl.ds(lane, LANES)] = value
+
+                build_tiles(first, count, conn_ref[:, cut], grads_ref[:, cut], store)
+            copy(step, slot).start()
+        return carry
+
+    steps = blocks * parts
+    lax.fori_loop(0, steps // 2, pair, 0)
+    for slot in range(2):
+        copy(steps - 2 + slot, slot).wait()
+
+
+def all_weights(mark, data, nodes):
+    elems = data.shape[1]
+    count = nodes // 4
+    return pl.pallas_call(
+        all_weights_kernel,
+        out_shape=shaped((elems // WIDE, 3, nodes, WIDE), BF16),
+        in_specs=[ANY, VMEM, VMEM],
+        out_specs=ANY,
+        scratch_shapes=[pltpu.VMEM((2, 3, count, WIDE), BF16), pltpu.SemaphoreType.DMA((2,))],
+        compiler_params=params(12),
+        cost_estimate=cost(),
+        name="all_weights",
+    )(mark, data[:8], data[8:32])
 
 
 def element_weights(mark, data, first, count):
@@ -438,50 +524,57 @@
         in_specs=[ANY, VMEM, VMEM],
         out_specs=VMEM,
         compiler_params=params(8),
-        cost_estimate=cost(count * elems * 1500, 6 * count * elems),
+        cost_estimate=cost(),
         name="element_weights",
     )(mark, data[:8], data[8:32])
 
 
-def multiply_kernel(pieces, mark_ref, values_ref, *refs):
-    del mark_ref
-    weights_refs, rest = refs[:pieces], refs[pieces:]
-    acc_ref, out_ref = rest if len(rest) == 2 else (None,) + rest
+def multiply_kernel(first, mark_ref, values_ref, weights_ref, *refs):
+    del mark_ref
+    acc_ref, out_ref, held, sems = refs if len(refs) == 4 else (None,) + refs
     comps, rows, nodes = values_ref.shape
     values = values_ref[...].reshape(comps * rows, nodes)
-
-    def piece(step, carry):
-        cut = pl.ds(pl.multiple_of(step * WIDE, WIDE), WIDE)
-        for d in range(3):
-            total = None if acc_ref is None else acc_ref[d, :, cut]
-            at = 0
-            for ref in weights_refs:
-                count = ref.shape[1]
-                term = jnp.dot(values[:, at : at + count], ref[d, :, cut], preferred_element_type=F32)
-                total = term if total is None else total + term
-                at += count
-            out_ref[d, :, cut] = total
+    blocks = weights_ref.shape[0]
+
+    def copy(block, slot):
+        return pltpu.make_async_copy(
+            weights_ref.at[block, :, pl.ds(first, nodes), :], held.at[slot], sems.at[slot]
+        )
+
+    for slot in range(2):
+        copy(slot, slot).start()
+
+    def pair(twice, carry):
+        for slot in range(2):
+            block = twice * 2 + slot
+            copy(block, slot).wait()
+            cut = pl.ds(pl.multiple_of(block * WIDE, WIDE), WIDE)
+            for d in range(3):
+                term = jnp.dot(values, held[slot, d], preferred_element_type=F32)
+                out_ref[d, :, cut] = term if acc_ref is None else term + acc_ref[d, :, cut]
+
+            @pl.when(twice < blocks // 2 - 1)
+            def _():
+                copy(block + 2, slot).start()
+
         return carry
 
-    lax.fori_loop(0, out_ref.shape[2] // WIDE, piece, 0)
-
-
-WIDE = 256
-
-
-def multiply(mark, values, weights, acc):
+    lax.fori_loop(0, blocks // 2, pair, 0)
+
+
+def multiply(mark, values, weights, first, acc):
     comps, rows, nodes = values.shape
-    elems = weights[0].shape[2]
-    total = comps * rows
-    args = [mark, values] + list(weights) + ([] if acc is None else [acc])
-    return pl.pallas_call(
-        functools.partial(multiply_kernel, len(weights)),
-        out_shape=shaped((3, total, elems), F32),
-        in_specs=[ANY] + [VMEM] * (len(args) - 1),
+    elems = weights.shape[0] * WIDE
+    args = [mark, values, weights] + ([] if acc is None else [acc])
+    return pl.pallas_call(
+        functools.partial(multiply_kernel, first),
+        out_shape=shaped((3, comps * rows, elems), F32),
+        in_specs=[ANY, VMEM, ANY] + [VMEM] * (len(args) - 3),
         out_specs=VMEM,
-        input_output_aliases={} if acc is None else {len(args) - 1: 0},
-        compiler_params=params(8),
-        cost_estimate=cost(6 * total * nodes * elems, 6 * nodes * elems),
+        input_output_aliases={} if acc is None else {3: 0},
+        scratch_shapes=[pltpu.VMEM((2, 3, nodes, WIDE), BF16), pltpu.SemaphoreType.DMA((2,))],
+        compiler_params=params(20),
+        cost_estimate=cost(),
         name="multiply",
     )(*args)
 
@@ -557,7 +650,7 @@
         out_specs=VMEM,
         scratch_shapes=[pltpu.VMEM((3, comps * rows, WIDE), F32)],
         compiler_params=params(8),
-        cost_estimate=cost(12 * comps * rows * rim * elems, 24 * comps * rows * elems),
+        cost_estimate=cost(),
         name="element_spectra",
     )(before, after, weights, acc, modulus)
 
@@ -574,7 +667,7 @@
         in_specs=[SMEM] + [VMEM] * Z,
         out_specs=VMEM,
         compiler_params=params(8),
-        cost_estimate=cost(1, 8 * Z * blocks[0].size),
+        cost_estimate=cost(),
         name="collect",
     )(place, *blocks)
 
@@ -628,7 +721,7 @@
     pair = (chip.astype(F32) + got.astype(F32)).astype(BF16)
     ring = [pair] + [lax.ppermute(pair, "mesh", mesh_perm(dy)) for dy in range(1, Y)]
 
-    data = element_data(theirs, connectivity, shape_grads, modulus)
+    data = element_data(chip, connectivity, shape_grads, modulus)
     data = jnp.concatenate(
         [data] + [lax.ppermute(data, "mode", mode_perm(-j)) for j in range(1, Z)], axis=1
     )
@@ -638,61 +731,41 @@
     side = lambda v: lax.ppermute(v, "mode", side_perm)
     full = 2 * rows
 
-    w_1, w_0, w_2, w_3 = nodes * 5 // 16, nodes * 4 // 16, nodes * 5 // 16, nodes * 2 // 16
-    c_1, c_0 = (0, w_1), (w_1, w_0)
-    c_2, c_3 = (w_1 + w_0, w_2), (w_1 + w_0 + w_2, w_3)
-
-    part = 2 * NODE_BLOCK
-    early = w_2 - part
-    build = lambda mark, first, count: element_weights(mark, data, first, count)
-    weights_1 = [build(pair, 0, part)]
-    resp_mine = half_response(weights_1[0], ring, direct, cross)
+    w_0 = nodes * 7 // 16
+    w_1 = nodes - w_0
+    c_0, c_1 = (0, w_0), (w_0, w_1)
+    middle = w_0 + w_1 // 2
+
+    resp_mine = half_response(data, ring, direct, cross)
     resp_theirs = lax.ppermute(resp_mine, "mesh", mesh_perm(0, 0, 1))
-    away, keep, resp = x_first_terms(core_arg, resp_mine, resp_theirs, order, shapes, c_0)
+    away, keep, resp = x_first_terms(core_arg, resp_mine, resp_theirs, order, shapes, c_0, 43)
     got_0 = side(away)
-    ways_1 = z_first_terms(keep, resp, shapes, c_1)
+    ways_1 = z_first_terms(keep, resp, shapes, c_1, 43)
     plus_1, minus_1 = up(ways_1[0]), down(ways_1[1])
-    ways_2 = z_first_terms(ways_1[2], resp, shapes, c_2)
-    plus_2, minus_2 = up(ways_2[0]), down(ways_2[1])
-    weights_1.append(build(ways_2[2], part, w_1 - part))
-    on_1 = pass_on(weights_1[1], ways_1[2], ways_1[3], plus_1, minus_1)
+    weights = all_weights(ways_1[2], data, nodes)
+    rim_weights = element_weights(weights, data, nodes, 2 * bound)
+    on_1 = pass_on(rim_weights, ways_1[2], ways_1[3], plus_1, minus_1)
     up_1, down_1 = up(on_1[0]), down(on_1[1])
-    ways_3 = z_first_terms(on_1[0], resp, shapes, c_3)
-    weights_0 = [build(ways_3[2], c_0[0], part)]
-    ways_0 = x_sum(weights_0[0], keep, got_0)
+    ways_0 = x_sum(on_1[0], keep, got_0)
     plus_0, minus_0 = up(ways_0[0]), down(ways_0[1])
-    weights_0.append(build(ways_0[2], c_0[0] + part, w_0 - part))
-    on_2 = pass_on(weights_0[1], ways_2[2], ways_2[3], plus_2, minus_2)
-    up_2, down_2 = up(on_2[0]), down(on_2[1])
-    plus_3, minus_3 = up(ways_3[0]), down(ways_3[1])
-    weights_2 = [build(on_2[0], c_2[0], early)]
-    own_1 = ring_sum(weights_2[0], ways_1[4], plus_1, minus_1, up_1, down_1)
-    side_1 = side(own_1)
-    on_0 = pass_on(own_1, ways_0[2], ways_0[3], plus_0, minus_0)
+    low_1 = half_sum(ways_0[2], ways_0[2], 0, ways_1[4], minus_1, up_1)
+    side_low = side(low_1)
+    high_1 = half_sum(low_1, low_1, 1, ways_1[4], plus_1, down_1)
+    side_high = side(high_1)
+    on_0 = pass_on(high_1, ways_0[2], ways_0[3], plus_0, minus_0)
     up_0, down_0 = up(on_0[0]), down(on_0[1])
-    own_2 = ring_sum(on_0[0], ways_2[4], plus_2, minus_2, up_2, down_2)
-    side_2 = side(own_2)
-    values_1, rim = gather_rows(own_2, lists, own_1, side_1, None, c_1[0], full)
-    acc = multiply(rim, values_1, weights_1, None)
-    on_3 = pass_on(acc, ways_3[2], ways_3[3], plus_3, minus_3)
-    up_3, down_3 = up(on_3[0]), down(on_3[1])
-    own_0 = ring_sum(on_3[0], ways_0[4], plus_0, minus_0, up_0, down_0)
+    values_low, rim = gather_rows(on_0[0], lists, low_1, side_low, None, w_0, full)
+    acc = multiply(rim, values_low, weights, w_0, None)
+    own_0 = ring_sum(acc, ways_0[4], plus_0, minus_0, up_0, down_0)
     side_0 = side(own_0)
-    weights_2.append(build(own_0, c_2[0] + early, w_2 - early))
-    own_3 = ring_sum(weights_2[1], ways_3[4], plus_3, minus_3, up_3, down_3)
-    side_3 = side(own_3)
-    values_2, rim = gather_rows(own_3, lists, own_2, side_2, rim, c_2[0], full)
-    acc = multiply(rim, values_2, weights_2, acc)
-    weights_3 = [build(acc, nodes - w_3, w_3)]
-    values_0, rim = gather_rows(weights_3[0], lists, own_0, side_0, rim, c_0[0], full)
-    acc = multiply(rim, values_0, weights_0, acc)
-    rim_weights = build(acc, nodes, 2 * bound)
-    values_3, rim = gather_rows(rim_weights, lists, own_3, side_3, rim, c_3[0], full)
+    values_high, rim = gather_rows(own_0, lists, high_1, side_high, rim, middle, full)
+    acc = multiply(rim, values_high, weights, middle, acc)
+    values_0, rim = gather_rows(acc, lists, own_0, side_0, rim, 0, full)
 
     count = lax.axis_size("mesh")
     before = lax.ppermute(rim[..., bound:], "mesh", [(p, p + 1) for p in range(count - 1)])
     after = lax.ppermute(rim[..., :bound], "mesh", [(p + 1, p) for p in range(count - 1)])
-    acc = multiply(rim, values_3, weights_3, acc)
+    acc = multiply(rim, values_0, weights, 0, acc)
     spectra = element_spectra(before, after, rim_weights, acc, data[32:40])
     back = [spectra[0]] + [lax.ppermute(spectra[j], "mode", mode_perm(j)) for j in range(1, Z)]
     return collect(z_at.astype(jnp.int32).reshape(1), back)

time: 196 us -> 189 us (0.964)
  Pallas kernels: 81.6 us -> 102 us
  starting transfers between devices: 57.3 us -> 41.3 us
  local copies, waits for them, and re-layouts: 11 us -> 1.16 us
    pallas_call x4 -> x6, Pallas kernels: 22.2 us -> 65 us  [the longest x3 33.4 us: multiply(): pl.pallas_call(functools.partial(multiply_kernel, first), out_shape=shape...]
    pallas_call x8 -> x1, Pallas kernels: 25.9 us -> 2.9 us  [element_weights(): pl.pallas_call(functools.partial(weights_kernel, float(first)), out_shape...]
    unnamed x37 -> x15, local copies, waits for them, and re-layouts: 9.85 us -> 0.03 us
    ppermute x8 -> x4, starting transfers between devices: 19.1 us -> 9.51 us  [local(): down = lambda v: lax.ppermute(v, 'mode', down_perm)]
    ppermute x3, waiting for transfers between devices: 3.95 us -> 11.2 us  [local(): lax.ppermute(pair, 'mesh', mesh_perm(dy))]
    ppermute x8 -> x4, waiting for transfers between devices: 6.44 us -> 0.01 us  [local(): down = lambda v: lax.ppermute(v, 'mode', down_perm)]
    ppermute x1, starting transfers between devices: 9.83 us -> 4.25 us  [local(): lax.ppermute(rim[..., bound:], 'mesh', [(p, p + 1) for p in range(count -...]
    ppermute x1, waiting for transfers between devices: 4.83 us -> 0.01 us  [local(): got = lax.ppermute(chip, 'mesh', mesh_perm(0, 1, 0))]
  transfers between devices with their start and end apart: 35 -> 26, of which waited for: 12 -> 11; matrix products, arithmetic and copies ran while one was open for 1% -> 0% of each run, Pallas kernels for 31% -> 41%
where the time goes in v4:
time: 189 us; the launch traced here: 188 us
  Pallas kernels  102 us (54%)
  waiting for transfers between devices  42 us (22%)
  starting transfers between devices  41.3 us (22%)
    pallas_call x3, Pallas kernels, multiply(): pl.pallas_call(functools.partial(multiply_kernel, first), out_shape=shape...  33.4 us
    pallas_call x1, Pallas kernels, all_weights(): pl.pallas_call(all_weights_kernel, out_shape=shaped((elems // WIDE, 3, no...  30.8 us
    ppermute x4, waiting for transfers between devices, local(): up = lambda v: lax.ppermute(v, 'mode', up_perm)  20.4 us
    ppermute x3, waiting for transfers between devices, local(): lax.ppermute(pair, 'mesh', mesh_perm(dy))  11.2 us
    pallas_call x1, Pallas kernels, partial_loads(): pl.pallas_call(functools.partial(loads_kernel, cuts), out_shape=(shaped((...  11.1 us
    ppermute x4, starting transfers between devices, local(): down = lambda v: lax.ppermute(v, 'mode', down_perm)  9.51 us
    ppermute x1, starting transfers between devices, local(): lax.ppermute(rim[..., :bound], 'mesh', [(p + 1, p) for p in range(count -...  6.16 us
    pallas_call x1, Pallas kernels, element_spectra(): pl.pallas_call(spectra_kernel, out_shape=shaped((Z, 36, elems // Z), F32)...  6.1 us
  transfers between devices with their start and end apart: 26, of which 11 were waited for; matrix products, arithmetic and copies ran while one was open for 0% of the time, Pallas kernels for 41%

profile of v4, /device:TPU:1, one launch (start us, length us, event | category | flops | bytes accessed | tf_op | source)
XLA Modules:
  0.0 188.1 jit_solution(3152220214098723723)
XLA Ops:
  0.0 11.1 %modal_loads.1 = (f32[256,384]{1,0:T(8,128)}, bf16[256,384]{1,0:T(8,128)(2,1)}) custom-call(s32[1]{0:T(128)} %bitcast.1.core_ref, bf16[3,500,4096]{2,1,0:T(8,128)(2,1)} %bitcast.19, bf16[3,4096,384]{2,1,0:T(8,128)(2,1)} %load_ref.1), custom_call_target="tpu_custom_call" | custom-call | flops 1 | bytes 1 | tf_op jit(solution)/shard_map/modal_loads/pallas_call | solution.py:88
  15.0 2.9 %collective-permute-start.4 = (bf16[256,384]{1,0:T(8,128)(2,1)S(1)}, bf16[256,384]{1,0:T(8,128)(2,1)S(1)}, u32[]{:S(2)}, u32[]{:S(2)}) collective-permute-start(bf16[256,384]{1,0:T(8,128)(2,1)S(1)} %add_convert_fusion.1.mark_ref), channel_id=1, source_target_pairs={{0,16},{8,24},{16,0},{24,8},{32,48},{40,56},{48,32},{56,40},{64,80... | collective-permute-start | bytes 589832 | tf_op jit(solution)/shard_map/ppermute | solution.py:720
  19.9 3.3 %collective-permute-start.2 = (f32[40,512]{1,0:T(8,128)S(1)}, f32[40,512]{1,0:T(8,128)S(1)}, u32[]{:S(2)}, u32[]{:S(2)}) collective-permute-start(f32[40,512]{1,0:T(8,128)S(1)} %element_data.1), channel_id=1, source_target_pairs={{0,4},{1,5},{2,6},{3,7},{4,0},{5,1},{6,2},{7,3},{8,12},{9,13},{10,... | collective-permute-start | bytes 245768 | tf_op jit(solution)/shard_map/ppermute | solution.py:726
  24.0 2.8 %collective-permute-start.7 = (bf16[256,384]{1,0:T(8,128)(2,1)S(1)}, bf16[256,384]{1,0:T(8,128)(2,1)S(1)}, u32[]{:S(2)}, u32[]{:S(2)}) collective-permute-start(bf16[256,384]{1,0:T(8,128)(2,1)S(1)} %add_convert_fusion.a_ref), channel_id=1, source_target_pairs={{0,96},{8,104},{16,112},{24,120},{32,0},{40,8},{48,16},{56,24},{64... | collective-permute-start | bytes 589832 | tf_op jit(solution)/shard_map/ppermute | solution.py:722
  27.9 3.8 %collective-permute-done.7.d_ref = bf16[256,384]{1,0:T(8,128)(2,1)S(1)} collective-permute-done((bf16[256,384]{1,0:T(8,128)(2,1)S(1)}, bf16[256,384]{1,0:T(8,128)(2,1)S(1)}, u32[]{:S(2)}, u32[]{:S(2)}) %collective-permute-start.7) | collective-permute-done | bytes 196640 | tf_op jit(solution)/shard_map/ppermute | solution.py:722
  32.9 6.2 %collective-permute-done.5.b_ref = bf16[256,384]{1,0:T(8,128)(2,1)S(1)} collective-permute-done((bf16[256,384]{1,0:T(8,128)(2,1)S(1)}, bf16[256,384]{1,0:T(8,128)(2,1)S(1)}, u32[]{:S(2)}, u32[]{:S(2)}) %collective-permute-start.5) | collective-permute-done | bytes 196640 | tf_op jit(solution)/shard_map/ppermute | solution.py:722
  41.3 5.2 %x_first_terms.1 = (bf16[4,3,48,1792]{3,2,1,0:T(8,128)(2,1)S(1)}, bf16[4,3,48,1792]{3,2,1,0:T(8,128)(2,1)S(1)}, bf16[384,500]{1,0:T(8,128)(2,1)S(1)}) custom-call(s32[1]{0:T(128)} %bitcast.1.core_ref, bf16[256,384]{1,0:T(8,128)(2,1)S(1)} %modal_response.1.mine_ref, bf16[256,384]{1,0:T(8,128)(2,1)S(1)} %collective-permute-done.8.theirs_ref, ...), custom_call_target="tpu_custom_call" | custom-call | flops 1 | bytes 1 | tf_op jit(solution)/shard_map/x_first_terms/pallas_call | solution.py:266
  46.9 5.1 %z_first_terms.1 = (bf16[2,3,96,1152]{3,2,1,0:T(8,128)(2,1)S(1)}, bf16[2,3,96,1152]{3,2,1,0:T(8,128)(2,1)S(1)}, bf16[3,96,1152]{2,1,0:T(8,128)(2,1)S(1)}, bf16[3...) custom-call(bf16[4,3,48,1792]{3,2,1,0:T(8,128)(2,1)S(1)} %get-tuple-element.32.mark_ref.keep_ref, ...), custom_call_target="tpu_custom_call" | custom-call | flops 1 | bytes 1 | tf_op jit(solution)/shard_map/z_first_terms/pallas_call | solution.py:223
  53.6 2.4 %collective-permute-start.10 = (bf16[2,3,96,1152]{3,2,1,0:T(8,128)(2,1)S(1)}, bf16[2,3,96,1152]{3,2,1,0:T(8,128)(2,1)S(1)}, u32[]{:S(2)}, u32[]{:S(2)}) collective-permute-start(bf16[2,3,96,1152]{3,2,1,0:T(8,128)(2,1)S(1)} %get-tuple-element.37), channel_id=1, source_target_pairs={{0,6},{1,7},{2,0},{3,1},{4,2},{5,3},{6,4},{7,5},{8,14},{9,15},{10,... | collective-permute-start | bytes 3981320 | tf_op jit(solution)/shard_map/ppermute | solution.py:730
  56.0 30.8 %all_weights.1.mark_ref.weights_ref = bf16[8,3,4096,256]{3,2,1,0:T(8,128)(2,1)} custom-call(bf16[3,96,1152]{2,1,0:T(8,128)(2,1)S(1)} %get-tuple-element.34.mark_ref.up_ref, f32[8,2048]{1,0:T(8,128)S(1)} %get-tuple-element.60.conn_ref, f32[24,2048]{1,0:T(8,128)S(1)} %slice.39.grads_ref), custom_call_target="tpu_custom_call" | custom-call | flops 1 | bytes 1 | tf_op jit(solution)/shard_map/all_weights/pallas_call | solution.py:507
  86.8 2.9 %element_weights.1.mark_ref.weights_ref = bf16[3,512,2048]{2,1,0:T(8,128)(2,1)S(1)} custom-call(bf16[8,3,4096,256]{3,2,1,0:T(8,128)(2,1)} %all_weights.1.mark_ref.weights_ref, f32[8,2048]{1,0:T(8,128)S(1)} %get-tuple-element.60.conn_ref, f32[24,2048]{1,0:T(8,128)S(1)} %slice.39.grads_ref), custom_call_target="tpu_custom_call" | custom-call | flops 1 | bytes 1 | tf_op jit(solution)/shard_map/element_weights/pallas_call | solution.py:521
  90.2 2.7 %collective-permute-start.13 = (bf16[3,96,1152]{2,1,0:T(8,128)(2,1)S(1)}, bf16[3,96,1152]{2,1,0:T(8,128)(2,1)S(1)}, u32[]{:S(2)}, u32[]{:S(2)}) collective-permute-start(bf16[3,96,1152]{2,1,0:T(8,128)(2,1)S(1)} %get-tuple-element.42), channel_id=1, source_target_pairs={{0,6},{1,7},{2,0},{3,1},{4,2},{5,3},{6,4},{7,5},{8,14},{9,15},{10,... | collective-permute-start | bytes 1990664 | tf_op jit(solution)/shard_map/ppermute | solution.py:730
  96.5 10.4 %collective-permute-done.12.passed_ref = bf16[3,96,1152]{2,1,0:T(8,128)(2,1)S(1)} collective-permute-done((bf16[3,96,1152]{2,1,0:T(8,128)(2,1)S(1)}, bf16[3,96,1152]{2,1,0:T(8,128)(2,1)S(1)}, u32[]{:S(2)}, u32[]{:S(2)}) %collective-permute-start.12) | collective-permute-done | bytes 663584 | tf_op jit(solution)/shard_map/ppermute | solution.py:729
  107.9 10.0 %collective-permute-done.14.plus_ref = bf16[2,3,48,896]{3,2,1,0:T(8,128)(2,1)S(1)} collective-permute-done((bf16[2,3,48,896]{3,2,1,0:T(8,128)(2,1)S(1)}, bf16[2,3,48,896]{3,2,1,0:T(8,128)(2,1)S(1)}, u32[]{:S(2)}, u32[]{:S(2)}) %collective-permute-start.14) | collective-permute-done | bytes 516128 | tf_op jit(solution)/shard_map/ppermute | solution.py:729
  118.1 2.5 %collective-permute-start.18 = (bf16[3,48,896]{2,1,0:T(8,128)(2,1)S(1)}, bf16[3,48,896]{2,1,0:T(8,128)(2,1)S(1)}, u32[]{:S(2)}, u32[]{:S(2)}) collective-permute-start(bf16[3,48,896]{2,1,0:T(8,128)(2,1)S(1)} %get-tuple-element.50), channel_id=1, source_target_pairs={{0,6},{1,7},{2,0},{3,1},{4,2},{5,3},{6,4},{7,5},{8,14},{9,15},{10,... | collective-permute-start | bytes 774152 | tf_op jit(solution)/shard_map/ppermute | solution.py:730
  122.1 10.2 %multiply.3.mark_ref.refs_0_ = f32[3,288,2048]{2,1,0:T(8,128)S(1)} custom-call(bf16[3,96,512]{2,1,0:T(8,128)(2,1)S(1)} %get-tuple-element.47.mark_ref.refs_0_, bf16[3,96,1152]{2,1,0:T(8,128)(2,1)S(1)} %get-tuple-element.48.values_ref, bf16[8,3,4096,256]{3,2,1,0:T(8,128)(2,1)} %all_weights.1.mark_ref.weights_ref), custom_call_target="tpu_custom_call" | custom-call | flops 1 | bytes 1 | tf_op jit(solution)/shard_map/multiply/pallas_call | solution.py:569
  133.9 2.6 %collective-permute-done.19.got_ref = bf16[3,96,1152]{2,1,0:T(8,128)(2,1)S(1)} collective-permute-done((bf16[3,96,1152]{2,1,0:T(8,128)(2,1)S(1)}, bf16[3,96,1152]{2,1,0:T(8,128)(2,1)S(1)}, u32[]{:S(2)}, u32[]{:S(2)}) %collective-permute-start.19) | collective-permute-done | bytes 663584 | tf_op jit(solution)/shard_map/ppermute | solution.py:731
  137.9 10.2 %multiply.4.mark_ref.refs_0_ = f32[3,288,2048]{2,1,0:T(8,128)S(1)} custom-call(bf16[3,96,512]{2,1,0:T(8,128)(2,1)S(1)} %get-tuple-element.51.mark_ref.refs_0_, bf16[3,96,1152]{2,1,0:T(8,128)(2,1)S(1)} %get-tuple-element.52.values_ref, bf16[8,3,4096,256]{3,2,1,0:T(8,128)(2,1)} %all_weights.1.mark_ref.weights_ref, ...), custom_call_target="tpu_custom_call", output_to_operand_aliasing={{}: (3, {})} | custom-call | flops 1 | bytes 1 | tf_op jit(solution)/shard_map/multiply/pallas_call | solution.py:569
  149.6 6.2 %collective-permute-start.22 = (bf16[3,96,256]{2,1,0:T(8,128)(2,1)S(1)}, bf16[3,96,256]{2,1,0:T(8,128)(2,1)S(1)}, u32[]{:S(2)}, u32[]{:S(2)}) collective-permute-start(bf16[3,96,256]{2,1,0:T(8,128)(2,1)S(1)} %get-tuple-element.61), channel_id=1, source_target_pairs={{8,0},{16,8},{24,16},{32,24},{40,32},{48,40},{56,48},{64,56},{72,6... | collective-permute-start | bytes 442376 | tf_op jit(solution)/shard_map/ppermute | solution.py:767
  155.7 4.3 %collective-permute-start.21 = (bf16[3,96,256]{2,1,0:T(8,128)(2,1)S(1)}, bf16[3,96,256]{2,1,0:T(8,128)(2,1)S(1)}, u32[]{:S(2)}, u32[]{:S(2)}) collective-permute-start(bf16[3,96,256]{2,1,0:T(8,128)(2,1)S(1)} %get-tuple-element.62), channel_id=1, source_target_pairs={{0,8},{8,16},{16,24},{24,32},{32,40},{40,48},{48,56},{56,64},{64,7... | collective-permute-start | bytes 442376 | tf_op jit(solution)/shard_map/ppermute | solution.py:766
  160.0 13.0 %multiply.5.acc_ref = f32[3,288,2048]{2,1,0:T(8,128)S(1)} custom-call(bf16[3,96,512]{2,1,0:T(8,128)(2,1)S(1)} %get-tuple-element.53.mark_ref, bf16[3,96,1792]{2,1,0:T(8,128)(2,1)S(1)} %get-tuple-element.54.values_ref, bf16[8,3,4096,256]{3,2,1,0:T(8,128)(2,1)} %all_weights.1.mark_ref.weights_ref, ...), custom_call_target="tpu_custom_call", output_to_operand_aliasing={{}: (3, {})} | custom-call | flops 1 | bytes 1 | tf_op jit(solution)/shard_map/multiply/pallas_call | solution.py:569
  173.1 6.1 %element_spectra.1 = f32[4,36,512]{2,1,0:T(8,128)S(1)} custom-call(bf16[3,96,256]{2,1,0:T(8,128)(2,1)S(1)} %collective-permute-done.21.before_ref, bf16[3,96,256]{2,1,0:T(8,128)(2,1)S(1)} %collective-permute-done.22.after_ref, bf16[3,512,2048]{2,1,0:T(8,128)(2,1)S(1)} %element_weights.1.mark_ref.weights_ref, f32[3,288,2048]{2,1,0:T(8,128)S(1)} %multiply.5.acc_ref, ...), custom_call_target="tpu_custom_call" | custom-call | flops 1 | bytes 1 | tf_op jit(solution)/shard_map/element_spectra/pallas_call | solution.py:646
  181.3 2.4 %collective-permute-done.25.d_ref = f32[36,512]{1,0:T(8,128)S(1)} collective-permute-done((f32[36,512]{1,0:T(8,128)S(1)}, f32[36,512]{1,0:T(8,128)S(1)}, u32[]{:S(2)}, u32[]{:S(2)}) %collective-permute-start.25) | collective-permute-done | bytes 73760 | tf_op jit(solution)/shard_map/ppermute | solution.py:770
  183.7 2.6 %collective-permute-done.24.c_ref = f32[36,512]{1,0:T(8,128)S(1)} collective-permute-done((f32[36,512]{1,0:T(8,128)S(1)}, f32[36,512]{1,0:T(8,128)S(1)}, u32[]{:S(2)}, u32[]{:S(2)}) %collective-permute-start.24) | collective-permute-done | bytes 73760 | tf_op jit(solution)/shard_map/ppermute | solution.py:770
  (80 shorter events, 28.1 us)
Async XLA Ops:
  15.0 8.9 %collective-permute-start.4 = (bf16[256,384]{1,0:T(8,128)(2,1)S(1)}, bf16[256,384]{1,0:T(8,128)(2,1)S(1)}, u32[]{:S(2)}, u32[]{:S(2)}) collective-permute-start(bf16[256,384]{1,0:T(8,128)(2,1)S(1)} %add_convert_fusion.1.mark_ref), channel_id=1, source_target_pairs={{0,16},{8,24},{16,0},{24,8},{32,48},{40,56},{48,32},{56,40},{64,80... | collective-permute-start | bytes 589832 | tf_op jit(solution)/shard_map/ppermute | solution.py:720
  18.2 9.0 %collective-permute-start.3 = (f32[40,512]{1,0:T(8,128)S(1)}, f32[40,512]{1,0:T(8,128)S(1)}, u32[]{:S(2)}, u32[]{:S(2)}) collective-permute-start(f32[40,512]{1,0:T(8,128)S(1)} %element_data.1), channel_id=1, source_target_pairs={{0,2},{1,3},{2,4},{3,5},{4,6},{5,7},{6,0},{7,1},{8,10},{9,11},{10,... | collective-permute-start | bytes 245768 | tf_op jit(solution)/shard_map/ppermute | solution.py:726
  19.9 7.9 %collective-permute-start.2 = (f32[40,512]{1,0:T(8,128)S(1)}, f32[40,512]{1,0:T(8,128)S(1)}, u32[]{:S(2)}, u32[]{:S(2)}) collective-permute-start(f32[40,512]{1,0:T(8,128)S(1)} %element_data.1), channel_id=1, source_target_pairs={{0,4},{1,5},{2,6},{3,7},{4,0},{5,1},{6,2},{7,3},{8,12},{9,13},{10,... | collective-permute-start | bytes 245768 | tf_op jit(solution)/shard_map/ppermute | solution.py:726
  23.2 4.6 %collective-permute-start.1 = (f32[40,512]{1,0:T(8,128)S(1)}, f32[40,512]{1,0:T(8,128)S(1)}, u32[]{:S(2)}, u32[]{:S(2)}) collective-permute-start(f32[40,512]{1,0:T(8,128)S(1)} %element_data.1), channel_id=1, source_target_pairs={{0,6},{1,7},{2,0},{3,1},{4,2},{5,3},{6,4},{7,5},{8,14},{9,15},{10,... | collective-permute-start | bytes 245768 | tf_op jit(solution)/shard_map/ppermute | solution.py:726
  24.0 7.6 %collective-permute-start.7 = (bf16[256,384]{1,0:T(8,128)(2,1)S(1)}, bf16[256,384]{1,0:T(8,128)(2,1)S(1)}, u32[]{:S(2)}, u32[]{:S(2)}) collective-permute-start(bf16[256,384]{1,0:T(8,128)(2,1)S(1)} %add_convert_fusion.a_ref), channel_id=1, source_target_pairs={{0,96},{8,104},{16,112},{24,120},{32,0},{40,8},{48,16},{56,24},{64... | collective-permute-start | bytes 589832 | tf_op jit(solution)/shard_map/ppermute | solution.py:722
  26.8 6.1 %collective-permute-start.6 = (bf16[256,384]{1,0:T(8,128)(2,1)S(1)}, bf16[256,384]{1,0:T(8,128)(2,1)S(1)}, u32[]{:S(2)}, u32[]{:S(2)}) collective-permute-start(bf16[256,384]{1,0:T(8,128)(2,1)S(1)} %add_convert_fusion.a_ref), channel_id=1, source_target_pairs={{0,64},{8,72},{16,80},{24,88},{32,96},{40,104},{48,112},{56,120},{... | collective-permute-start | bytes 589832 | tf_op jit(solution)/shard_map/ppermute | solution.py:722
  27.2 11.9 %collective-permute-start.5 = (bf16[256,384]{1,0:T(8,128)(2,1)S(1)}, bf16[256,384]{1,0:T(8,128)(2,1)S(1)}, u32[]{:S(2)}, u32[]{:S(2)}) collective-permute-start(bf16[256,384]{1,0:T(8,128)(2,1)S(1)} %add_convert_fusion.a_ref), channel_id=1, source_target_pairs={{0,32},{8,40},{16,48},{24,56},{32,64},{40,72},{48,80},{56,88},{64,... | collective-permute-start | bytes 589832 | tf_op jit(solution)/shard_map/ppermute | solution.py:722
  46.5 46.3 %collective-permute-start.11 = (bf16[4,3,48,1792]{3,2,1,0:T(8,128)(2,1)S(1)}, bf16[4,3,48,1792]{3,2,1,0:T(8,128)(2,1)S(1)}, u32[]{:S(2)}, u32[]{:S(2)}) collective-permute-start(bf16[4,3,48,1792]{3,2,1,0:T(8,128)(2,1)S(1)} %get-tuple-element.39), channel_id=1, source_target_pairs={{0,1},{1,0},{2,3},{3,2},{4,5},{5,4},{6,7},{7,6},{8,9},{9,8},{10,11... | collective-permute-start | bytes 6193160 | tf_op jit(solution)/shard_map/ppermute | solution.py:731
  52.1 37.6 %collective-permute-start.9 = (bf16[2,3,96,1152]{3,2,1,0:T(8,128)(2,1)S(1)}, bf16[2,3,96,1152]{3,2,1,0:T(8,128)(2,1)S(1)}, u32[]{:S(2)}, u32[]{:S(2)}) collective-permute-start(bf16[2,3,96,1152]{3,2,1,0:T(8,128)(2,1)S(1)} %get-tuple-element.36), channel_id=1, source_target_pairs={{0,2},{1,3},{2,4},{3,5},{4,6},{5,7},{6,0},{7,1},{8,10},{9,11},{10,... | collective-permute-start | bytes 3981320 | tf_op jit(solution)/shard_map/ppermute | solution.py:729
  53.6 36.2 %collective-permute-start.10 = (bf16[2,3,96,1152]{3,2,1,0:T(8,128)(2,1)S(1)}, bf16[2,3,96,1152]{3,2,1,0:T(8,128)(2,1)S(1)}, u32[]{:S(2)}, u32[]{:S(2)}) collective-permute-start(bf16[2,3,96,1152]{3,2,1,0:T(8,128)(2,1)S(1)} %get-tuple-element.37), channel_id=1, source_target_pairs={{0,6},{1,7},{2,0},{3,1},{4,2},{5,3},{6,4},{7,5},{8,14},{9,15},{10,... | collective-permute-start | bytes 3981320 | tf_op jit(solution)/shard_map/ppermute | solution.py:730
  90.1 16.8 %collective-permute-start.12 = (bf16[3,96,1152]{2,1,0:T(8,128)(2,1)S(1)}, bf16[3,96,1152]{2,1,0:T(8,128)(2,1)S(1)}, u32[]{:S(2)}, u32[]{:S(2)}) collective-permute-start(bf16[3,96,1152]{2,1,0:T(8,128)(2,1)S(1)} %get-tuple-element.38.mark_ref), channel_id=1, source_target_pairs={{0,2},{1,3},{2,4},{3,5},{4,6},{5,7},{6,0},{7,1},{8,10},{9,11},{10,... | collective-permute-start | bytes 1990664 | tf_op jit(solution)/shard_map/ppermute | solution.py:729
  90.2 17.3 %collective-permute-start.13 = (bf16[3,96,1152]{2,1,0:T(8,128)(2,1)S(1)}, bf16[3,96,1152]{2,1,0:T(8,128)(2,1)S(1)}, u32[]{:S(2)}, u32[]{:S(2)}) collective-permute-start(bf16[3,96,1152]{2,1,0:T(8,128)(2,1)S(1)} %get-tuple-element.42), channel_id=1, source_target_pairs={{0,6},{1,7},{2,0},{3,1},{4,2},{5,3},{6,4},{7,5},{8,14},{9,15},{10,... | collective-permute-start | bytes 1990664 | tf_op jit(solution)/shard_map/ppermute | solution.py:730
  93.8 24.2 %collective-permute-start.14 = (bf16[2,3,48,896]{3,2,1,0:T(8,128)(2,1)S(1)}, bf16[2,3,48,896]{3,2,1,0:T(8,128)(2,1)S(1)}, u32[]{:S(2)}, u32[]{:S(2)}) collective-permute-start(bf16[2,3,48,896]{3,2,1,0:T(8,128)(2,1)S(1)} %get-tuple-element.44), channel_id=1, source_target_pairs={{0,2},{1,3},{2,4},{3,5},{4,6},{5,7},{6,0},{7,1},{8,10},{9,11},{10,... | collective-permute-start | bytes 1548296 | tf_op jit(solution)/shard_map/ppermute | solution.py:729
  94.5 23.4 %collective-permute-start.15 = (bf16[2,3,48,896]{3,2,1,0:T(8,128)(2,1)S(1)}, bf16[2,3,48,896]{3,2,1,0:T(8,128)(2,1)S(1)}, u32[]{:S(2)}, u32[]{:S(2)}) collective-permute-start(bf16[2,3,48,896]{3,2,1,0:T(8,128)(2,1)S(1)} %get-tuple-element.45), channel_id=1, source_target_pairs={{0,6},{1,7},{2,0},{3,1},{4,2},{5,3},{6,4},{7,5},{8,14},{9,15},{10,... | collective-permute-start | bytes 1548296 | tf_op jit(solution)/shard_map/ppermute | solution.py:730
  107.3 13.5 %collective-permute-start.16 = (bf16[3,96,1152]{2,1,0:T(8,128)(2,1)S(1)}, bf16[3,96,1152]{2,1,0:T(8,128)(2,1)S(1)}, u32[]{:S(2)}, u32[]{:S(2)}) collective-permute-start(bf16[3,96,1152]{2,1,0:T(8,128)(2,1)S(1)} %half_sum.2.mark_ref.after_ref.own_ref), channel_id=1, source_target_pairs={{0,1},{1,0},{2,3},{3,2},{4,5},{5,4},{6,7},{7,6},{8,9},{9,8},{10,11... | collective-permute-start | bytes 1990664 | tf_op jit(solution)/shard_map/ppermute | solution.py:731
  118.1 14.2 %collective-permute-start.18 = (bf16[3,48,896]{2,1,0:T(8,128)(2,1)S(1)}, bf16[3,48,896]{2,1,0:T(8,128)(2,1)S(1)}, u32[]{:S(2)}, u32[]{:S(2)}) collective-permute-start(bf16[3,48,896]{2,1,0:T(8,128)(2,1)S(1)} %get-tuple-element.50), channel_id=1, source_target_pairs={{0,6},{1,7},{2,0},{3,1},{4,2},{5,3},{6,4},{7,5},{8,14},{9,15},{10,... | collective-permute-start | bytes 774152 | tf_op jit(solution)/shard_map/ppermute | solution.py:730
  120.5 11.7 %collective-permute-start.17 = (bf16[3,48,896]{2,1,0:T(8,128)(2,1)S(1)}, bf16[3,48,896]{2,1,0:T(8,128)(2,1)S(1)}, u32[]{:S(2)}, u32[]{:S(2)}) collective-permute-start(bf16[3,48,896]{2,1,0:T(8,128)(2,1)S(1)} %get-tuple-element.46.mark_ref), channel_id=1, source_target_pairs={{0,2},{1,3},{2,4},{3,5},{4,6},{5,7},{6,0},{7,1},{8,10},{9,11},{10,... | collective-permute-start | bytes 774152 | tf_op jit(solution)/shard_map/ppermute | solution.py:729
  120.5 16.0 %collective-permute-start.19 = (bf16[3,96,1152]{2,1,0:T(8,128)(2,1)S(1)}, bf16[3,96,1152]{2,1,0:T(8,128)(2,1)S(1)}, u32[]{:S(2)}, u32[]{:S(2)}) collective-permute-start(bf16[3,96,1152]{2,1,0:T(8,128)(2,1)S(1)} %half_sum.3.mark_ref.own_ref), channel_id=1, source_target_pairs={{0,1},{1,0},{2,3},{3,2},{4,5},{5,4},{6,7},{7,6},{8,9},{9,8},{10,11... | collective-permute-start | bytes 1990664 | tf_op jit(solution)/shard_map/ppermute | solution.py:731
  132.5 15.6 %collective-permute-start.20 = (bf16[3,48,1792]{2,1,0:T(8,128)(2,1)S(1)}, bf16[3,48,1792]{2,1,0:T(8,128)(2,1)S(1)}, u32[]{:S(2)}, u32[]{:S(2)}) collective-permute-start(bf16[3,48,1792]{2,1,0:T(8,128)(2,1)S(1)} %ring_sum.1.mark_ref.own_ref), channel_id=1, source_target_pairs={{0,1},{1,0},{2,3},{3,2},{4,5},{5,4},{6,7},{7,6},{8,9},{9,8},{10,11... | collective-permute-start | bytes 1548296 | tf_op jit(solution)/shard_map/ppermute | solution.py:731
  149.6 23.5 %collective-permute-start.22 = (bf16[3,96,256]{2,1,0:T(8,128)(2,1)S(1)}, bf16[3,96,256]{2,1,0:T(8,128)(2,1)S(1)}, u32[]{:S(2)}, u32[]{:S(2)}) collective-permute-start(bf16[3,96,256]{2,1,0:T(8,128)(2,1)S(1)} %get-tuple-element.61), channel_id=1, source_target_pairs={{8,0},{16,8},{24,16},{32,24},{40,32},{48,40},{56,48},{64,56},{72,6... | collective-permute-start | bytes 442376 | tf_op jit(solution)/shard_map/ppermute | solution.py:767
  155.7 17.3 %collective-permute-start.21 = (bf16[3,96,256]{2,1,0:T(8,128)(2,1)S(1)}, bf16[3,96,256]{2,1,0:T(8,128)(2,1)S(1)}, u32[]{:S(2)}, u32[]{:S(2)}) collective-permute-start(bf16[3,96,256]{2,1,0:T(8,128)(2,1)S(1)} %get-tuple-element.62), channel_id=1, source_target_pairs={{0,8},{8,16},{16,24},{24,32},{32,40},{40,48},{48,56},{56,64},{64,7... | collective-permute-start | bytes 442376 | tf_op jit(solution)/shard_map/ppermute | solution.py:766
  179.2 4.5 %collective-permute-start.25 = (f32[36,512]{1,0:T(8,128)S(1)}, f32[36,512]{1,0:T(8,128)S(1)}, u32[]{:S(2)}, u32[]{:S(2)}) collective-permute-start(f32[36,512]{1,0:T(8,128)S(1)} %get-tuple-element.55), channel_id=1, source_target_pairs={{0,6},{1,7},{2,0},{3,1},{4,2},{5,3},{6,4},{7,5},{8,14},{9,15},{10,... | collective-permute-start | bytes 221192 | tf_op jit(solution)/shard_map/ppermute | solution.py:770
  180.7 5.7 %collective-permute-start.24 = (f32[36,512]{1,0:T(8,128)S(1)}, f32[36,512]{1,0:T(8,128)S(1)}, u32[]{:S(2)}, u32[]{:S(2)}) collective-permute-start(f32[36,512]{1,0:T(8,128)S(1)} %get-tuple-element.56), channel_id=1, source_target_pairs={{0,4},{1,5},{2,6},{3,7},{4,0},{5,1},{6,2},{7,3},{8,12},{9,13},{10,... | collective-permute-start | bytes 221192 | tf_op jit(solution)/shard_map/ppermute | solution.py:770
  180.7 6.5 %collective-permute-start.23 = (f32[36,512]{1,0:T(8,128)S(1)}, f32[36,512]{1,0:T(8,128)S(1)}, u32[]{:S(2)}, u32[]{:S(2)}) collective-permute-start(f32[36,512]{1,0:T(8,128)S(1)} %get-tuple-element.57), channel_id=1, source_target_pairs={{0,2},{1,3},{2,4},{3,5},{4,6},{5,7},{6,0},{7,1},{8,10},{9,11},{10,... | collective-permute-start | bytes 221192 | tf_op jit(solution)/shard_map/ppermute | solution.py:770
  (9 other events, 110.3 us)

commit v5 on v4

--- a/solution.py
+++ b/solution.py
@@ -469,48 +469,53 @@
 def all_weights_kernel(mark_ref, conn_ref, grads_ref, out_ref, made, sems):
     del mark_ref
     blocks, _, nodes, _ = out_ref.shape
-    _, _, count, wide = made.shape
+    slots, _, count, wide = made.shape
     parts = nodes // count
 
-    def copy(step, slot):
-        rows = pl.ds(pl.multiple_of((step % parts) * count, count), count)
-        return pltpu.make_async_copy(made.at[slot], out_ref.at[step // parts, :, rows, :], sems.at[slot])
-
-    def pair(twice, carry):
-        for slot in range(2):
-            step = twice * 2 + slot
-
-            @pl.when(twice > 0)
+    def copies(block, part, slot):
+        rows = pl.ds(part * count, count)
+        return [
+            pltpu.make_async_copy(made.at[slot, d], out_ref.at[block, d, rows, :], sems.at[slot, d])
+            for d in range(3)
+        ]
+
+    def block_of_elements(block, carry):
+        for part in range(parts):
+            slot = part % slots
+
+            @pl.when(block > 0)
             def _():
-                copy(step - 2, slot).wait()
-
-            first = ((step % parts) * count).astype(F32)
+                for copy in copies(block - 1, part, slot):
+                    copy.wait()
+
             for lane in range(0, wide, LANES):
-                cut = pl.ds(pl.multiple_of((step // parts) * wide + lane, LANES), LANES)
+                cut = pl.ds(pl.multiple_of(block * wide + lane, LANES), LANES)
 
                 def store(d, row, value):
                     made[slot, d, pl.ds(row, ROWS), pl.ds(lane, LANES)] = value
 
-                build_tiles(first, count, conn_ref[:, cut], grads_ref[:, cut], store)
-            copy(step, slot).start()
+                build_tiles(float(part * count), count, conn_ref[:, cut], grads_ref[:, cut], store)
+            for copy in copies(block, part, slot):
+                copy.start()
         return carry
 
-    steps = blocks * parts
-    lax.fori_loop(0, steps // 2, pair, 0)
-    for slot in range(2):
-        copy(steps - 2 + slot, slot).wait()
+    lax.fori_loop(0, blocks, block_of_elements, 0)
+    for part in range(parts):
+        for copy in copies(blocks - 1, part, part):
+            copy.wait()
 
 
 def all_weights(mark, data, nodes):
     elems = data.shape[1]
-    count = nodes // 4
+    slots = 4
+    count = nodes // slots
     return pl.pallas_call(
         all_weights_kernel,
         out_shape=shaped((elems // WIDE, 3, nodes, WIDE), BF16),
         in_specs=[ANY, VMEM, VMEM],
         out_specs=ANY,
-        scratch_shapes=[pltpu.VMEM((2, 3, count, WIDE), BF16), pltpu.SemaphoreType.DMA((2,))],
-        compiler_params=params(12),
+        scratch_shapes=[pltpu.VMEM((slots, 3, count, WIDE), BF16), pltpu.SemaphoreType.DMA((slots, 3))],
+        compiler_params=params(16),
         cost_estimate=cost(),
         name="all_weights",
     )(mark, data[:8], data[8:32])
@@ -529,6 +534,9 @@
     )(mark, data[:8], data[8:32])
 
 
+SLOTS = 4
+
+
 def multiply_kernel(first, mark_ref, values_ref, weights_ref, *refs):
     del mark_ref
     acc_ref, out_ref, held, sems = refs if len(refs) == 4 else (None,) + refs
@@ -536,30 +544,31 @@
     values = values_ref[...].reshape(comps * rows, nodes)
     blocks = weights_ref.shape[0]
 
-    def copy(block, slot):
+    def copy(block, slot, d):
         return pltpu.make_async_copy(
-            weights_ref.at[block, :, pl.ds(first, nodes), :], held.at[slot], sems.at[slot]
+            weights_ref.at[block, d, pl.ds(first, nodes), :], held.at[slot, d], sems.at[slot, d]
         )
 
-    for slot in range(2):
-        copy(slot, slot).start()
-
-    def pair(twice, carry):
-        for slot in range(2):
-            block = twice * 2 + slot
-            copy(block, slot).wait()
+    for slot in range(SLOTS):
+        for d in range(3):
+            copy(slot, slot, d).start()
+
+    def turn(step, carry):
+        for slot in range(SLOTS):
+            block = step * SLOTS + slot
             cut = pl.ds(pl.multiple_of(block * WIDE, WIDE), WIDE)
             for d in range(3):
+                copy(block, slot, d).wait()
                 term = jnp.dot(values, held[slot, d], preferred_element_type=F32)
                 out_ref[d, :, cut] = term if acc_ref is None else term + acc_ref[d, :, cut]
 
-            @pl.when(twice < blocks // 2 - 1)
-            def _():
-                copy(block + 2, slot).start()
+                @pl.when(step < blocks // SLOTS - 1)
+                def _():
+                    copy(block + SLOTS, slot, d).start()
 
         return carry
 
-    lax.fori_loop(0, blocks // 2, pair, 0)
+    lax.fori_loop(0, blocks // SLOTS, turn, 0)
 
 
 def multiply(mark, values, weights, first, acc):
@@ -572,8 +581,8 @@
         in_specs=[ANY, VMEM, ANY] + [VMEM] * (len(args) - 3),
         out_specs=VMEM,
         input_output_aliases={} if acc is None else {3: 0},
-        scratch_shapes=[pltpu.VMEM((2, 3, nodes, WIDE), BF16), pltpu.SemaphoreType.DMA((2,))],
-        compiler_params=params(20),
+        scratch_shapes=[pltpu.VMEM((SLOTS, 3, nodes, WIDE), BF16), pltpu.SemaphoreType.DMA((SLOTS, 3))],
+        compiler_params=params(24),
         cost_estimate=cost(),
         name="multiply",
     )(*args)

time: 189 us -> 193 us (1.021)
  Pallas kernels: 102 us -> 106 us
    pallas_call x3, Pallas kernels: 33.4 us -> 45.5 us  [multiply(): pl.pallas_call(functools.partial(multiply_kernel, first), out_shape=shape...]
    pallas_call x1, Pallas kernels: 30.8 us -> 23.6 us  [all_weights(): pl.pallas_call(all_weights_kernel, out_shape=shaped((elems // WIDE, 3, no...]
    ppermute x4, waiting for transfers between devices: 20.4 us -> 17.2 us  [local(): up = lambda v: lax.ppermute(v, 'mode', up_perm)]
    ppermute x4, waiting for transfers between devices: 2.64 us -> 5.09 us  [local(): side = lambda v: lax.ppermute(v, 'mode', side_perm)]
  transfers between devices with their start and end apart: 26 -> 26, of which waited for: 11 -> 12; matrix products, arithmetic and copies ran while one was open for 0% -> 0% of each run, Pallas kernels for 41% -> 43%
where the time goes in v5:
time: 193 us; the launch traced here: 192 us
  Pallas kernels  106 us (55%)
  starting transfers between devices  42 us (22%)
  waiting for transfers between devices  40.9 us (21%)
    pallas_call x3, Pallas kernels, multiply(): pl.pallas_call(functools.partial(multiply_kernel, first), out_shape=shape...  45.5 us
    pallas_call x1, Pallas kernels, all_weights(): pl.pallas_call(all_weights_kernel, out_shape=shaped((elems // WIDE, 3, no...  23.6 us
    ppermute x4, waiting for transfers between devices, local(): up = lambda v: lax.ppermute(v, 'mode', up_perm)  17.2 us
    ppermute x3, waiting for transfers between devices, local(): lax.ppermute(pair, 'mesh', mesh_perm(dy))  11.2 us
    pallas_call x1, Pallas kernels, partial_loads(): pl.pallas_call(functools.partial(loads_kernel, cuts), out_shape=(shaped((...  11.1 us
    ppermute x4, starting transfers between devices, local(): down = lambda v: lax.ppermute(v, 'mode', down_perm)  9.14 us
    pallas_call x1, Pallas kernels, element_spectra(): pl.pallas_call(spectra_kernel, out_shape=shaped((Z, 36, elems // Z), F32)...  6.1 us
    ppermute x3, starting transfers between devices, local(): lax.ppermute(data, 'mode', mode_perm(-j))  5.74 us
  transfers between devices with their start and end apart: 26, of which 12 were waited for; matrix products, arithmetic and copies ran while one was open for 0% of the time, Pallas kernels for 43%

profile of v5, /device:TPU:1, one launch (start us, length us, event | category | flops | bytes accessed | tf_op | source)
XLA Modules:
  0.0 192.4 jit_solution(13235455753016284664)
XLA Ops:
  0.0 11.1 %modal_loads.1 = (f32[256,384]{1,0:T(8,128)}, bf16[256,384]{1,0:T(8,128)(2,1)}) custom-call(s32[1]{0:T(128)} %bitcast.1.core_ref, bf16[3,500,4096]{2,1,0:T(8,128)(2,1)} %bitcast.19, bf16[3,4096,384]{2,1,0:T(8,128)(2,1)} %load_ref.1), custom_call_target="tpu_custom_call" | custom-call | flops 1 | bytes 1 | tf_op jit(solution)/shard_map/modal_loads/pallas_call | solution.py:88
  15.0 2.9 %collective-permute-start.4 = (bf16[256,384]{1,0:T(8,128)(2,1)S(1)}, bf16[256,384]{1,0:T(8,128)(2,1)S(1)}, u32[]{:S(2)}, u32[]{:S(2)}) collective-permute-start(bf16[256,384]{1,0:T(8,128)(2,1)S(1)} %add_convert_fusion.1.mark_ref), channel_id=1, source_target_pairs={{0,16},{8,24},{16,0},{24,8},{32,48},{40,56},{48,32},{56,40},{64,80... | collective-permute-start | bytes 589832 | tf_op jit(solution)/shard_map/ppermute | solution.py:729
  19.9 3.3 %collective-permute-start.2 = (f32[40,512]{1,0:T(8,128)S(1)}, f32[40,512]{1,0:T(8,128)S(1)}, u32[]{:S(2)}, u32[]{:S(2)}) collective-permute-start(f32[40,512]{1,0:T(8,128)S(1)} %element_data.1), channel_id=1, source_target_pairs={{0,4},{1,5},{2,6},{3,7},{4,0},{5,1},{6,2},{7,3},{8,12},{9,13},{10,... | collective-permute-start | bytes 245768 | tf_op jit(solution)/shard_map/ppermute | solution.py:735
  24.0 2.8 %collective-permute-start.7 = (bf16[256,384]{1,0:T(8,128)(2,1)S(1)}, bf16[256,384]{1,0:T(8,128)(2,1)S(1)}, u32[]{:S(2)}, u32[]{:S(2)}) collective-permute-start(bf16[256,384]{1,0:T(8,128)(2,1)S(1)} %add_convert_fusion.a_ref), channel_id=1, source_target_pairs={{0,96},{8,104},{16,112},{24,120},{32,0},{40,8},{48,16},{56,24},{64... | collective-permute-start | bytes 589832 | tf_op jit(solution)/shard_map/ppermute | solution.py:731
  27.9 3.8 %collective-permute-done.7.d_ref = bf16[256,384]{1,0:T(8,128)(2,1)S(1)} collective-permute-done((bf16[256,384]{1,0:T(8,128)(2,1)S(1)}, bf16[256,384]{1,0:T(8,128)(2,1)S(1)}, u32[]{:S(2)}, u32[]{:S(2)}) %collective-permute-start.7) | collective-permute-done | bytes 196640 | tf_op jit(solution)/shard_map/ppermute | solution.py:731
  32.9 6.2 %collective-permute-done.5.b_ref = bf16[256,384]{1,0:T(8,128)(2,1)S(1)} collective-permute-done((bf16[256,384]{1,0:T(8,128)(2,1)S(1)}, bf16[256,384]{1,0:T(8,128)(2,1)S(1)}, u32[]{:S(2)}, u32[]{:S(2)}) %collective-permute-start.5) | collective-permute-done | bytes 196640 | tf_op jit(solution)/shard_map/ppermute | solution.py:731
  41.3 5.2 %x_first_terms.1 = (bf16[4,3,48,1792]{3,2,1,0:T(8,128)(2,1)S(1)}, bf16[4,3,48,1792]{3,2,1,0:T(8,128)(2,1)S(1)}, bf16[384,500]{1,0:T(8,128)(2,1)S(1)}) custom-call(s32[1]{0:T(128)} %bitcast.1.core_ref, bf16[256,384]{1,0:T(8,128)(2,1)S(1)} %modal_response.1.mine_ref, bf16[256,384]{1,0:T(8,128)(2,1)S(1)} %collective-permute-done.8.theirs_ref, ...), custom_call_target="tpu_custom_call" | custom-call | flops 1 | bytes 1 | tf_op jit(solution)/shard_map/x_first_terms/pallas_call | solution.py:266
  46.9 5.1 %z_first_terms.1 = (bf16[2,3,96,1152]{3,2,1,0:T(8,128)(2,1)S(1)}, bf16[2,3,96,1152]{3,2,1,0:T(8,128)(2,1)S(1)}, bf16[3,96,1152]{2,1,0:T(8,128)(2,1)S(1)}, bf16[3...) custom-call(bf16[4,3,48,1792]{3,2,1,0:T(8,128)(2,1)S(1)} %get-tuple-element.32.mark_ref.keep_ref, ...), custom_call_target="tpu_custom_call" | custom-call | flops 1 | bytes 1 | tf_op jit(solution)/shard_map/z_first_terms/pallas_call | solution.py:223
  53.6 2.4 %collective-permute-start.10 = (bf16[2,3,96,1152]{3,2,1,0:T(8,128)(2,1)S(1)}, bf16[2,3,96,1152]{3,2,1,0:T(8,128)(2,1)S(1)}, u32[]{:S(2)}, u32[]{:S(2)}) collective-permute-start(bf16[2,3,96,1152]{3,2,1,0:T(8,128)(2,1)S(1)} %get-tuple-element.37), channel_id=1, source_target_pairs={{0,6},{1,7},{2,0},{3,1},{4,2},{5,3},{6,4},{7,5},{8,14},{9,15},{10,... | collective-permute-start | bytes 3981320 | tf_op jit(solution)/shard_map/ppermute | solution.py:739
  56.0 23.6 %all_weights.1.mark_ref.weights_ref = bf16[8,3,4096,256]{3,2,1,0:T(8,128)(2,1)} custom-call(bf16[3,96,1152]{2,1,0:T(8,128)(2,1)S(1)} %get-tuple-element.34.mark_ref.up_ref, f32[8,2048]{1,0:T(8,128)S(1)} %get-tuple-element.60.conn_ref, f32[24,2048]{1,0:T(8,128)S(1)} %slice.39.grads_ref), custom_call_target="tpu_custom_call" | custom-call | flops 1 | bytes 1 | tf_op jit(solution)/shard_map/all_weights/pallas_call | solution.py:512
  79.5 2.9 %element_weights.1.mark_ref.weights_ref = bf16[3,512,2048]{2,1,0:T(8,128)(2,1)S(1)} custom-call(bf16[8,3,4096,256]{3,2,1,0:T(8,128)(2,1)} %all_weights.1.mark_ref.weights_ref, f32[8,2048]{1,0:T(8,128)S(1)} %get-tuple-element.60.conn_ref, f32[24,2048]{1,0:T(8,128)S(1)} %slice.39.grads_ref), custom_call_target="tpu_custom_call" | custom-call | flops 1 | bytes 1 | tf_op jit(solution)/shard_map/element_weights/pallas_call | solution.py:526
  82.4 2.1 %collective-permute-done.9.plus_ref.direct_ref = bf16[2,3,96,1152]{3,2,1,0:T(8,128)(2,1)S(1)} collective-permute-done((bf16[2,3,96,1152]{3,2,1,0:T(8,128)(2,1)S(1)}, bf16[2,3,96,1152]{3,2,1,0:T(8,128)(2,1)S(1)}, u32[]{:S(2)}, u32[]{:S(2)}) %collective-permute-start.9) | collective-permute-done | bytes 1327136 | tf_op jit(solution)/shard_map/ppermute | solution.py:738
  85.3 2.4 %collective-permute-start.13 = (bf16[3,96,1152]{2,1,0:T(8,128)(2,1)S(1)}, bf16[3,96,1152]{2,1,0:T(8,128)(2,1)S(1)}, u32[]{:S(2)}, u32[]{:S(2)}) collective-permute-start(bf16[3,96,1152]{2,1,0:T(8,128)(2,1)S(1)} %get-tuple-element.42), channel_id=1, source_target_pairs={{0,6},{1,7},{2,0},{3,1},{4,2},{5,3},{6,4},{7,5},{8,14},{9,15},{10,... | collective-permute-start | bytes 1990664 | tf_op jit(solution)/shard_map/ppermute | solution.py:739
  87.7 5.1 %collective-permute-done.11.got_ref = bf16[4,3,48,1792]{3,2,1,0:T(8,128)(2,1)S(1)} collective-permute-done((bf16[4,3,48,1792]{3,2,1,0:T(8,128)(2,1)S(1)}, bf16[4,3,48,1792]{3,2,1,0:T(8,128)(2,1)S(1)}, u32[]{:S(2)}, u32[]{:S(2)}) %collective-permute-start.11) | collective-permute-done | bytes 2064416 | tf_op jit(solution)/shard_map/ppermute | solution.py:740
  96.4 5.0 %collective-permute-done.12.passed_ref = bf16[3,96,1152]{2,1,0:T(8,128)(2,1)S(1)} collective-permute-done((bf16[3,96,1152]{2,1,0:T(8,128)(2,1)S(1)}, bf16[3,96,1152]{2,1,0:T(8,128)(2,1)S(1)}, u32[]{:S(2)}, u32[]{:S(2)}) %collective-permute-start.12) | collective-permute-done | bytes 663584 | tf_op jit(solution)/shard_map/ppermute | solution.py:738
  102.3 10.1 %collective-permute-done.14.plus_ref = bf16[2,3,48,896]{3,2,1,0:T(8,128)(2,1)S(1)} collective-permute-done((bf16[2,3,48,896]{3,2,1,0:T(8,128)(2,1)S(1)}, bf16[2,3,48,896]{3,2,1,0:T(8,128)(2,1)S(1)}, u32[]{:S(2)}, u32[]{:S(2)}) %collective-permute-start.14) | collective-permute-done | bytes 516128 | tf_op jit(solution)/shard_map/ppermute | solution.py:738
  112.6 2.4 %collective-permute-start.18 = (bf16[3,48,896]{2,1,0:T(8,128)(2,1)S(1)}, bf16[3,48,896]{2,1,0:T(8,128)(2,1)S(1)}, u32[]{:S(2)}, u32[]{:S(2)}) collective-permute-start(bf16[3,48,896]{2,1,0:T(8,128)(2,1)S(1)} %get-tuple-element.50), channel_id=1, source_target_pairs={{0,6},{1,7},{2,0},{3,1},{4,2},{5,3},{6,4},{7,5},{8,14},{9,15},{10,... | collective-permute-start | bytes 774152 | tf_op jit(solution)/shard_map/ppermute | solution.py:739
  116.5 13.9 %multiply.3.mark_ref.refs_0_ = f32[3,288,2048]{2,1,0:T(8,128)S(1)} custom-call(bf16[3,96,512]{2,1,0:T(8,128)(2,1)S(1)} %get-tuple-element.47.mark_ref.refs_0_, bf16[3,96,1152]{2,1,0:T(8,128)(2,1)S(1)} %get-tuple-element.48.values_ref, bf16[8,3,4096,256]{3,2,1,0:T(8,128)(2,1)} %all_weights.1.mark_ref.weights_ref), custom_call_target="tpu_custom_call" | custom-call | flops 1 | bytes 1 | tf_op jit(solution)/shard_map/multiply/pallas_call | solution.py:578
  133.8 13.9 %multiply.4.mark_ref.refs_0_ = f32[3,288,2048]{2,1,0:T(8,128)S(1)} custom-call(bf16[3,96,512]{2,1,0:T(8,128)(2,1)S(1)} %get-tuple-element.51.mark_ref.refs_0_, bf16[3,96,1152]{2,1,0:T(8,128)(2,1)S(1)} %get-tuple-element.52.values_ref, bf16[8,3,4096,256]{3,2,1,0:T(8,128)(2,1)} %all_weights.1.mark_ref.weights_ref, ...), custom_call_target="tpu_custom_call", output_to_operand_aliasing={{}: (3, {})} | custom-call | flops 1 | bytes 1 | tf_op jit(solution)/shard_map/multiply/pallas_call | solution.py:578
  149.1 5.7 %collective-permute-start.22 = (bf16[3,96,256]{2,1,0:T(8,128)(2,1)S(1)}, bf16[3,96,256]{2,1,0:T(8,128)(2,1)S(1)}, u32[]{:S(2)}, u32[]{:S(2)}) collective-permute-start(bf16[3,96,256]{2,1,0:T(8,128)(2,1)S(1)} %get-tuple-element.61), channel_id=1, source_target_pairs={{8,0},{16,8},{24,16},{32,24},{40,32},{48,40},{56,48},{64,56},{72,6... | collective-permute-start | bytes 442376 | tf_op jit(solution)/shard_map/ppermute | solution.py:776
  154.8 4.8 %collective-permute-start.21 = (bf16[3,96,256]{2,1,0:T(8,128)(2,1)S(1)}, bf16[3,96,256]{2,1,0:T(8,128)(2,1)S(1)}, u32[]{:S(2)}, u32[]{:S(2)}) collective-permute-start(bf16[3,96,256]{2,1,0:T(8,128)(2,1)S(1)} %get-tuple-element.62), channel_id=1, source_target_pairs={{0,8},{8,16},{16,24},{24,32},{32,40},{40,48},{48,56},{56,64},{64,7... | collective-permute-start | bytes 442376 | tf_op jit(solution)/shard_map/ppermute | solution.py:775
  159.6 17.7 %multiply.5.acc_ref = f32[3,288,2048]{2,1,0:T(8,128)S(1)} custom-call(bf16[3,96,512]{2,1,0:T(8,128)(2,1)S(1)} %get-tuple-element.53.mark_ref, bf16[3,96,1792]{2,1,0:T(8,128)(2,1)S(1)} %get-tuple-element.54.values_ref, bf16[8,3,4096,256]{3,2,1,0:T(8,128)(2,1)} %all_weights.1.mark_ref.weights_ref, ...), custom_call_target="tpu_custom_call", output_to_operand_aliasing={{}: (3, {})} | custom-call | flops 1 | bytes 1 | tf_op jit(solution)/shard_map/multiply/pallas_call | solution.py:578
  177.3 6.1 %element_spectra.1 = f32[4,36,512]{2,1,0:T(8,128)S(1)} custom-call(bf16[3,96,256]{2,1,0:T(8,128)(2,1)S(1)} %collective-permute-done.21.before_ref, bf16[3,96,256]{2,1,0:T(8,128)(2,1)S(1)} %collective-permute-done.22.after_ref, bf16[3,512,2048]{2,1,0:T(8,128)(2,1)S(1)} %element_weights.1.mark_ref.weights_ref, f32[3,288,2048]{2,1,0:T(8,128)S(1)} %multiply.5.acc_ref, ...), custom_call_target="tpu_custom_call" | custom-call | flops 1 | bytes 1 | tf_op jit(solution)/shard_map/element_spectra/pallas_call | solution.py:655
  188.0 2.8 %collective-permute-done.24.c_ref = f32[36,512]{1,0:T(8,128)S(1)} collective-permute-done((f32[36,512]{1,0:T(8,128)S(1)}, f32[36,512]{1,0:T(8,128)S(1)}, u32[]{:S(2)}, u32[]{:S(2)}) %collective-permute-start.24) | collective-permute-done | bytes 73760 | tf_op jit(solution)/shard_map/ppermute | solution.py:779
  (80 shorter events, 30.7 us)
Async XLA Ops:
  15.0 8.9 %collective-permute-start.4 = (bf16[256,384]{1,0:T(8,128)(2,1)S(1)}, bf16[256,384]{1,0:T(8,128)(2,1)S(1)}, u32[]{:S(2)}, u32[]{:S(2)}) collective-permute-start(bf16[256,384]{1,0:T(8,128)(2,1)S(1)} %add_convert_fusion.1.mark_ref), channel_id=1, source_target_pairs={{0,16},{8,24},{16,0},{24,8},{32,48},{40,56},{48,32},{56,40},{64,80... | collective-permute-start | bytes 589832 | tf_op jit(solution)/shard_map/ppermute | solution.py:729
  18.2 9.0 %collective-permute-start.3 = (f32[40,512]{1,0:T(8,128)S(1)}, f32[40,512]{1,0:T(8,128)S(1)}, u32[]{:S(2)}, u32[]{:S(2)}) collective-permute-start(f32[40,512]{1,0:T(8,128)S(1)} %element_data.1), channel_id=1, source_target_pairs={{0,2},{1,3},{2,4},{3,5},{4,6},{5,7},{6,0},{7,1},{8,10},{9,11},{10,... | collective-permute-start | bytes 245768 | tf_op jit(solution)/shard_map/ppermute | solution.py:735
  19.9 7.9 %collective-permute-start.2 = (f32[40,512]{1,0:T(8,128)S(1)}, f32[40,512]{1,0:T(8,128)S(1)}, u32[]{:S(2)}, u32[]{:S(2)}) collective-permute-start(f32[40,512]{1,0:T(8,128)S(1)} %element_data.1), channel_id=1, source_target_pairs={{0,4},{1,5},{2,6},{3,7},{4,0},{5,1},{6,2},{7,3},{8,12},{9,13},{10,... | collective-permute-start | bytes 245768 | tf_op jit(solution)/shard_map/ppermute | solution.py:735
  23.2 4.6 %collective-permute-start.1 = (f32[40,512]{1,0:T(8,128)S(1)}, f32[40,512]{1,0:T(8,128)S(1)}, u32[]{:S(2)}, u32[]{:S(2)}) collective-permute-start(f32[40,512]{1,0:T(8,128)S(1)} %element_data.1), channel_id=1, source_target_pairs={{0,6},{1,7},{2,0},{3,1},{4,2},{5,3},{6,4},{7,5},{8,14},{9,15},{10,... | collective-permute-start | bytes 245768 | tf_op jit(solution)/shard_map/ppermute | solution.py:735
  24.0 7.6 %collective-permute-start.7 = (bf16[256,384]{1,0:T(8,128)(2,1)S(1)}, bf16[256,384]{1,0:T(8,128)(2,1)S(1)}, u32[]{:S(2)}, u32[]{:S(2)}) collective-permute-start(bf16[256,384]{1,0:T(8,128)(2,1)S(1)} %add_convert_fusion.a_ref), channel_id=1, source_target_pairs={{0,96},{8,104},{16,112},{24,120},{32,0},{40,8},{48,16},{56,24},{64... | collective-permute-start | bytes 589832 | tf_op jit(solution)/shard_map/ppermute | solution.py:731
  26.8 6.1 %collective-permute-start.6 = (bf16[256,384]{1,0:T(8,128)(2,1)S(1)}, bf16[256,384]{1,0:T(8,128)(2,1)S(1)}, u32[]{:S(2)}, u32[]{:S(2)}) collective-permute-start(bf16[256,384]{1,0:T(8,128)(2,1)S(1)} %add_convert_fusion.a_ref), channel_id=1, source_target_pairs={{0,64},{8,72},{16,80},{24,88},{32,96},{40,104},{48,112},{56,120},{... | collective-permute-start | bytes 589832 | tf_op jit(solution)/shard_map/ppermute | solution.py:731
  27.2 11.9 %collective-permute-start.5 = (bf16[256,384]{1,0:T(8,128)(2,1)S(1)}, bf16[256,384]{1,0:T(8,128)(2,1)S(1)}, u32[]{:S(2)}, u32[]{:S(2)}) collective-permute-start(bf16[256,384]{1,0:T(8,128)(2,1)S(1)} %add_convert_fusion.a_ref), channel_id=1, source_target_pairs={{0,32},{8,40},{16,48},{24,56},{32,64},{40,72},{48,80},{56,88},{64,... | collective-permute-start | bytes 589832 | tf_op jit(solution)/shard_map/ppermute | solution.py:731
  46.5 46.2 %collective-permute-start.11 = (bf16[4,3,48,1792]{3,2,1,0:T(8,128)(2,1)S(1)}, bf16[4,3,48,1792]{3,2,1,0:T(8,128)(2,1)S(1)}, u32[]{:S(2)}, u32[]{:S(2)}) collective-permute-start(bf16[4,3,48,1792]{3,2,1,0:T(8,128)(2,1)S(1)} %get-tuple-element.39), channel_id=1, source_target_pairs={{0,1},{1,0},{2,3},{3,2},{4,5},{5,4},{6,7},{7,6},{8,9},{9,8},{10,11... | collective-permute-start | bytes 6193160 | tf_op jit(solution)/shard_map/ppermute | solution.py:740
  52.1 32.5 %collective-permute-start.9 = (bf16[2,3,96,1152]{3,2,1,0:T(8,128)(2,1)S(1)}, bf16[2,3,96,1152]{3,2,1,0:T(8,128)(2,1)S(1)}, u32[]{:S(2)}, u32[]{:S(2)}) collective-permute-start(bf16[2,3,96,1152]{3,2,1,0:T(8,128)(2,1)S(1)} %get-tuple-element.36), channel_id=1, source_target_pairs={{0,2},{1,3},{2,4},{3,5},{4,6},{5,7},{6,0},{7,1},{8,10},{9,11},{10,... | collective-permute-start | bytes 3981320 | tf_op jit(solution)/shard_map/ppermute | solution.py:738
  53.6 31.0 %collective-permute-start.10 = (bf16[2,3,96,1152]{3,2,1,0:T(8,128)(2,1)S(1)}, bf16[2,3,96,1152]{3,2,1,0:T(8,128)(2,1)S(1)}, u32[]{:S(2)}, u32[]{:S(2)}) collective-permute-start(bf16[2,3,96,1152]{3,2,1,0:T(8,128)(2,1)S(1)} %get-tuple-element.37), channel_id=1, source_target_pairs={{0,6},{1,7},{2,0},{3,1},{4,2},{5,3},{6,4},{7,5},{8,14},{9,15},{10,... | collective-permute-start | bytes 3981320 | tf_op jit(solution)/shard_map/ppermute | solution.py:739
  84.9 16.5 %collective-permute-start.12 = (bf16[3,96,1152]{2,1,0:T(8,128)(2,1)S(1)}, bf16[3,96,1152]{2,1,0:T(8,128)(2,1)S(1)}, u32[]{:S(2)}, u32[]{:S(2)}) collective-permute-start(bf16[3,96,1152]{2,1,0:T(8,128)(2,1)S(1)} %get-tuple-element.38.mark_ref), channel_id=1, source_target_pairs={{0,2},{1,3},{2,4},{3,5},{4,6},{5,7},{6,0},{7,1},{8,10},{9,11},{10,... | collective-permute-start | bytes 1990664 | tf_op jit(solution)/shard_map/ppermute | solution.py:738
  85.3 16.6 %collective-permute-start.13 = (bf16[3,96,1152]{2,1,0:T(8,128)(2,1)S(1)}, bf16[3,96,1152]{2,1,0:T(8,128)(2,1)S(1)}, u32[]{:S(2)}, u32[]{:S(2)}) collective-permute-start(bf16[3,96,1152]{2,1,0:T(8,128)(2,1)S(1)} %get-tuple-element.42), channel_id=1, source_target_pairs={{0,6},{1,7},{2,0},{3,1},{4,2},{5,3},{6,4},{7,5},{8,14},{9,15},{10,... | collective-permute-start | bytes 1990664 | tf_op jit(solution)/shard_map/ppermute | solution.py:739
  93.7 18.8 %collective-permute-start.14 = (bf16[2,3,48,896]{3,2,1,0:T(8,128)(2,1)S(1)}, bf16[2,3,48,896]{3,2,1,0:T(8,128)(2,1)S(1)}, u32[]{:S(2)}, u32[]{:S(2)}) collective-permute-start(bf16[2,3,48,896]{3,2,1,0:T(8,128)(2,1)S(1)} %get-tuple-element.44), channel_id=1, source_target_pairs={{0,2},{1,3},{2,4},{3,5},{4,6},{5,7},{6,0},{7,1},{8,10},{9,11},{10,... | collective-permute-start | bytes 1548296 | tf_op jit(solution)/shard_map/ppermute | solution.py:738
  94.5 18.0 %collective-permute-start.15 = (bf16[2,3,48,896]{3,2,1,0:T(8,128)(2,1)S(1)}, bf16[2,3,48,896]{3,2,1,0:T(8,128)(2,1)S(1)}, u32[]{:S(2)}, u32[]{:S(2)}) collective-permute-start(bf16[2,3,48,896]{3,2,1,0:T(8,128)(2,1)S(1)} %get-tuple-element.45), channel_id=1, source_target_pairs={{0,6},{1,7},{2,0},{3,1},{4,2},{5,3},{6,4},{7,5},{8,14},{9,15},{10,... | collective-permute-start | bytes 1548296 | tf_op jit(solution)/shard_map/ppermute | solution.py:739
  101.8 13.3 %collective-permute-start.16 = (bf16[3,96,1152]{2,1,0:T(8,128)(2,1)S(1)}, bf16[3,96,1152]{2,1,0:T(8,128)(2,1)S(1)}, u32[]{:S(2)}, u32[]{:S(2)}) collective-permute-start(bf16[3,96,1152]{2,1,0:T(8,128)(2,1)S(1)} %half_sum.2.mark_ref.after_ref.own_ref), channel_id=1, source_target_pairs={{0,1},{1,0},{2,3},{3,2},{4,5},{5,4},{6,7},{7,6},{8,9},{9,8},{10,11... | collective-permute-start | bytes 1990664 | tf_op jit(solution)/shard_map/ppermute | solution.py:740
  112.6 17.7 %collective-permute-start.18 = (bf16[3,48,896]{2,1,0:T(8,128)(2,1)S(1)}, bf16[3,48,896]{2,1,0:T(8,128)(2,1)S(1)}, u32[]{:S(2)}, u32[]{:S(2)}) collective-permute-start(bf16[3,48,896]{2,1,0:T(8,128)(2,1)S(1)} %get-tuple-element.50), channel_id=1, source_target_pairs={{0,6},{1,7},{2,0},{3,1},{4,2},{5,3},{6,4},{7,5},{8,14},{9,15},{10,... | collective-permute-start | bytes 774152 | tf_op jit(solution)/shard_map/ppermute | solution.py:739
  115.1 15.3 %collective-permute-start.17 = (bf16[3,48,896]{2,1,0:T(8,128)(2,1)S(1)}, bf16[3,48,896]{2,1,0:T(8,128)(2,1)S(1)}, u32[]{:S(2)}, u32[]{:S(2)}) collective-permute-start(bf16[3,48,896]{2,1,0:T(8,128)(2,1)S(1)} %get-tuple-element.46.mark_ref), channel_id=1, source_target_pairs={{0,2},{1,3},{2,4},{3,5},{4,6},{5,7},{6,0},{7,1},{8,10},{9,11},{10,... | collective-permute-start | bytes 774152 | tf_op jit(solution)/shard_map/ppermute | solution.py:738
  115.1 17.3 %collective-permute-start.19 = (bf16[3,96,1152]{2,1,0:T(8,128)(2,1)S(1)}, bf16[3,96,1152]{2,1,0:T(8,128)(2,1)S(1)}, u32[]{:S(2)}, u32[]{:S(2)}) collective-permute-start(bf16[3,96,1152]{2,1,0:T(8,128)(2,1)S(1)} %half_sum.3.mark_ref.own_ref), channel_id=1, source_target_pairs={{0,1},{1,0},{2,3},{3,2},{4,5},{5,4},{6,7},{7,6},{8,9},{9,8},{10,11... | collective-permute-start | bytes 1990664 | tf_op jit(solution)/shard_map/ppermute | solution.py:740
  130.7 17.0 %collective-permute-start.20 = (bf16[3,48,1792]{2,1,0:T(8,128)(2,1)S(1)}, bf16[3,48,1792]{2,1,0:T(8,128)(2,1)S(1)}, u32[]{:S(2)}, u32[]{:S(2)}) collective-permute-start(bf16[3,48,1792]{2,1,0:T(8,128)(2,1)S(1)} %ring_sum.1.mark_ref.own_ref), channel_id=1, source_target_pairs={{0,1},{1,0},{2,3},{3,2},{4,5},{5,4},{6,7},{7,6},{8,9},{9,8},{10,11... | collective-permute-start | bytes 1548296 | tf_op jit(solution)/shard_map/ppermute | solution.py:740
  149.1 28.2 %collective-permute-start.22 = (bf16[3,96,256]{2,1,0:T(8,128)(2,1)S(1)}, bf16[3,96,256]{2,1,0:T(8,128)(2,1)S(1)}, u32[]{:S(2)}, u32[]{:S(2)}) collective-permute-start(bf16[3,96,256]{2,1,0:T(8,128)(2,1)S(1)} %get-tuple-element.61), channel_id=1, source_target_pairs={{8,0},{16,8},{24,16},{32,24},{40,32},{48,40},{56,48},{64,56},{72,6... | collective-permute-start | bytes 442376 | tf_op jit(solution)/shard_map/ppermute | solution.py:776
  154.8 22.5 %collective-permute-start.21 = (bf16[3,96,256]{2,1,0:T(8,128)(2,1)S(1)}, bf16[3,96,256]{2,1,0:T(8,128)(2,1)S(1)}, u32[]{:S(2)}, u32[]{:S(2)}) collective-permute-start(bf16[3,96,256]{2,1,0:T(8,128)(2,1)S(1)} %get-tuple-element.62), channel_id=1, source_target_pairs={{0,8},{8,16},{16,24},{24,32},{32,40},{40,48},{48,56},{56,64},{64,7... | collective-permute-start | bytes 442376 | tf_op jit(solution)/shard_map/ppermute | solution.py:775
  183.5 4.6 %collective-permute-start.25 = (f32[36,512]{1,0:T(8,128)S(1)}, f32[36,512]{1,0:T(8,128)S(1)}, u32[]{:S(2)}, u32[]{:S(2)}) collective-permute-start(f32[36,512]{1,0:T(8,128)S(1)} %get-tuple-element.55), channel_id=1, source_target_pairs={{0,6},{1,7},{2,0},{3,1},{4,2},{5,3},{6,4},{7,5},{8,14},{9,15},{10,... | collective-permute-start | bytes 221192 | tf_op jit(solution)/shard_map/ppermute | solution.py:779
  185.4 5.5 %collective-permute-start.24 = (f32[36,512]{1,0:T(8,128)S(1)}, f32[36,512]{1,0:T(8,128)S(1)}, u32[]{:S(2)}, u32[]{:S(2)}) collective-permute-start(f32[36,512]{1,0:T(8,128)S(1)} %get-tuple-element.56), channel_id=1, source_target_pairs={{0,4},{1,5},{2,6},{3,7},{4,0},{5,1},{6,2},{7,3},{8,12},{9,13},{10,... | collective-permute-start | bytes 221192 | tf_op jit(solution)/shard_map/ppermute | solution.py:779
  185.4 6.0 %collective-permute-start.23 = (f32[36,512]{1,0:T(8,128)S(1)}, f32[36,512]{1,0:T(8,128)S(1)}, u32[]{:S(2)}, u32[]{:S(2)}) collective-permute-start(f32[36,512]{1,0:T(8,128)S(1)} %get-tuple-element.57), channel_id=1, source_target_pairs={{0,2},{1,3},{2,4},{3,5},{4,6},{5,7},{6,0},{7,1},{8,10},{9,11},{10,... | collective-permute-start | bytes 221192 | tf_op jit(solution)/shard_map/ppermute | solution.py:779
  (9 other events, 110.2 us)

commit v6 on v5

--- a/solution.py
+++ b/solution.py
@@ -553,22 +553,22 @@
         for d in range(3):
             copy(slot, slot, d).start()
 
-    def turn(step, carry):
-        for slot in range(SLOTS):
-            block = step * SLOTS + slot
-            cut = pl.ds(pl.multiple_of(block * WIDE, WIDE), WIDE)
+    def turn(block, carry):
+        slot = block % SLOTS
+        cut = pl.ds(pl.multiple_of(block * WIDE, WIDE), WIDE)
+        for d in range(3):
+            copy(block, slot, d).wait()
+            term = jnp.dot(values, held[slot, d], preferred_element_type=F32)
+            out_ref[d, :, cut] = term if acc_ref is None else term + acc_ref[d, :, cut]
+
+        @pl.when(block < blocks - SLOTS)
+        def _():
             for d in range(3):
-                copy(block, slot, d).wait()
-                term = jnp.dot(values, held[slot, d], preferred_element_type=F32)
-                out_ref[d, :, cut] = term if acc_ref is None else term + acc_ref[d, :, cut]
-
-                @pl.when(step < blocks // SLOTS - 1)
-                def _():
-                    copy(block + SLOTS, slot, d).start()
+                copy(block + SLOTS, slot, d).start()
 
         return carry
 
-    lax.fori_loop(0, blocks // SLOTS, turn, 0)
+    lax.fori_loop(0, blocks, turn, 0)
 
 
 def multiply(mark, values, weights, first, acc):

time: 193 us -> 188 us (0.974)
  Pallas kernels: 106 us -> 102 us
    pallas_call x3, Pallas kernels: 45.5 us -> 41.1 us  [multiply(): pl.pallas_call(functools.partial(multiply_kernel, first), out_shape=shape...]
  transfers between devices with their start and end apart: 26 -> 26, of which waited for: 12 -> 12; matrix products, arithmetic and copies ran while one was open for 0% -> 0% of each run, Pallas kernels for 43% -> 42%
where the time goes in v6:
time: 188 us
  Pallas kernels  102 us (54%)
  starting transfers between devices  41.8 us (22%)
  waiting for transfers between devices  40.9 us (22%)
    pallas_call x3, Pallas kernels, multiply(): pl.pallas_call(functools.partial(multiply_kernel, first), out_shape=shape...  41.1 us
    pallas_call x1, Pallas kernels, all_weights(): pl.pallas_call(all_weights_kernel, out_shape=shaped((elems // WIDE, 3, no...  23.6 us
    ppermute x4, waiting for transfers between devices, local(): up = lambda v: lax.ppermute(v, 'mode', up_perm)  17.2 us
    ppermute x3, waiting for transfers between devices, local(): lax.ppermute(pair, 'mesh', mesh_perm(dy))  11.2 us
    pallas_call x1, Pallas kernels, partial_loads(): pl.pallas_call(functools.partial(loads_kernel, cuts), out_shape=(shaped((...  11.1 us
    ppermute x4, starting transfers between devices, local(): down = lambda v: lax.ppermute(v, 'mode', down_perm)  9.14 us
    pallas_call x1, Pallas kernels, element_spectra(): pl.pallas_call(spectra_kernel, out_shape=shaped((Z, 36, elems // Z), F32)...  6.09 us
    ppermute x3, starting transfers between devices, local(): lax.ppermute(data, 'mode', mode_perm(-j))  5.74 us
  transfers between devices with their start and end apart: 26, of which 12 were waited for; matrix products, arithmetic and copies ran while one was open for 0% of the time, Pallas kernels for 42%

profile of v6, /device:TPU:1, one launch (start us, length us, event | category | flops | bytes accessed | tf_op | source)
XLA Modules:
  0.0 187.8 jit_solution(6570775710330760148)
XLA Ops:
  0.0 11.1 %modal_loads.1 = (f32[256,384]{1,0:T(8,128)}, bf16[256,384]{1,0:T(8,128)(2,1)}) custom-call(s32[1]{0:T(128)} %bitcast.1.core_ref, bf16[3,500,4096]{2,1,0:T(8,128)(2,1)} %bitcast.19, bf16[3,4096,384]{2,1,0:T(8,128)(2,1)} %load_ref.1), custom_call_target="tpu_custom_call" | custom-call | flops 1 | bytes 1 | tf_op jit(solution)/shard_map/modal_loads/pallas_call | solution.py:88
  15.0 2.9 %collective-permute-start.4 = (bf16[256,384]{1,0:T(8,128)(2,1)S(1)}, bf16[256,384]{1,0:T(8,128)(2,1)S(1)}, u32[]{:S(2)}, u32[]{:S(2)}) collective-permute-start(bf16[256,384]{1,0:T(8,128)(2,1)S(1)} %add_convert_fusion.1.mark_ref), channel_id=1, source_target_pairs={{0,16},{8,24},{16,0},{24,8},{32,48},{40,56},{48,32},{56,40},{64,80... | collective-permute-start | bytes 589832 | tf_op jit(solution)/shard_map/ppermute | solution.py:729
  19.9 3.3 %collective-permute-start.2 = (f32[40,512]{1,0:T(8,128)S(1)}, f32[40,512]{1,0:T(8,128)S(1)}, u32[]{:S(2)}, u32[]{:S(2)}) collective-permute-start(f32[40,512]{1,0:T(8,128)S(1)} %element_data.1), channel_id=1, source_target_pairs={{0,4},{1,5},{2,6},{3,7},{4,0},{5,1},{6,2},{7,3},{8,12},{9,13},{10,... | collective-permute-start | bytes 245768 | tf_op jit(solution)/shard_map/ppermute | solution.py:735
  24.0 2.8 %collective-permute-start.7 = (bf16[256,384]{1,0:T(8,128)(2,1)S(1)}, bf16[256,384]{1,0:T(8,128)(2,1)S(1)}, u32[]{:S(2)}, u32[]{:S(2)}) collective-permute-start(bf16[256,384]{1,0:T(8,128)(2,1)S(1)} %add_convert_fusion.a_ref), channel_id=1, source_target_pairs={{0,96},{8,104},{16,112},{24,120},{32,0},{40,8},{48,16},{56,24},{64... | collective-permute-start | bytes 589832 | tf_op jit(solution)/shard_map/ppermute | solution.py:731
  27.9 3.8 %collective-permute-done.7.d_ref = bf16[256,384]{1,0:T(8,128)(2,1)S(1)} collective-permute-done((bf16[256,384]{1,0:T(8,128)(2,1)S(1)}, bf16[256,384]{1,0:T(8,128)(2,1)S(1)}, u32[]{:S(2)}, u32[]{:S(2)}) %collective-permute-start.7) | collective-permute-done | bytes 196640 | tf_op jit(solution)/shard_map/ppermute | solution.py:731
  32.9 6.2 %collective-permute-done.5.b_ref = bf16[256,384]{1,0:T(8,128)(2,1)S(1)} collective-permute-done((bf16[256,384]{1,0:T(8,128)(2,1)S(1)}, bf16[256,384]{1,0:T(8,128)(2,1)S(1)}, u32[]{:S(2)}, u32[]{:S(2)}) %collective-permute-start.5) | collective-permute-done | bytes 196640 | tf_op jit(solution)/shard_map/ppermute | solution.py:731
  41.3 5.2 %x_first_terms.1 = (bf16[4,3,48,1792]{3,2,1,0:T(8,128)(2,1)S(1)}, bf16[4,3,48,1792]{3,2,1,0:T(8,128)(2,1)S(1)}, bf16[384,500]{1,0:T(8,128)(2,1)S(1)}) custom-call(s32[1]{0:T(128)} %bitcast.1.core_ref, bf16[256,384]{1,0:T(8,128)(2,1)S(1)} %modal_response.1.mine_ref, bf16[256,384]{1,0:T(8,128)(2,1)S(1)} %collective-permute-done.8.theirs_ref, ...), custom_call_target="tpu_custom_call" | custom-call | flops 1 | bytes 1 | tf_op jit(solution)/shard_map/x_first_terms/pallas_call | solution.py:266
  46.9 5.1 %z_first_terms.1 = (bf16[2,3,96,1152]{3,2,1,0:T(8,128)(2,1)S(1)}, bf16[2,3,96,1152]{3,2,1,0:T(8,128)(2,1)S(1)}, bf16[3,96,1152]{2,1,0:T(8,128)(2,1)S(1)}, bf16[3...) custom-call(bf16[4,3,48,1792]{3,2,1,0:T(8,128)(2,1)S(1)} %get-tuple-element.32.mark_ref.keep_ref, ...), custom_call_target="tpu_custom_call" | custom-call | flops 1 | bytes 1 | tf_op jit(solution)/shard_map/z_first_terms/pallas_call | solution.py:223
  53.6 2.4 %collective-permute-start.10 = (bf16[2,3,96,1152]{3,2,1,0:T(8,128)(2,1)S(1)}, bf16[2,3,96,1152]{3,2,1,0:T(8,128)(2,1)S(1)}, u32[]{:S(2)}, u32[]{:S(2)}) collective-permute-start(bf16[2,3,96,1152]{3,2,1,0:T(8,128)(2,1)S(1)} %get-tuple-element.37), channel_id=1, source_target_pairs={{0,6},{1,7},{2,0},{3,1},{4,2},{5,3},{6,4},{7,5},{8,14},{9,15},{10,... | collective-permute-start | bytes 3981320 | tf_op jit(solution)/shard_map/ppermute | solution.py:739
  56.0 23.6 %all_weights.1.mark_ref.weights_ref = bf16[8,3,4096,256]{3,2,1,0:T(8,128)(2,1)} custom-call(bf16[3,96,1152]{2,1,0:T(8,128)(2,1)S(1)} %get-tuple-element.34.mark_ref.up_ref, f32[8,2048]{1,0:T(8,128)S(1)} %get-tuple-element.60.conn_ref, f32[24,2048]{1,0:T(8,128)S(1)} %slice.39.grads_ref), custom_call_target="tpu_custom_call" | custom-call | flops 1 | bytes 1 | tf_op jit(solution)/shard_map/all_weights/pallas_call | solution.py:512
  79.5 2.9 %element_weights.1.mark_ref.weights_ref = bf16[3,512,2048]{2,1,0:T(8,128)(2,1)S(1)} custom-call(bf16[8,3,4096,256]{3,2,1,0:T(8,128)(2,1)} %all_weights.1.mark_ref.weights_ref, f32[8,2048]{1,0:T(8,128)S(1)} %get-tuple-element.60.conn_ref, f32[24,2048]{1,0:T(8,128)S(1)} %slice.39.grads_ref), custom_call_target="tpu_custom_call" | custom-call | flops 1 | bytes 1 | tf_op jit(solution)/shard_map/element_weights/pallas_call | solution.py:526
  82.4 2.1 %collective-permute-done.9.plus_ref.direct_ref = bf16[2,3,96,1152]{3,2,1,0:T(8,128)(2,1)S(1)} collective-permute-done((bf16[2,3,96,1152]{3,2,1,0:T(8,128)(2,1)S(1)}, bf16[2,3,96,1152]{3,2,1,0:T(8,128)(2,1)S(1)}, u32[]{:S(2)}, u32[]{:S(2)}) %collective-permute-start.9) | collective-permute-done | bytes 1327136 | tf_op jit(solution)/shard_map/ppermute | solution.py:738
  85.3 2.4 %collective-permute-start.13 = (bf16[3,96,1152]{2,1,0:T(8,128)(2,1)S(1)}, bf16[3,96,1152]{2,1,0:T(8,128)(2,1)S(1)}, u32[]{:S(2)}, u32[]{:S(2)}) collective-permute-start(bf16[3,96,1152]{2,1,0:T(8,128)(2,1)S(1)} %get-tuple-element.42), channel_id=1, source_target_pairs={{0,6},{1,7},{2,0},{3,1},{4,2},{5,3},{6,4},{7,5},{8,14},{9,15},{10,... | collective-permute-start | bytes 1990664 | tf_op jit(solution)/shard_map/ppermute | solution.py:739
  87.7 5.1 %collective-permute-done.11.got_ref = bf16[4,3,48,1792]{3,2,1,0:T(8,128)(2,1)S(1)} collective-permute-done((bf16[4,3,48,1792]{3,2,1,0:T(8,128)(2,1)S(1)}, bf16[4,3,48,1792]{3,2,1,0:T(8,128)(2,1)S(1)}, u32[]{:S(2)}, u32[]{:S(2)}) %collective-permute-start.11) | collective-permute-done | bytes 2064416 | tf_op jit(solution)/shard_map/ppermute | solution.py:740
  96.4 5.0 %collective-permute-done.12.passed_ref = bf16[3,96,1152]{2,1,0:T(8,128)(2,1)S(1)} collective-permute-done((bf16[3,96,1152]{2,1,0:T(8,128)(2,1)S(1)}, bf16[3,96,1152]{2,1,0:T(8,128)(2,1)S(1)}, u32[]{:S(2)}, u32[]{:S(2)}) %collective-permute-start.12) | collective-permute-done | bytes 663584 | tf_op jit(solution)/shard_map/ppermute | solution.py:738
  102.3 10.1 %collective-permute-done.14.plus_ref = bf16[2,3,48,896]{3,2,1,0:T(8,128)(2,1)S(1)} collective-permute-done((bf16[2,3,48,896]{3,2,1,0:T(8,128)(2,1)S(1)}, bf16[2,3,48,896]{3,2,1,0:T(8,128)(2,1)S(1)}, u32[]{:S(2)}, u32[]{:S(2)}) %collective-permute-start.14) | collective-permute-done | bytes 516128 | tf_op jit(solution)/shard_map/ppermute | solution.py:738
  112.6 2.4 %collective-permute-start.18 = (bf16[3,48,896]{2,1,0:T(8,128)(2,1)S(1)}, bf16[3,48,896]{2,1,0:T(8,128)(2,1)S(1)}, u32[]{:S(2)}, u32[]{:S(2)}) collective-permute-start(bf16[3,48,896]{2,1,0:T(8,128)(2,1)S(1)} %get-tuple-element.50), channel_id=1, source_target_pairs={{0,6},{1,7},{2,0},{3,1},{4,2},{5,3},{6,4},{7,5},{8,14},{9,15},{10,... | collective-permute-start | bytes 774152 | tf_op jit(solution)/shard_map/ppermute | solution.py:739
  116.5 12.6 %multiply.3.mark_ref.refs_0_ = f32[3,288,2048]{2,1,0:T(8,128)S(1)} custom-call(bf16[3,96,512]{2,1,0:T(8,128)(2,1)S(1)} %get-tuple-element.47.mark_ref.refs_0_, bf16[3,96,1152]{2,1,0:T(8,128)(2,1)S(1)} %get-tuple-element.48.values_ref, bf16[8,3,4096,256]{3,2,1,0:T(8,128)(2,1)} %all_weights.1.mark_ref.weights_ref), custom_call_target="tpu_custom_call" | custom-call | flops 1 | bytes 1 | tf_op jit(solution)/shard_map/multiply/pallas_call | solution.py:578
  132.3 12.7 %multiply.4.mark_ref.refs_0_ = f32[3,288,2048]{2,1,0:T(8,128)S(1)} custom-call(bf16[3,96,512]{2,1,0:T(8,128)(2,1)S(1)} %get-tuple-element.51.mark_ref.refs_0_, bf16[3,96,1152]{2,1,0:T(8,128)(2,1)S(1)} %get-tuple-element.52.values_ref, bf16[8,3,4096,256]{3,2,1,0:T(8,128)(2,1)} %all_weights.1.mark_ref.weights_ref, ...), custom_call_target="tpu_custom_call", output_to_operand_aliasing={{}: (3, {})} | custom-call | flops 1 | bytes 1 | tf_op jit(solution)/shard_map/multiply/pallas_call | solution.py:578
  146.4 5.7 %collective-permute-start.22 = (bf16[3,96,256]{2,1,0:T(8,128)(2,1)S(1)}, bf16[3,96,256]{2,1,0:T(8,128)(2,1)S(1)}, u32[]{:S(2)}, u32[]{:S(2)}) collective-permute-start(bf16[3,96,256]{2,1,0:T(8,128)(2,1)S(1)} %get-tuple-element.61), channel_id=1, source_target_pairs={{8,0},{16,8},{24,16},{32,24},{40,32},{48,40},{56,48},{64,56},{72,6... | collective-permute-start | bytes 442376 | tf_op jit(solution)/shard_map/ppermute | solution.py:776
  152.1 4.8 %collective-permute-start.21 = (bf16[3,96,256]{2,1,0:T(8,128)(2,1)S(1)}, bf16[3,96,256]{2,1,0:T(8,128)(2,1)S(1)}, u32[]{:S(2)}, u32[]{:S(2)}) collective-permute-start(bf16[3,96,256]{2,1,0:T(8,128)(2,1)S(1)} %get-tuple-element.62), channel_id=1, source_target_pairs={{0,8},{8,16},{16,24},{24,32},{32,40},{40,48},{48,56},{56,64},{64,7... | collective-permute-start | bytes 442376 | tf_op jit(solution)/shard_map/ppermute | solution.py:775
  156.9 15.8 %multiply.5.acc_ref = f32[3,288,2048]{2,1,0:T(8,128)S(1)} custom-call(bf16[3,96,512]{2,1,0:T(8,128)(2,1)S(1)} %get-tuple-element.53.mark_ref, bf16[3,96,1792]{2,1,0:T(8,128)(2,1)S(1)} %get-tuple-element.54.values_ref, bf16[8,3,4096,256]{3,2,1,0:T(8,128)(2,1)} %all_weights.1.mark_ref.weights_ref, ...), custom_call_target="tpu_custom_call", output_to_operand_aliasing={{}: (3, {})} | custom-call | flops 1 | bytes 1 | tf_op jit(solution)/shard_map/multiply/pallas_call | solution.py:578
  172.8 6.1 %element_spectra.1 = f32[4,36,512]{2,1,0:T(8,128)S(1)} custom-call(bf16[3,96,256]{2,1,0:T(8,128)(2,1)S(1)} %collective-permute-done.21.before_ref, bf16[3,96,256]{2,1,0:T(8,128)(2,1)S(1)} %collective-permute-done.22.after_ref, bf16[3,512,2048]{2,1,0:T(8,128)(2,1)S(1)} %element_weights.1.mark_ref.weights_ref, f32[3,288,2048]{2,1,0:T(8,128)S(1)} %multiply.5.acc_ref, ...), custom_call_target="tpu_custom_call" | custom-call | flops 1 | bytes 1 | tf_op jit(solution)/shard_map/element_spectra/pallas_call | solution.py:655
  183.5 2.8 %collective-permute-done.24.c_ref = f32[36,512]{1,0:T(8,128)S(1)} collective-permute-done((f32[36,512]{1,0:T(8,128)S(1)}, f32[36,512]{1,0:T(8,128)S(1)}, u32[]{:S(2)}, u32[]{:S(2)}) %collective-permute-start.24) | collective-permute-done | bytes 73760 | tf_op jit(solution)/shard_map/ppermute | solution.py:779
  (80 shorter events, 30.5 us)
Async XLA Ops:
  15.0 8.9 %collective-permute-start.4 = (bf16[256,384]{1,0:T(8,128)(2,1)S(1)}, bf16[256,384]{1,0:T(8,128)(2,1)S(1)}, u32[]{:S(2)}, u32[]{:S(2)}) collective-permute-start(bf16[256,384]{1,0:T(8,128)(2,1)S(1)} %add_convert_fusion.1.mark_ref), channel_id=1, source_target_pairs={{0,16},{8,24},{16,0},{24,8},{32,48},{40,56},{48,32},{56,40},{64,80... | collective-permute-start | bytes 589832 | tf_op jit(solution)/shard_map/ppermute | solution.py:729
  18.2 9.0 %collective-permute-start.3 = (f32[40,512]{1,0:T(8,128)S(1)}, f32[40,512]{1,0:T(8,128)S(1)}, u32[]{:S(2)}, u32[]{:S(2)}) collective-permute-start(f32[40,512]{1,0:T(8,128)S(1)} %element_data.1), channel_id=1, source_target_pairs={{0,2},{1,3},{2,4},{3,5},{4,6},{5,7},{6,0},{7,1},{8,10},{9,11},{10,... | collective-permute-start | bytes 245768 | tf_op jit(solution)/shard_map/ppermute | solution.py:735
  19.9 7.9 %collective-permute-start.2 = (f32[40,512]{1,0:T(8,128)S(1)}, f32[40,512]{1,0:T(8,128)S(1)}, u32[]{:S(2)}, u32[]{:S(2)}) collective-permute-start(f32[40,512]{1,0:T(8,128)S(1)} %element_data.1), channel_id=1, source_target_pairs={{0,4},{1,5},{2,6},{3,7},{4,0},{5,1},{6,2},{7,3},{8,12},{9,13},{10,... | collective-permute-start | bytes 245768 | tf_op jit(solution)/shard_map/ppermute | solution.py:735
  23.2 4.6 %collective-permute-start.1 = (f32[40,512]{1,0:T(8,128)S(1)}, f32[40,512]{1,0:T(8,128)S(1)}, u32[]{:S(2)}, u32[]{:S(2)}) collective-permute-start(f32[40,512]{1,0:T(8,128)S(1)} %element_data.1), channel_id=1, source_target_pairs={{0,6},{1,7},{2,0},{3,1},{4,2},{5,3},{6,4},{7,5},{8,14},{9,15},{10,... | collective-permute-start | bytes 245768 | tf_op jit(solution)/shard_map/ppermute | solution.py:735
  24.0 7.6 %collective-permute-start.7 = (bf16[256,384]{1,0:T(8,128)(2,1)S(1)}, bf16[256,384]{1,0:T(8,128)(2,1)S(1)}, u32[]{:S(2)}, u32[]{:S(2)}) collective-permute-start(bf16[256,384]{1,0:T(8,128)(2,1)S(1)} %add_convert_fusion.a_ref), channel_id=1, source_target_pairs={{0,96},{8,104},{16,112},{24,120},{32,0},{40,8},{48,16},{56,24},{64... | collective-permute-start | bytes 589832 | tf_op jit(solution)/shard_map/ppermute | solution.py:731
  26.8 6.1 %collective-permute-start.6 = (bf16[256,384]{1,0:T(8,128)(2,1)S(1)}, bf16[256,384]{1,0:T(8,128)(2,1)S(1)}, u32[]{:S(2)}, u32[]{:S(2)}) collective-permute-start(bf16[256,384]{1,0:T(8,128)(2,1)S(1)} %add_convert_fusion.a_ref), channel_id=1, source_target_pairs={{0,64},{8,72},{16,80},{24,88},{32,96},{40,104},{48,112},{56,120},{... | collective-permute-start | bytes 589832 | tf_op jit(solution)/shard_map/ppermute | solution.py:731
  27.2 11.9 %collective-permute-start.5 = (bf16[256,384]{1,0:T(8,128)(2,1)S(1)}, bf16[256,384]{1,0:T(8,128)(2,1)S(1)}, u32[]{:S(2)}, u32[]{:S(2)}) collective-permute-start(bf16[256,384]{1,0:T(8,128)(2,1)S(1)} %add_convert_fusion.a_ref), channel_id=1, source_target_pairs={{0,32},{8,40},{16,48},{24,56},{32,64},{40,72},{48,80},{56,88},{64,... | collective-permute-start | bytes 589832 | tf_op jit(solution)/shard_map/ppermute | solution.py:731
  46.5 46.2 %collective-permute-start.11 = (bf16[4,3,48,1792]{3,2,1,0:T(8,128)(2,1)S(1)}, bf16[4,3,48,1792]{3,2,1,0:T(8,128)(2,1)S(1)}, u32[]{:S(2)}, u32[]{:S(2)}) collective-permute-start(bf16[4,3,48,1792]{3,2,1,0:T(8,128)(2,1)S(1)} %get-tuple-element.39), channel_id=1, source_target_pairs={{0,1},{1,0},{2,3},{3,2},{4,5},{5,4},{6,7},{7,6},{8,9},{9,8},{10,11... | collective-permute-start | bytes 6193160 | tf_op jit(solution)/shard_map/ppermute | solution.py:740
  52.1 32.5 %collective-permute-start.9 = (bf16[2,3,96,1152]{3,2,1,0:T(8,128)(2,1)S(1)}, bf16[2,3,96,1152]{3,2,1,0:T(8,128)(2,1)S(1)}, u32[]{:S(2)}, u32[]{:S(2)}) collective-permute-start(bf16[2,3,96,1152]{3,2,1,0:T(8,128)(2,1)S(1)} %get-tuple-element.36), channel_id=1, source_target_pairs={{0,2},{1,3},{2,4},{3,5},{4,6},{5,7},{6,0},{7,1},{8,10},{9,11},{10,... | collective-permute-start | bytes 3981320 | tf_op jit(solution)/shard_map/ppermute | solution.py:738
  53.6 31.0 %collective-permute-start.10 = (bf16[2,3,96,1152]{3,2,1,0:T(8,128)(2,1)S(1)}, bf16[2,3,96,1152]{3,2,1,0:T(8,128)(2,1)S(1)}, u32[]{:S(2)}, u32[]{:S(2)}) collective-permute-start(bf16[2,3,96,1152]{3,2,1,0:T(8,128)(2,1)S(1)} %get-tuple-element.37), channel_id=1, source_target_pairs={{0,6},{1,7},{2,0},{3,1},{4,2},{5,3},{6,4},{7,5},{8,14},{9,15},{10,... | collective-permute-start | bytes 3981320 | tf_op jit(solution)/shard_map/ppermute | solution.py:739
  84.9 16.5 %collective-permute-start.12 = (bf16[3,96,1152]{2,1,0:T(8,128)(2,1)S(1)}, bf16[3,96,1152]{2,1,0:T(8,128)(2,1)S(1)}, u32[]{:S(2)}, u32[]{:S(2)}) collective-permute-start(bf16[3,96,1152]{2,1,0:T(8,128)(2,1)S(1)} %get-tuple-element.38.mark_ref), channel_id=1, source_target_pairs={{0,2},{1,3},{2,4},{3,5},{4,6},{5,7},{6,0},{7,1},{8,10},{9,11},{10,... | collective-permute-start | bytes 1990664 | tf_op jit(solution)/shard_map/ppermute | solution.py:738
  85.3 16.6 %collective-permute-start.13 = (bf16[3,96,1152]{2,1,0:T(8,128)(2,1)S(1)}, bf16[3,96,1152]{2,1,0:T(8,128)(2,1)S(1)}, u32[]{:S(2)}, u32[]{:S(2)}) collective-permute-start(bf16[3,96,1152]{2,1,0:T(8,128)(2,1)S(1)} %get-tuple-element.42), channel_id=1, source_target_pairs={{0,6},{1,7},{2,0},{3,1},{4,2},{5,3},{6,4},{7,5},{8,14},{9,15},{10,... | collective-permute-start | bytes 1990664 | tf_op jit(solution)/shard_map/ppermute | solution.py:739
  93.7 18.8 %collective-permute-start.14 = (bf16[2,3,48,896]{3,2,1,0:T(8,128)(2,1)S(1)}, bf16[2,3,48,896]{3,2,1,0:T(8,128)(2,1)S(1)}, u32[]{:S(2)}, u32[]{:S(2)}) collective-permute-start(bf16[2,3,48,896]{3,2,1,0:T(8,128)(2,1)S(1)} %get-tuple-element.44), channel_id=1, source_target_pairs={{0,2},{1,3},{2,4},{3,5},{4,6},{5,7},{6,0},{7,1},{8,10},{9,11},{10,... | collective-permute-start | bytes 1548296 | tf_op jit(solution)/shard_map/ppermute | solution.py:738
  94.5 18.0 %collective-permute-start.15 = (bf16[2,3,48,896]{3,2,1,0:T(8,128)(2,1)S(1)}, bf16[2,3,48,896]{3,2,1,0:T(8,128)(2,1)S(1)}, u32[]{:S(2)}, u32[]{:S(2)}) collective-permute-start(bf16[2,3,48,896]{3,2,1,0:T(8,128)(2,1)S(1)} %get-tuple-element.45), channel_id=1, source_target_pairs={{0,6},{1,7},{2,0},{3,1},{4,2},{5,3},{6,4},{7,5},{8,14},{9,15},{10,... | collective-permute-start | bytes 1548296 | tf_op jit(solution)/shard_map/ppermute | solution.py:739
  101.8 13.3 %collective-permute-start.16 = (bf16[3,96,1152]{2,1,0:T(8,128)(2,1)S(1)}, bf16[3,96,1152]{2,1,0:T(8,128)(2,1)S(1)}, u32[]{:S(2)}, u32[]{:S(2)}) collective-permute-start(bf16[3,96,1152]{2,1,0:T(8,128)(2,1)S(1)} %half_sum.2.mark_ref.after_ref.own_ref), channel_id=1, source_target_pairs={{0,1},{1,0},{2,3},{3,2},{4,5},{5,4},{6,7},{7,6},{8,9},{9,8},{10,11... | collective-permute-start | bytes 1990664 | tf_op jit(solution)/shard_map/ppermute | solution.py:740
  112.6 16.5 %collective-permute-start.18 = (bf16[3,48,896]{2,1,0:T(8,128)(2,1)S(1)}, bf16[3,48,896]{2,1,0:T(8,128)(2,1)S(1)}, u32[]{:S(2)}, u32[]{:S(2)}) collective-permute-start(bf16[3,48,896]{2,1,0:T(8,128)(2,1)S(1)} %get-tuple-element.50), channel_id=1, source_target_pairs={{0,6},{1,7},{2,0},{3,1},{4,2},{5,3},{6,4},{7,5},{8,14},{9,15},{10,... | collective-permute-start | bytes 774152 | tf_op jit(solution)/shard_map/ppermute | solution.py:739
  115.1 14.0 %collective-permute-start.17 = (bf16[3,48,896]{2,1,0:T(8,128)(2,1)S(1)}, bf16[3,48,896]{2,1,0:T(8,128)(2,1)S(1)}, u32[]{:S(2)}, u32[]{:S(2)}) collective-permute-start(bf16[3,48,896]{2,1,0:T(8,128)(2,1)S(1)} %get-tuple-element.46.mark_ref), channel_id=1, source_target_pairs={{0,2},{1,3},{2,4},{3,5},{4,6},{5,7},{6,0},{7,1},{8,10},{9,11},{10,... | collective-permute-start | bytes 774152 | tf_op jit(solution)/shard_map/ppermute | solution.py:738
  115.1 15.8 %collective-permute-start.19 = (bf16[3,96,1152]{2,1,0:T(8,128)(2,1)S(1)}, bf16[3,96,1152]{2,1,0:T(8,128)(2,1)S(1)}, u32[]{:S(2)}, u32[]{:S(2)}) collective-permute-start(bf16[3,96,1152]{2,1,0:T(8,128)(2,1)S(1)} %half_sum.3.mark_ref.own_ref), channel_id=1, source_target_pairs={{0,1},{1,0},{2,3},{3,2},{4,5},{5,4},{6,7},{7,6},{8,9},{9,8},{10,11... | collective-permute-start | bytes 1990664 | tf_op jit(solution)/shard_map/ppermute | solution.py:740
  129.4 15.6 %collective-permute-start.20 = (bf16[3,48,1792]{2,1,0:T(8,128)(2,1)S(1)}, bf16[3,48,1792]{2,1,0:T(8,128)(2,1)S(1)}, u32[]{:S(2)}, u32[]{:S(2)}) collective-permute-start(bf16[3,48,1792]{2,1,0:T(8,128)(2,1)S(1)} %ring_sum.1.mark_ref.own_ref), channel_id=1, source_target_pairs={{0,1},{1,0},{2,3},{3,2},{4,5},{5,4},{6,7},{7,6},{8,9},{9,8},{10,11... | collective-permute-start | bytes 1548296 | tf_op jit(solution)/shard_map/ppermute | solution.py:740
  146.4 26.4 %collective-permute-start.22 = (bf16[3,96,256]{2,1,0:T(8,128)(2,1)S(1)}, bf16[3,96,256]{2,1,0:T(8,128)(2,1)S(1)}, u32[]{:S(2)}, u32[]{:S(2)}) collective-permute-start(bf16[3,96,256]{2,1,0:T(8,128)(2,1)S(1)} %get-tuple-element.61), channel_id=1, source_target_pairs={{8,0},{16,8},{24,16},{32,24},{40,32},{48,40},{56,48},{64,56},{72,6... | collective-permute-start | bytes 442376 | tf_op jit(solution)/shard_map/ppermute | solution.py:776
  152.1 20.7 %collective-permute-start.21 = (bf16[3,96,256]{2,1,0:T(8,128)(2,1)S(1)}, bf16[3,96,256]{2,1,0:T(8,128)(2,1)S(1)}, u32[]{:S(2)}, u32[]{:S(2)}) collective-permute-start(bf16[3,96,256]{2,1,0:T(8,128)(2,1)S(1)} %get-tuple-element.62), channel_id=1, source_target_pairs={{0,8},{8,16},{16,24},{24,32},{32,40},{40,48},{48,56},{56,64},{64,7... | collective-permute-start | bytes 442376 | tf_op jit(solution)/shard_map/ppermute | solution.py:775
  178.9 4.6 %collective-permute-start.25 = (f32[36,512]{1,0:T(8,128)S(1)}, f32[36,512]{1,0:T(8,128)S(1)}, u32[]{:S(2)}, u32[]{:S(2)}) collective-permute-start(f32[36,512]{1,0:T(8,128)S(1)} %get-tuple-element.55), channel_id=1, source_target_pairs={{0,6},{1,7},{2,0},{3,1},{4,2},{5,3},{6,4},{7,5},{8,14},{9,15},{10,... | collective-permute-start | bytes 221192 | tf_op jit(solution)/shard_map/ppermute | solution.py:779
  180.8 5.5 %collective-permute-start.24 = (f32[36,512]{1,0:T(8,128)S(1)}, f32[36,512]{1,0:T(8,128)S(1)}, u32[]{:S(2)}, u32[]{:S(2)}) collective-permute-start(f32[36,512]{1,0:T(8,128)S(1)} %get-tuple-element.56), channel_id=1, source_target_pairs={{0,4},{1,5},{2,6},{3,7},{4,0},{5,1},{6,2},{7,3},{8,12},{9,13},{10,... | collective-permute-start | bytes 221192 | tf_op jit(solution)/shard_map/ppermute | solution.py:779
  180.8 6.1 %collective-permute-start.23 = (f32[36,512]{1,0:T(8,128)S(1)}, f32[36,512]{1,0:T(8,128)S(1)}, u32[]{:S(2)}, u32[]{:S(2)}) collective-permute-start(f32[36,512]{1,0:T(8,128)S(1)} %get-tuple-element.57), channel_id=1, source_target_pairs={{0,2},{1,3},{2,4},{3,5},{4,6},{5,7},{6,0},{7,1},{8,10},{9,11},{10,... | collective-permute-start | bytes 221192 | tf_op jit(solution)/shard_map/ppermute | solution.py:779
  (9 other events, 110.2 us)

commit v7 on v5

--- a/solution.py
+++ b/solution.py
@@ -440,7 +440,7 @@
     for at in range(0, nodes, NODE_BLOCK):
         keys = (conn - (first + at)).astype(BF16)
         key = [jnp.broadcast_to(keys[a : a + 1, :], (ROWS, LANES)) for a in range(corners)]
-        for row in range(0, NODE_BLOCK, ROWS):
+        for row in range(0, min(NODE_BLOCK, nodes - at), ROWS):
             node = base + BF16(row)
             sums = [zero] * 3
             for a in range(corners):
@@ -515,7 +515,7 @@
         in_specs=[ANY, VMEM, VMEM],
         out_specs=ANY,
         scratch_shapes=[pltpu.VMEM((slots, 3, count, WIDE), BF16), pltpu.SemaphoreType.DMA((slots, 3))],
-        compiler_params=params(16),
+        compiler_params=params(30),
         cost_estimate=cost(),
         name="all_weights",
     )(mark, data[:8], data[8:32])
@@ -534,58 +534,81 @@
     )(mark, data[:8], data[8:32])
 
 
-SLOTS = 4
-
-
-def multiply_kernel(first, mark_ref, values_ref, weights_ref, *refs):
-    del mark_ref
-    acc_ref, out_ref, held, sems = refs if len(refs) == 4 else (None,) + refs
+def multiply_kernel(mark_ref, values_ref, weights_ref, *refs):
+    del mark_ref
+    acc_ref, out_ref = refs if len(refs) == 2 else (None,) + refs
+    comps, rows, nodes = values_ref.shape
+    values = values_ref[...].reshape(comps * rows, nodes)
+
+    def piece(step, carry):
+        cut = pl.ds(pl.multiple_of(step * WIDE, WIDE), WIDE)
+        for d in range(3):
+            term = jnp.dot(values, weights_ref[d, :, cut], preferred_element_type=F32)
+            out_ref[d, :, cut] = term if acc_ref is None else term + acc_ref[d, :, cut]
+        return carry
+
+    lax.fori_loop(0, out_ref.shape[2] // WIDE, piece, 0)
+
+
+def multiply(mark, values, weights, acc):
+    comps, rows, _ = values.shape
+    elems = weights.shape[2]
+    args = [mark, values, weights] + ([] if acc is None else [acc])
+    return pl.pallas_call(
+        multiply_kernel,
+        out_shape=shaped((3, comps * rows, elems), F32),
+        in_specs=[ANY] + [VMEM] * (len(args) - 1),
+        out_specs=VMEM,
+        input_output_aliases={} if acc is None else {3: 0},
+        compiler_params=params(8),
+        cost_estimate=cost(),
+        name="multiply",
+    )(*args)
+
+
+def fetch_multiply_kernel(mark_ref, values_ref, weights_ref, acc_ref, out_ref, held, sems):
+    del mark_ref
     comps, rows, nodes = values_ref.shape
     values = values_ref[...].reshape(comps * rows, nodes)
     blocks = weights_ref.shape[0]
 
-    def copy(block, slot, d):
-        return pltpu.make_async_copy(
-            weights_ref.at[block, d, pl.ds(first, nodes), :], held.at[slot, d], sems.at[slot, d]
-        )
-
-    for slot in range(SLOTS):
-        for d in range(3):
-            copy(slot, slot, d).start()
-
-    def turn(step, carry):
-        for slot in range(SLOTS):
-            block = step * SLOTS + slot
+    def copy(block, slot):
+        return pltpu.make_async_copy(weights_ref.at[block], held.at[slot], sems.at[slot])
+
+    for slot in range(2):
+        copy(slot, slot).start()
+
+    def pair(twice, carry):
+        for slot in range(2):
+            block = twice * 2 + slot
+            copy(block, slot).wait()
             cut = pl.ds(pl.multiple_of(block * WIDE, WIDE), WIDE)
             for d in range(3):
-                copy(block, slot, d).wait()
                 term = jnp.dot(values, held[slot, d], preferred_element_type=F32)
-                out_ref[d, :, cut] = term if acc_ref is None else term + acc_ref[d, :, cut]
-
-                @pl.when(step < blocks // SLOTS - 1)
-                def _():
-                    copy(block + SLOTS, slot, d).start()
+                out_ref[d, :, cut] = term + acc_ref[d, :, cut]
+
+            @pl.when(twice < blocks // 2 - 1)
+            def _():
+                copy(block + 2, slot).start()
 
         return carry
 
-    lax.fori_loop(0, blocks // SLOTS, turn, 0)
-
-
-def multiply(mark, values, weights, first, acc):
-    comps, rows, nodes = values.shape
-    elems = weights.shape[0] * WIDE
-    args = [mark, values, weights] + ([] if acc is None else [acc])
-    return pl.pallas_call(
-        functools.partial(multiply_kernel, first),
-        out_shape=shaped((3, comps * rows, elems), F32),
-        in_specs=[ANY, VMEM, ANY] + [VMEM] * (len(args) - 3),
+    lax.fori_loop(0, blocks // 2, pair, 0)
+
+
+def fetch_multiply(mark, values, weights, acc):
+    nodes = values.shape[2]
+    return pl.pallas_call(
+        fetch_multiply_kernel,
+        out_shape=shaped(acc.shape, F32),
+        in_specs=[ANY, VMEM, ANY, VMEM],
         out_specs=VMEM,
-        input_output_aliases={} if acc is None else {3: 0},
-        scratch_shapes=[pltpu.VMEM((SLOTS, 3, nodes, WIDE), BF16), pltpu.SemaphoreType.DMA((SLOTS, 3))],
-        compiler_params=params(24),
-        cost_estimate=cost(),
-        name="multiply",
-    )(*args)
+        input_output_aliases={3: 0},
+        scratch_shapes=[pltpu.VMEM((2, 3, nodes, WIDE), BF16), pltpu.SemaphoreType.DMA((2,))],
+        compiler_params=params(34),
+        cost_estimate=cost(),
+        name="fetch_multiply",
+    )(mark, values, weights, acc)
 
 
 def spectra_kernel(before_ref, after_ref, weights_ref, acc_ref, modulus_ref, out_ref, grads):
@@ -751,30 +774,32 @@
     got_0 = side(away)
     ways_1 = z_first_terms(keep, resp, shapes, c_1, 43)
     plus_1, minus_1 = up(ways_1[0]), down(ways_1[1])
-    weights = all_weights(ways_1[2], data, nodes)
-    rim_weights = element_weights(weights, data, nodes, 2 * bound)
-    on_1 = pass_on(rim_weights, ways_1[2], ways_1[3], plus_1, minus_1)
+    weights_0 = all_weights(ways_1[2], data, w_0)
+    on_1 = pass_on(weights_0, ways_1[2], ways_1[3], plus_1, minus_1)
     up_1, down_1 = up(on_1[0]), down(on_1[1])
     ways_0 = x_sum(on_1[0], keep, got_0)
     plus_0, minus_0 = up(ways_0[0]), down(ways_0[1])
-    low_1 = half_sum(ways_0[2], ways_0[2], 0, ways_1[4], minus_1, up_1)
+    weights_low = element_weights(ways_0[2], data, w_0, w_1 // 2)
+    low_1 = half_sum(weights_low, weights_low, 0, ways_1[4], minus_1, up_1)
     side_low = side(low_1)
     high_1 = half_sum(low_1, low_1, 1, ways_1[4], plus_1, down_1)
     side_high = side(high_1)
-    on_0 = pass_on(high_1, ways_0[2], ways_0[3], plus_0, minus_0)
+    weights_high = element_weights(high_1, data, middle, w_1 // 2)
+    on_0 = pass_on(weights_high, ways_0[2], ways_0[3], plus_0, minus_0)
     up_0, down_0 = up(on_0[0]), down(on_0[1])
     values_low, rim = gather_rows(on_0[0], lists, low_1, side_low, None, w_0, full)
-    acc = multiply(rim, values_low, weights, w_0, None)
+    acc = multiply(rim, values_low, weights_low, None)
     own_0 = ring_sum(acc, ways_0[4], plus_0, minus_0, up_0, down_0)
     side_0 = side(own_0)
-    values_high, rim = gather_rows(own_0, lists, high_1, side_high, rim, middle, full)
-    acc = multiply(rim, values_high, weights, middle, acc)
+    rim_weights = element_weights(own_0, data, nodes, 2 * bound)
+    values_high, rim = gather_rows(rim_weights, lists, high_1, side_high, rim, middle, full)
+    acc = multiply(rim, values_high, weights_high, acc)
     values_0, rim = gather_rows(acc, lists, own_0, side_0, rim, 0, full)
 
     count = lax.axis_size("mesh")
     before = lax.ppermute(rim[..., bound:], "mesh", [(p, p + 1) for p in range(count - 1)])
     after = lax.ppermute(rim[..., :bound], "mesh", [(p + 1, p) for p in range(count - 1)])
-    acc = multiply(rim, values_0, weights, 0, acc)
+    acc = fetch_multiply(rim, values_0, weights_0, acc)
     spectra = element_spectra(before, after, rim_weights, acc, data[32:40])
     back = [spectra[0]] + [lax.ppermute(spectra[j], "mode", mode_perm(j)) for j in range(1, Z)]
     return collect(z_at.astype(jnp.int32).reshape(1), back)

time: 193 us -> 196 us (1.016)
  waiting for transfers between devices: 40.9 us -> 24 us
  Pallas kernels: 106 us -> 118 us
  local copies, waits for them, and re-layouts: 1.16 us -> 8.09 us
    pallas_call x3, Pallas kernels: 45.5 us -> 25.8 us  [the longest x1 13 us: fetch_multiply(): pl.pallas_call(fetch_multiply_kernel, out_shape=shaped(acc.shape, F32), i...]
    pallas_call x1, Pallas kernels: 23.6 us -> 38.4 us  [all_weights(): pl.pallas_call(all_weights_kernel, out_shape=shaped((elems // WIDE, 3, no...]
    pallas_call x1 -> x3, Pallas kernels: 2.9 us -> 15.5 us  [element_weights(): pl.pallas_call(functools.partial(weights_kernel, float(first)), out_shape...]
    ppermute x4, waiting for transfers between devices: 17.2 us -> 5.94 us  [local(): up = lambda v: lax.ppermute(v, 'mode', up_perm)]
    unnamed x15 -> x17, local copies, waits for them, and re-layouts: 0.03 us -> 6.96 us
    ppermute x3, waiting for transfers between devices: 11.2 us -> 6.05 us  [local(): lax.ppermute(pair, 'mesh', mesh_perm(dy))]
    ppermute x1, starting transfers between devices: 5.72 us -> 1.92 us  [local(): lax.ppermute(rim[..., :bound], 'mesh', [(p + 1, p) for p in range(count -...]
    ppermute x4, starting transfers between devices: 9.14 us -> 11.3 us  [local(): down = lambda v: lax.ppermute(v, 'mode', down_perm)]
  transfers between devices with their start and end apart: 26 -> 26, of which waited for: 12 -> 11; matrix products, arithmetic and copies ran while one was open for 0% -> 0% of each run, Pallas kernels for 43% -> 48%
where the time goes in v7:
time: 196 us; the launch traced here: 195 us
  Pallas kernels  118 us (60%)
  starting transfers between devices  43.2 us (22%)
  waiting for transfers between devices  24 us (12%)
  local copies, waits for them, and re-layouts  8.09 us (4%)
    pallas_call x1, Pallas kernels, all_weights(): pl.pallas_call(all_weights_kernel, out_shape=shaped((elems // WIDE, 3, no...  38.4 us
    pallas_call x3, Pallas kernels, element_weights(): pl.pallas_call(functools.partial(weights_kernel, float(first)), out_shape...  15.5 us
    pallas_call x1, Pallas kernels, fetch_multiply(): pl.pallas_call(fetch_multiply_kernel, out_shape=shaped(acc.shape, F32), i...  13 us
    pallas_call x2, Pallas kernels, multiply(): pl.pallas_call(multiply_kernel, out_shape=shaped((3, comps * rows, elems)...  12.8 us
    ppermute x4, starting transfers between devices, local(): down = lambda v: lax.ppermute(v, 'mode', down_perm)  11.3 us
    pallas_call x1, Pallas kernels, partial_loads(): pl.pallas_call(functools.partial(loads_kernel, cuts), out_shape=(shaped((...  11.1 us
    unnamed x17, local copies, waits for them, and re-layouts  6.96 us
    ppermute x1, starting transfers between devices, local(): lax.ppermute(rim[..., bound:], 'mesh', [(p, p + 1) for p in range(count -...  6.84 us
  transfers between devices with their start and end apart: 26, of which 11 were waited for; matrix products, arithmetic and copies ran while one was open for 0% of the time, Pallas kernels for 48%

profile of v7, /device:TPU:1, one launch (start us, length us, event | category | flops | bytes accessed | tf_op | source)
XLA Modules:
  0.0 194.7 jit_solution(79457221143760538)
XLA Ops:
  0.0 11.1 %modal_loads.1 = (f32[256,384]{1,0:T(8,128)}, bf16[256,384]{1,0:T(8,128)(2,1)}) custom-call(s32[1]{0:T(128)} %bitcast.1.core_ref, bf16[3,500,4096]{2,1,0:T(8,128)(2,1)} %bitcast.19, bf16[3,4096,384]{2,1,0:T(8,128)(2,1)} %load_ref.1), custom_call_target="tpu_custom_call" | custom-call | flops 1 | bytes 1 | tf_op jit(solution)/shard_map/modal_loads/pallas_call | solution.py:88
  15.0 2.9 %collective-permute-start.4 = (bf16[256,384]{1,0:T(8,128)(2,1)S(1)}, bf16[256,384]{1,0:T(8,128)(2,1)S(1)}, u32[]{:S(2)}, u32[]{:S(2)}) collective-permute-start(bf16[256,384]{1,0:T(8,128)(2,1)S(1)} %add_convert_fusion.1.mark_ref), channel_id=1, source_target_pairs={{0,16},{8,24},{16,0},{24,8},{32,48},{40,56},{48,32},{56,40},{64,80... | collective-permute-start | bytes 589832 | tf_op jit(solution)/shard_map/ppermute | solution.py:752
  18.2 3.8 %collective-permute-start.1 = (f32[40,512]{1,0:T(8,128)S(1)}, f32[40,512]{1,0:T(8,128)S(1)}, u32[]{:S(2)}, u32[]{:S(2)}) collective-permute-start(f32[40,512]{1,0:T(8,128)S(1)} %element_data.1), channel_id=1, source_target_pairs={{0,6},{1,7},{2,0},{3,1},{4,2},{5,3},{6,4},{7,5},{8,14},{9,15},{10,... | collective-permute-start | bytes 245768 | tf_op jit(solution)/shard_map/ppermute | solution.py:758
  29.2 5.3 %collective-permute-done.6.c_ref = bf16[256,384]{1,0:T(8,128)(2,1)S(1)} collective-permute-done((bf16[256,384]{1,0:T(8,128)(2,1)S(1)}, bf16[256,384]{1,0:T(8,128)(2,1)S(1)}, u32[]{:S(2)}, u32[]{:S(2)}) %collective-permute-start.6) | collective-permute-done | bytes 196640 | tf_op jit(solution)/shard_map/ppermute | solution.py:754
  38.4 5.9 %x_first_terms.1 = (bf16[4,3,48,1792]{3,2,1,0:T(8,128)(2,1)}, bf16[4,3,48,1792]{3,2,1,0:T(8,128)(2,1)S(1)}, bf16[384,500]{1,0:T(8,128)(2,1)S(1)}) custom-call(s32[1]{0:T(128)} %bitcast.1.core_ref, bf16[256,384]{1,0:T(8,128)(2,1)S(1)} %modal_response.1.mine_ref, bf16[256,384]{1,0:T(8,128)(2,1)S(1)} %collective-permute-done.8.theirs_ref, ...), custom_call_target="tpu_custom_call" | custom-call | flops 1 | bytes 1 | tf_op jit(solution)/shard_map/x_first_terms/pallas_call | solution.py:266
  45.6 6.0 %z_first_terms.1 = (bf16[2,3,96,1152]{3,2,1,0:T(8,128)(2,1)}, bf16[2,3,96,1152]{3,2,1,0:T(8,128)(2,1)}, bf16[3,96,1152]{2,1,0:T(8,128)(2,1)S(1)}, bf16[3,96,1152...) custom-call(bf16[4,3,48,1792]{3,2,1,0:T(8,128)(2,1)S(1)} %get-tuple-element.32.mark_ref.keep_ref, ...), custom_call_target="tpu_custom_call" | custom-call | flops 1 | bytes 1 | tf_op jit(solution)/shard_map/z_first_terms/pallas_call | solution.py:223
  51.6 3.8 %collective-permute-start.10 = (bf16[2,3,96,1152]{3,2,1,0:T(8,128)(2,1)}, bf16[2,3,96,1152]{3,2,1,0:T(8,128)(2,1)S(1)}, u32[]{:S(2)}, u32[]{:S(2)}) collective-permute-start(bf16[2,3,96,1152]{3,2,1,0:T(8,128)(2,1)} %get-tuple-element.37), channel_id=1, source_target_pairs={{0,6},{1,7},{2,0},{3,1},{4,2},{5,3},{6,4},{7,5},{8,14},{9,15},{10,... | collective-permute-start | bytes 3981320 | tf_op jit(solution)/shard_map/ppermute | solution.py:762
  55.5 38.4 %all_weights.1.mark_ref.weights_ref = bf16[8,3,1792,256]{3,2,1,0:T(8,128)(2,1)S(1)} custom-call(bf16[3,96,1152]{2,1,0:T(8,128)(2,1)S(1)} %get-tuple-element.34.mark_ref.up_ref, f32[8,2048]{1,0:T(8,128)S(1)} %get-tuple-element.60.conn_ref, f32[24,2048]{1,0:T(8,128)S(1)} %slice.43.grads_ref), custom_call_target="tpu_custom_call" | custom-call | flops 1 | bytes 1 | tf_op jit(solution)/shard_map/all_weights/pallas_call | solution.py:512
  94.3 6.9 %copy-done = bf16[8,3,1792,256]{3,2,1,0:T(8,128)(2,1)} copy-done((bf16[8,3,1792,256]{3,2,1,0:T(8,128)(2,1)}, bf16[8,3,1792,256]{3,2,1,0:T(8,128)(2,1)S(1)}, u32[]{:S(2)}) %copy-start) | copy-done | bytes 22020120
  101.2 2.7 %collective-permute-start.13 = (bf16[3,96,1152]{2,1,0:T(8,128)(2,1)S(1)}, bf16[3,96,1152]{2,1,0:T(8,128)(2,1)S(1)}, u32[]{:S(2)}, u32[]{:S(2)}) collective-permute-start(bf16[3,96,1152]{2,1,0:T(8,128)(2,1)S(1)} %get-tuple-element.42), channel_id=1, source_target_pairs={{0,6},{1,7},{2,0},{3,1},{4,2},{5,3},{6,4},{7,5},{8,14},{9,15},{10,... | collective-permute-start | bytes 1990664 | tf_op jit(solution)/shard_map/ppermute | solution.py:762
  103.9 2.7 %x_sum.1 = (bf16[2,3,48,896]{3,2,1,0:T(8,128)(2,1)S(1)}, bf16[2,3,48,896]{3,2,1,0:T(8,128)(2,1)S(1)}, bf16[3,48,896]{2,1,0:T(8,128)(2,1)S(1)}, bf16[3,48,896]{2,1,0:T(8,128)(2,1)S(1)}, bf16[3,48,1792]{2,1,0:T(8,128)(2,1)S(1)}) custom-call(bf16[3,96,1152]{2,1,0:T(8,128)(2,1)S(1)} %get-tuple-element.38.mark_ref, ...), custom_call_target="tpu_custom_call" | custom-call | flops 1 | bytes 1 | tf_op jit(solution)/shard_map/x_sum/pallas_call | solution.py:299
  106.7 2.7 %collective-permute-start.15 = (bf16[2,3,48,896]{3,2,1,0:T(8,128)(2,1)S(1)}, bf16[2,3,48,896]{3,2,1,0:T(8,128)(2,1)S(1)}, u32[]{:S(2)}, u32[]{:S(2)}) collective-permute-start(bf16[2,3,48,896]{3,2,1,0:T(8,128)(2,1)S(1)} %get-tuple-element.45), channel_id=1, source_target_pairs={{0,6},{1,7},{2,0},{3,1},{4,2},{5,3},{6,4},{7,5},{8,14},{9,15},{10,... | collective-permute-start | bytes 1548296 | tf_op jit(solution)/shard_map/ppermute | solution.py:762
  109.4 6.3 %element_weights.3.mark_ref.after_ref.weights_ref = bf16[3,1152,2048]{2,1,0:T(8,128)(2,1)S(1)} custom-call(bf16[3,48,896]{2,1,0:T(8,128)(2,1)S(1)} %get-tuple-element.40.mark_ref.up_ref, f32[8,2048]{1,0:T(8,128)S(1)} %get-tuple-element.60.conn_ref, f32[24,2048]{1,0:T(8,128)S(1)} %slice.43.grads_ref), custom_call_target="tpu_custom_call" | custom-call | flops 1 | bytes 1 | tf_op jit(solution)/shard_map/element_weights/pallas_call | solution.py:526
  119.0 6.3 %element_weights.4.mark_ref.weights_ref = bf16[3,1152,2048]{2,1,0:T(8,128)(2,1)S(1)} custom-call(bf16[3,96,1152]{2,1,0:T(8,128)(2,1)S(1)} %half_sum.3.mark_ref.own_ref, f32[8,2048]{1,0:T(8,128)S(1)} %get-tuple-element.60.conn_ref, f32[24,2048]{1,0:T(8,128)S(1)} %slice.43.grads_ref), custom_call_target="tpu_custom_call" | custom-call | flops 1 | bytes 1 | tf_op jit(solution)/shard_map/element_weights/pallas_call | solution.py:526
  125.3 3.7 %collective-permute-done.14.plus_ref = bf16[2,3,48,896]{3,2,1,0:T(8,128)(2,1)S(1)} collective-permute-done((bf16[2,3,48,896]{3,2,1,0:T(8,128)(2,1)S(1)}, bf16[2,3,48,896]{3,2,1,0:T(8,128)(2,1)S(1)}, u32[]{:S(2)}, u32[]{:S(2)}) %collective-permute-start.14) | collective-permute-done | bytes 516128 | tf_op jit(solution)/shard_map/ppermute | solution.py:761
  133.5 6.2 %multiply.2.mark_ref.refs_0_ = f32[3,288,2048]{2,1,0:T(8,128)S(1)} custom-call(bf16[3,96,512]{2,1,0:T(8,128)(2,1)S(1)} %get-tuple-element.47.mark_ref.refs_0_, bf16[3,96,1152]{2,1,0:T(8,128)(2,1)S(1)} %get-tuple-element.48.values_ref, bf16[3,1152,2048]{2,1,0:T(8,128)(2,1)S(1)} %element_weights.3.mark_ref.after_ref.weights_ref), custom_call_target="tpu_custom_call" | custom-call | flops 1 | bytes 1 | tf_op jit(solution)/shard_map/multiply/pallas_call | solution.py:557
  141.3 2.9 %element_weights.5.mark_ref.weights_ref = bf16[3,512,2048]{2,1,0:T(8,128)(2,1)S(1)} custom-call(bf16[3,48,1792]{2,1,0:T(8,128)(2,1)S(1)} %ring_sum.1.mark_ref.own_ref, f32[8,2048]{1,0:T(8,128)S(1)} %get-tuple-element.60.conn_ref, f32[24,2048]{1,0:T(8,128)S(1)} %slice.43.grads_ref), custom_call_target="tpu_custom_call" | custom-call | flops 1 | bytes 1 | tf_op jit(solution)/shard_map/element_weights/pallas_call | solution.py:526
  144.2 3.1 %collective-permute-done.19.got_ref = bf16[3,96,1152]{2,1,0:T(8,128)(2,1)S(1)} collective-permute-done((bf16[3,96,1152]{2,1,0:T(8,128)(2,1)S(1)}, bf16[3,96,1152]{2,1,0:T(8,128)(2,1)S(1)}, u32[]{:S(2)}, u32[]{:S(2)}) %collective-permute-start.19) | collective-permute-done | bytes 663584 | tf_op jit(solution)/shard_map/ppermute | solution.py:763
  148.7 6.6 %multiply.3.mark_ref.acc_ref = f32[3,288,2048]{2,1,0:T(8,128)S(1)} custom-call(bf16[3,96,512]{2,1,0:T(8,128)(2,1)S(1)} %get-tuple-element.51.mark_ref.refs_0_, bf16[3,96,1152]{2,1,0:T(8,128)(2,1)S(1)} %get-tuple-element.52.values_ref, bf16[3,1152,2048]{2,1,0:T(8,128)(2,1)S(1)} %element_weights.4.mark_ref.weights_ref, ...), custom_call_target="tpu_custom_call", output_to_operand_aliasing={{}: (3, {})} | custom-call | flops 1 | bytes 1 | tf_op jit(solution)/shard_map/multiply/pallas_call | solution.py:557
  155.3 3.1 %collective-permute-done.20.got_ref = bf16[3,48,1792]{2,1,0:T(8,128)(2,1)S(1)} collective-permute-done((bf16[3,48,1792]{2,1,0:T(8,128)(2,1)S(1)}, bf16[3,48,1792]{2,1,0:T(8,128)(2,1)S(1)}, u32[]{:S(2)}, u32[]{:S(2)}) %collective-permute-start.20) | collective-permute-done | bytes 516128 | tf_op jit(solution)/shard_map/ppermute | solution.py:763
  159.8 6.8 %collective-permute-start.21 = (bf16[3,96,256]{2,1,0:T(8,128)(2,1)S(1)}, bf16[3,96,256]{2,1,0:T(8,128)(2,1)S(1)}, u32[]{:S(2)}, u32[]{:S(2)}) collective-permute-start(bf16[3,96,256]{2,1,0:T(8,128)(2,1)S(1)} %get-tuple-element.62), channel_id=1, source_target_pairs={{0,8},{8,16},{16,24},{24,32},{32,40},{40,48},{48,56},{56,64},{64,7... | collective-permute-start | bytes 442376 | tf_op jit(solution)/shard_map/ppermute | solution.py:800
  168.6 13.0 %fetch_multiply.1.acc_ref = f32[3,288,2048]{2,1,0:T(8,128)S(1)} custom-call(bf16[3,96,512]{2,1,0:T(8,128)(2,1)S(1)} %get-tuple-element.53.mark_ref, bf16[3,96,1792]{2,1,0:T(8,128)(2,1)S(1)} %get-tuple-element.54.values_ref, bf16[8,3,1792,256]{3,2,1,0:T(8,128)(2,1)} %copy-done, ...), custom_call_target="tpu_custom_call", output_to_operand_aliasing={{}: (3, {})} | custom-call | flops 1 | bytes 1 | tf_op jit(solution)/shard_map/fetch_multiply/pallas_call | solution.py:601
  181.6 6.1 %element_spectra.1 = f32[4,36,512]{2,1,0:T(8,128)S(1)} custom-call(bf16[3,96,256]{2,1,0:T(8,128)(2,1)S(1)} %collective-permute-done.21.before_ref, bf16[3,96,256]{2,1,0:T(8,128)(2,1)S(1)} %collective-permute-done.22.after_ref, bf16[3,512,2048]{2,1,0:T(8,128)(2,1)S(1)} %element_weights.5.mark_ref.weights_ref, f32[3,288,2048]{2,1,0:T(8,128)S(1)} %fetch_multiply.1.acc_ref, ...), custom_call_target="tpu_custom_call" | custom-call | flops 1 | bytes 1 | tf_op jit(solution)/shard_map/element_spectra/pallas_call | solution.py:678
  190.5 2.7 %collective-permute-done.23.b_ref = f32[36,512]{1,0:T(8,128)S(1)} collective-permute-done((f32[36,512]{1,0:T(8,128)S(1)}, f32[36,512]{1,0:T(8,128)S(1)}, u32[]{:S(2)}, u32[]{:S(2)}) %collective-permute-start.23) | collective-permute-done | bytes 73760 | tf_op jit(solution)/shard_map/ppermute | solution.py:804
  (84 shorter events, 35.3 us)
Async XLA Ops:
  15.0 7.7 %collective-permute-start.4 = (bf16[256,384]{1,0:T(8,128)(2,1)S(1)}, bf16[256,384]{1,0:T(8,128)(2,1)S(1)}, u32[]{:S(2)}, u32[]{:S(2)}) collective-permute-start(bf16[256,384]{1,0:T(8,128)(2,1)S(1)} %add_convert_fusion.1.mark_ref), channel_id=1, source_target_pairs={{0,16},{8,24},{16,0},{24,8},{32,48},{40,56},{48,32},{56,40},{64,80... | collective-permute-start | bytes 589832 | tf_op jit(solution)/shard_map/ppermute | solution.py:752
  18.2 8.6 %collective-permute-start.1 = (f32[40,512]{1,0:T(8,128)S(1)}, f32[40,512]{1,0:T(8,128)S(1)}, u32[]{:S(2)}, u32[]{:S(2)}) collective-permute-start(f32[40,512]{1,0:T(8,128)S(1)} %element_data.1), channel_id=1, source_target_pairs={{0,6},{1,7},{2,0},{3,1},{4,2},{5,3},{6,4},{7,5},{8,14},{9,15},{10,... | collective-permute-start | bytes 245768 | tf_op jit(solution)/shard_map/ppermute | solution.py:758
  22.0 5.9 %collective-permute-start.2 = (f32[40,512]{1,0:T(8,128)S(1)}, f32[40,512]{1,0:T(8,128)S(1)}, u32[]{:S(2)}, u32[]{:S(2)}) collective-permute-start(f32[40,512]{1,0:T(8,128)S(1)} %element_data.1), channel_id=1, source_target_pairs={{0,4},{1,5},{2,6},{3,7},{4,0},{5,1},{6,2},{7,3},{8,12},{9,13},{10,... | collective-permute-start | bytes 245768 | tf_op jit(solution)/shard_map/ppermute | solution.py:758
  22.0 6.4 %collective-permute-start.3 = (f32[40,512]{1,0:T(8,128)S(1)}, f32[40,512]{1,0:T(8,128)S(1)}, u32[]{:S(2)}, u32[]{:S(2)}) collective-permute-start(f32[40,512]{1,0:T(8,128)S(1)} %element_data.1), channel_id=1, source_target_pairs={{0,2},{1,3},{2,4},{3,5},{4,6},{5,7},{6,0},{7,1},{8,10},{9,11},{10,... | collective-permute-start | bytes 245768 | tf_op jit(solution)/shard_map/ppermute | solution.py:758
  22.8 6.4 %collective-permute-start.5 = (bf16[256,384]{1,0:T(8,128)(2,1)S(1)}, bf16[256,384]{1,0:T(8,128)(2,1)S(1)}, u32[]{:S(2)}, u32[]{:S(2)}) collective-permute-start(bf16[256,384]{1,0:T(8,128)(2,1)S(1)} %add_convert_fusion.a_ref), channel_id=1, source_target_pairs={{0,32},{8,40},{16,48},{24,56},{32,64},{40,72},{48,80},{56,88},{64,... | collective-permute-start | bytes 589832 | tf_op jit(solution)/shard_map/ppermute | solution.py:754
  24.2 10.3 %collective-permute-start.6 = (bf16[256,384]{1,0:T(8,128)(2,1)S(1)}, bf16[256,384]{1,0:T(8,128)(2,1)S(1)}, u32[]{:S(2)}, u32[]{:S(2)}) collective-permute-start(bf16[256,384]{1,0:T(8,128)(2,1)S(1)} %add_convert_fusion.a_ref), channel_id=1, source_target_pairs={{0,64},{8,72},{16,80},{24,88},{32,96},{40,104},{48,112},{56,120},{... | collective-permute-start | bytes 589832 | tf_op jit(solution)/shard_map/ppermute | solution.py:754
  26.8 7.7 %collective-permute-start.7 = (bf16[256,384]{1,0:T(8,128)(2,1)S(1)}, bf16[256,384]{1,0:T(8,128)(2,1)S(1)}, u32[]{:S(2)}, u32[]{:S(2)}) collective-permute-start(bf16[256,384]{1,0:T(8,128)(2,1)S(1)} %add_convert_fusion.a_ref), channel_id=1, source_target_pairs={{0,96},{8,104},{16,112},{24,120},{32,0},{40,8},{48,16},{56,24},{64... | collective-permute-start | bytes 589832 | tf_op jit(solution)/shard_map/ppermute | solution.py:754
  44.3 59.6 %collective-permute-start.11 = (bf16[4,3,48,1792]{3,2,1,0:T(8,128)(2,1)}, bf16[4,3,48,1792]{3,2,1,0:T(8,128)(2,1)}, u32[]{:S(2)}, u32[]{:S(2)}) collective-permute-start(bf16[4,3,48,1792]{3,2,1,0:T(8,128)(2,1)} %get-tuple-element.39), channel_id=1, source_target_pairs={{0,1},{1,0},{2,3},{3,2},{4,5},{5,4},{6,7},{7,6},{8,9},{9,8},{10,11... | collective-permute-start | bytes 6193160 | tf_op jit(solution)/shard_map/ppermute | solution.py:763
  51.6 42.3 %collective-permute-start.10 = (bf16[2,3,96,1152]{3,2,1,0:T(8,128)(2,1)}, bf16[2,3,96,1152]{3,2,1,0:T(8,128)(2,1)S(1)}, u32[]{:S(2)}, u32[]{:S(2)}) collective-permute-start(bf16[2,3,96,1152]{3,2,1,0:T(8,128)(2,1)} %get-tuple-element.37), channel_id=1, source_target_pairs={{0,6},{1,7},{2,0},{3,1},{4,2},{5,3},{6,4},{7,5},{8,14},{9,15},{10,... | collective-permute-start | bytes 3981320 | tf_op jit(solution)/shard_map/ppermute | solution.py:762
  55.4 38.5 %collective-permute-start.9 = (bf16[2,3,96,1152]{3,2,1,0:T(8,128)(2,1)}, bf16[2,3,96,1152]{3,2,1,0:T(8,128)(2,1)S(1)}, u32[]{:S(2)}, u32[]{:S(2)}) collective-permute-start(bf16[2,3,96,1152]{3,2,1,0:T(8,128)(2,1)} %get-tuple-element.36), channel_id=1, source_target_pairs={{0,2},{1,3},{2,4},{3,5},{4,6},{5,7},{6,0},{7,1},{8,10},{9,11},{10,... | collective-permute-start | bytes 3981320 | tf_op jit(solution)/shard_map/ppermute | solution.py:761
  101.2 16.7 %collective-permute-start.12 = (bf16[3,96,1152]{2,1,0:T(8,128)(2,1)S(1)}, bf16[3,96,1152]{2,1,0:T(8,128)(2,1)S(1)}, u32[]{:S(2)}, u32[]{:S(2)}) collective-permute-start(bf16[3,96,1152]{2,1,0:T(8,128)(2,1)S(1)} %get-tuple-element.38.mark_ref), channel_id=1, source_target_pairs={{0,2},{1,3},{2,4},{3,5},{4,6},{5,7},{6,0},{7,1},{8,10},{9,11},{10,... | collective-permute-start | bytes 1990664 | tf_op jit(solution)/shard_map/ppermute | solution.py:761
  101.2 17.4 %collective-permute-start.13 = (bf16[3,96,1152]{2,1,0:T(8,128)(2,1)S(1)}, bf16[3,96,1152]{2,1,0:T(8,128)(2,1)S(1)}, u32[]{:S(2)}, u32[]{:S(2)}) collective-permute-start(bf16[3,96,1152]{2,1,0:T(8,128)(2,1)S(1)} %get-tuple-element.42), channel_id=1, source_target_pairs={{0,6},{1,7},{2,0},{3,1},{4,2},{5,3},{6,4},{7,5},{8,14},{9,15},{10,... | collective-permute-start | bytes 1990664 | tf_op jit(solution)/shard_map/ppermute | solution.py:762
  106.6 22.4 %collective-permute-start.14 = (bf16[2,3,48,896]{3,2,1,0:T(8,128)(2,1)S(1)}, bf16[2,3,48,896]{3,2,1,0:T(8,128)(2,1)S(1)}, u32[]{:S(2)}, u32[]{:S(2)}) collective-permute-start(bf16[2,3,48,896]{3,2,1,0:T(8,128)(2,1)S(1)} %get-tuple-element.44), channel_id=1, source_target_pairs={{0,2},{1,3},{2,4},{3,5},{4,6},{5,7},{6,0},{7,1},{8,10},{9,11},{10,... | collective-permute-start | bytes 1548296 | tf_op jit(solution)/shard_map/ppermute | solution.py:761
  106.7 22.3 %collective-permute-start.15 = (bf16[2,3,48,896]{3,2,1,0:T(8,128)(2,1)S(1)}, bf16[2,3,48,896]{3,2,1,0:T(8,128)(2,1)S(1)}, u32[]{:S(2)}, u32[]{:S(2)}) collective-permute-start(bf16[2,3,48,896]{3,2,1,0:T(8,128)(2,1)S(1)} %get-tuple-element.45), channel_id=1, source_target_pairs={{0,6},{1,7},{2,0},{3,1},{4,2},{5,3},{6,4},{7,5},{8,14},{9,15},{10,... | collective-permute-start | bytes 1548296 | tf_op jit(solution)/shard_map/ppermute | solution.py:762
  118.3 13.8 %collective-permute-start.16 = (bf16[3,96,1152]{2,1,0:T(8,128)(2,1)S(1)}, bf16[3,96,1152]{2,1,0:T(8,128)(2,1)S(1)}, u32[]{:S(2)}, u32[]{:S(2)}) collective-permute-start(bf16[3,96,1152]{2,1,0:T(8,128)(2,1)S(1)} %half_sum.2.mark_ref.after_ref.own_ref), channel_id=1, source_target_pairs={{0,1},{1,0},{2,3},{3,2},{4,5},{5,4},{6,7},{7,6},{8,9},{9,8},{10,11... | collective-permute-start | bytes 1990664 | tf_op jit(solution)/shard_map/ppermute | solution.py:763
  129.2 10.6 %collective-permute-start.17 = (bf16[3,48,896]{2,1,0:T(8,128)(2,1)S(1)}, bf16[3,48,896]{2,1,0:T(8,128)(2,1)S(1)}, u32[]{:S(2)}, u32[]{:S(2)}) collective-permute-start(bf16[3,48,896]{2,1,0:T(8,128)(2,1)S(1)} %get-tuple-element.46.mark_ref), channel_id=1, source_target_pairs={{0,2},{1,3},{2,4},{3,5},{4,6},{5,7},{6,0},{7,1},{8,10},{9,11},{10,... | collective-permute-start | bytes 774152 | tf_op jit(solution)/shard_map/ppermute | solution.py:761
  129.8 9.9 %collective-permute-start.18 = (bf16[3,48,896]{2,1,0:T(8,128)(2,1)S(1)}, bf16[3,48,896]{2,1,0:T(8,128)(2,1)S(1)}, u32[]{:S(2)}, u32[]{:S(2)}) collective-permute-start(bf16[3,48,896]{2,1,0:T(8,128)(2,1)S(1)} %get-tuple-element.50), channel_id=1, source_target_pairs={{0,6},{1,7},{2,0},{3,1},{4,2},{5,3},{6,4},{7,5},{8,14},{9,15},{10,... | collective-permute-start | bytes 774152 | tf_op jit(solution)/shard_map/ppermute | solution.py:762
  131.9 15.4 %collective-permute-start.19 = (bf16[3,96,1152]{2,1,0:T(8,128)(2,1)S(1)}, bf16[3,96,1152]{2,1,0:T(8,128)(2,1)S(1)}, u32[]{:S(2)}, u32[]{:S(2)}) collective-permute-start(bf16[3,96,1152]{2,1,0:T(8,128)(2,1)S(1)} %half_sum.3.mark_ref.own_ref), channel_id=1, source_target_pairs={{0,1},{1,0},{2,3},{3,2},{4,5},{5,4},{6,7},{7,6},{8,9},{9,8},{10,11... | collective-permute-start | bytes 1990664 | tf_op jit(solution)/shard_map/ppermute | solution.py:763
  140.0 18.4 %collective-permute-start.20 = (bf16[3,48,1792]{2,1,0:T(8,128)(2,1)S(1)}, bf16[3,48,1792]{2,1,0:T(8,128)(2,1)S(1)}, u32[]{:S(2)}, u32[]{:S(2)}) collective-permute-start(bf16[3,48,1792]{2,1,0:T(8,128)(2,1)S(1)} %ring_sum.1.mark_ref.own_ref), channel_id=1, source_target_pairs={{0,1},{1,0},{2,3},{3,2},{4,5},{5,4},{6,7},{7,6},{8,9},{9,8},{10,11... | collective-permute-start | bytes 1548296 | tf_op jit(solution)/shard_map/ppermute | solution.py:763
  159.8 21.8 %collective-permute-start.21 = (bf16[3,96,256]{2,1,0:T(8,128)(2,1)S(1)}, bf16[3,96,256]{2,1,0:T(8,128)(2,1)S(1)}, u32[]{:S(2)}, u32[]{:S(2)}) collective-permute-start(bf16[3,96,256]{2,1,0:T(8,128)(2,1)S(1)} %get-tuple-element.62), channel_id=1, source_target_pairs={{0,8},{8,16},{16,24},{24,32},{32,40},{40,48},{48,56},{56,64},{64,7... | collective-permute-start | bytes 442376 | tf_op jit(solution)/shard_map/ppermute | solution.py:800
  166.6 14.9 %collective-permute-start.22 = (bf16[3,96,256]{2,1,0:T(8,128)(2,1)S(1)}, bf16[3,96,256]{2,1,0:T(8,128)(2,1)S(1)}, u32[]{:S(2)}, u32[]{:S(2)}) collective-permute-start(bf16[3,96,256]{2,1,0:T(8,128)(2,1)S(1)} %get-tuple-element.61), channel_id=1, source_target_pairs={{8,0},{16,8},{24,16},{32,24},{40,32},{48,40},{56,48},{64,56},{72,6... | collective-permute-start | bytes 442376 | tf_op jit(solution)/shard_map/ppermute | solution.py:801
  187.7 5.4 %collective-permute-start.23 = (f32[36,512]{1,0:T(8,128)S(1)}, f32[36,512]{1,0:T(8,128)S(1)}, u32[]{:S(2)}, u32[]{:S(2)}) collective-permute-start(f32[36,512]{1,0:T(8,128)S(1)} %get-tuple-element.57), channel_id=1, source_target_pairs={{0,2},{1,3},{2,4},{3,5},{4,6},{5,7},{6,0},{7,1},{8,10},{9,11},{10,... | collective-permute-start | bytes 221192 | tf_op jit(solution)/shard_map/ppermute | solution.py:804
  187.8 5.4 %collective-permute-start.24 = (f32[36,512]{1,0:T(8,128)S(1)}, f32[36,512]{1,0:T(8,128)S(1)}, u32[]{:S(2)}, u32[]{:S(2)}) collective-permute-start(f32[36,512]{1,0:T(8,128)S(1)} %get-tuple-element.56), channel_id=1, source_target_pairs={{0,4},{1,5},{2,6},{3,7},{4,0},{5,1},{6,2},{7,3},{8,12},{9,13},{10,... | collective-permute-start | bytes 221192 | tf_op jit(solution)/shard_map/ppermute | solution.py:804
  190.1 3.6 %collective-permute-start.25 = (f32[36,512]{1,0:T(8,128)S(1)}, f32[36,512]{1,0:T(8,128)S(1)}, u32[]{:S(2)}, u32[]{:S(2)}) collective-permute-start(f32[36,512]{1,0:T(8,128)S(1)} %get-tuple-element.55), channel_id=1, source_target_pairs={{0,6},{1,7},{2,0},{3,1},{4,2},{5,3},{6,4},{7,5},{8,14},{9,15},{10,... | collective-permute-start | bytes 221192 | tf_op jit(solution)/shard_map/ppermute | solution.py:804
  (10 other events, 109.6 us)

commit v8 on v7

--- a/solution.py
+++ b/solution.py
@@ -468,9 +468,9 @@
 
 def all_weights_kernel(mark_ref, conn_ref, grads_ref, out_ref, made, sems):
     del mark_ref
-    blocks, _, nodes, _ = out_ref.shape
+    blocks = out_ref.shape[0]
     slots, _, count, wide = made.shape
-    parts = nodes // count
+    parts = slots
 
     def copies(block, part, slot):
         rows = pl.ds(part * count, count)
@@ -505,17 +505,17 @@
             copy.wait()
 
 
-def all_weights(mark, data, nodes):
+def all_weights(mark, data, nodes, room):
     elems = data.shape[1]
     slots = 4
     count = nodes // slots
     return pl.pallas_call(
         all_weights_kernel,
-        out_shape=shaped((elems // WIDE, 3, nodes, WIDE), BF16),
+        out_shape=shaped((elems // WIDE, 3, room, WIDE), BF16),
         in_specs=[ANY, VMEM, VMEM],
         out_specs=ANY,
         scratch_shapes=[pltpu.VMEM((slots, 3, count, WIDE), BF16), pltpu.SemaphoreType.DMA((slots, 3))],
-        compiler_params=params(30),
+        compiler_params=params(16),
         cost_estimate=cost(),
         name="all_weights",
     )(mark, data[:8], data[8:32])
@@ -573,7 +573,8 @@
     blocks = weights_ref.shape[0]
 
     def copy(block, slot):
-        return pltpu.make_async_copy(weights_ref.at[block], held.at[slot], sems.at[slot])
+        rows = pl.ds(0, nodes)
+        return pltpu.make_async_copy(weights_ref.at[block, :, rows, :], held.at[slot], sems.at[slot])
 
     for slot in range(2):
         copy(slot, slot).start()
@@ -605,7 +606,7 @@
         out_specs=VMEM,
         input_output_aliases={3: 0},
         scratch_shapes=[pltpu.VMEM((2, 3, nodes, WIDE), BF16), pltpu.SemaphoreType.DMA((2,))],
-        compiler_params=params(34),
+        compiler_params=params(20),
         cost_estimate=cost(),
         name="fetch_multiply",
     )(mark, values, weights, acc)
@@ -774,7 +775,7 @@
     got_0 = side(away)
     ways_1 = z_first_terms(keep, resp, shapes, c_1, 43)
     plus_1, minus_1 = up(ways_1[0]), down(ways_1[1])
-    weights_0 = all_weights(ways_1[2], data, w_0)
+    weights_0 = all_weights(ways_1[2], data, w_0, nodes)
     on_1 = pass_on(weights_0, ways_1[2], ways_1[3], plus_1, minus_1)
     up_1, down_1 = up(on_1[0]), down(on_1[1])
     ways_0 = x_sum(on_1[0], keep, got_0)

time: 196 us -> 180 us (0.918)
  Pallas kernels: 118 us -> 86.7 us
  waiting for transfers between devices: 24 us -> 41.1 us
  local copies, waits for them, and re-layouts: 8.09 us -> 1.16 us
  starting transfers between devices: 43.2 us -> 47.1 us
    pallas_call x1, Pallas kernels: 38.4 us -> 11 us  [all_weights(): pl.pallas_call(all_weights_kernel, out_shape=shaped((elems // WIDE, 3, ro...]
    ppermute x4, waiting for transfers between devices: 0.01 us -> 16.8 us  [local(): down = lambda v: lax.ppermute(v, 'mode', down_perm)]
    unnamed x17 -> x15, local copies, waits for them, and re-layouts: 6.96 us -> 0.03 us
  transfers between devices with their start and end apart: 26 -> 26, of which waited for: 11 -> 14; matrix products, arithmetic and copies ran while one was open for 0% -> 0% of each run, Pallas kernels for 48% -> 35%
where the time goes in v8:
time: 180 us; the launch traced here: 178 us
  Pallas kernels  86.7 us (48%)
  starting transfers between devices  47.1 us (26%)
  waiting for transfers between devices  41.1 us (23%)
    ppermute x4, waiting for transfers between devices, local(): down = lambda v: lax.ppermute(v, 'mode', down_perm)  16.8 us
    pallas_call x3, Pallas kernels, element_weights(): pl.pallas_call(functools.partial(weights_kernel, float(first)), out_shape...  15.5 us
    pallas_call x1, Pallas kernels, fetch_multiply(): pl.pallas_call(fetch_multiply_kernel, out_shape=shaped(acc.shape, F32), i...  13 us
    pallas_call x2, Pallas kernels, multiply(): pl.pallas_call(multiply_kernel, out_shape=shaped((3, comps * rows, elems)...  12.8 us
    pallas_call x1, Pallas kernels, partial_loads(): pl.pallas_call(functools.partial(loads_kernel, cuts), out_shape=(shaped((...  11.1 us
    ppermute x4, starting transfers between devices, local(): down = lambda v: lax.ppermute(v, 'mode', down_perm)  11.1 us
    pallas_call x1, Pallas kernels, all_weights(): pl.pallas_call(all_weights_kernel, out_shape=shaped((elems // WIDE, 3, ro...  11 us
    ppermute x1, starting transfers between devices, local(): lax.ppermute(rim[..., bound:], 'mesh', [(p, p + 1) for p in range(count -...  8.06 us
  transfers between devices with their start and end apart: 26, of which 14 were waited for; matrix products, arithmetic and copies ran while one was open for 0% of the time, Pallas kernels for 35%

profile of v8, /device:TPU:1, one launch (start us, length us, event | category | flops | bytes accessed | tf_op | source)
XLA Modules:
  0.0 178.0 jit_solution(14280346482483510977)
XLA Ops:
  0.0 11.1 %modal_loads.1 = (f32[256,384]{1,0:T(8,128)}, bf16[256,384]{1,0:T(8,128)(2,1)}) custom-call(s32[1]{0:T(128)} %bitcast.1.core_ref, bf16[3,500,4096]{2,1,0:T(8,128)(2,1)} %bitcast.19, bf16[3,4096,384]{2,1,0:T(8,128)(2,1)} %load_ref.1), custom_call_target="tpu_custom_call" | custom-call | flops 1 | bytes 1 | tf_op jit(solution)/shard_map/modal_loads/pallas_call | solution.py:88
  15.0 2.9 %collective-permute-start.4 = (bf16[256,384]{1,0:T(8,128)(2,1)S(1)}, bf16[256,384]{1,0:T(8,128)(2,1)S(1)}, u32[]{:S(2)}, u32[]{:S(2)}) collective-permute-start(bf16[256,384]{1,0:T(8,128)(2,1)S(1)} %add_convert_fusion.1.mark_ref), channel_id=1, source_target_pairs={{0,16},{8,24},{16,0},{24,8},{32,48},{40,56},{48,32},{56,40},{64,80... | collective-permute-start | bytes 589832 | tf_op jit(solution)/shard_map/ppermute | solution.py:753
  18.2 3.8 %collective-permute-start.1 = (f32[40,512]{1,0:T(8,128)S(1)}, f32[40,512]{1,0:T(8,128)S(1)}, u32[]{:S(2)}, u32[]{:S(2)}) collective-permute-start(f32[40,512]{1,0:T(8,128)S(1)} %element_data.1), channel_id=1, source_target_pairs={{0,6},{1,7},{2,0},{3,1},{4,2},{5,3},{6,4},{7,5},{8,14},{9,15},{10,... | collective-permute-start | bytes 245768 | tf_op jit(solution)/shard_map/ppermute | solution.py:759
  24.2 2.6 %collective-permute-start.6 = (bf16[256,384]{1,0:T(8,128)(2,1)S(1)}, bf16[256,384]{1,0:T(8,128)(2,1)S(1)}, u32[]{:S(2)}, u32[]{:S(2)}) collective-permute-start(bf16[256,384]{1,0:T(8,128)(2,1)S(1)} %add_convert_fusion.a_ref), channel_id=1, source_target_pairs={{0,64},{8,72},{16,80},{24,88},{32,96},{40,104},{48,112},{56,120},{... | collective-permute-start | bytes 589832 | tf_op jit(solution)/shard_map/ppermute | solution.py:755
  29.2 5.3 %collective-permute-done.6.c_ref = bf16[256,384]{1,0:T(8,128)(2,1)S(1)} collective-permute-done((bf16[256,384]{1,0:T(8,128)(2,1)S(1)}, bf16[256,384]{1,0:T(8,128)(2,1)S(1)}, u32[]{:S(2)}, u32[]{:S(2)}) %collective-permute-start.6) | collective-permute-done | bytes 196640 | tf_op jit(solution)/shard_map/ppermute | solution.py:755
  38.4 5.2 %x_first_terms.1 = (bf16[4,3,48,1792]{3,2,1,0:T(8,128)(2,1)S(1)}, bf16[4,3,48,1792]{3,2,1,0:T(8,128)(2,1)S(1)}, bf16[384,500]{1,0:T(8,128)(2,1)S(1)}) custom-call(s32[1]{0:T(128)} %bitcast.1.core_ref, bf16[256,384]{1,0:T(8,128)(2,1)S(1)} %modal_response.1.mine_ref, bf16[256,384]{1,0:T(8,128)(2,1)S(1)} %collective-permute-done.8.theirs_ref, ...), custom_call_target="tpu_custom_call" | custom-call | flops 1 | bytes 1 | tf_op jit(solution)/shard_map/x_first_terms/pallas_call | solution.py:266
  44.9 5.1 %z_first_terms.1 = (bf16[2,3,96,1152]{3,2,1,0:T(8,128)(2,1)S(1)}, bf16[2,3,96,1152]{3,2,1,0:T(8,128)(2,1)S(1)}, bf16[3,96,1152]{2,1,0:T(8,128)(2,1)S(1)}, bf16[3...) custom-call(bf16[4,3,48,1792]{3,2,1,0:T(8,128)(2,1)S(1)} %get-tuple-element.32.mark_ref.keep_ref, ...), custom_call_target="tpu_custom_call" | custom-call | flops 1 | bytes 1 | tf_op jit(solution)/shard_map/z_first_terms/pallas_call | solution.py:223
  50.1 3.8 %collective-permute-start.10 = (bf16[2,3,96,1152]{3,2,1,0:T(8,128)(2,1)S(1)}, bf16[2,3,96,1152]{3,2,1,0:T(8,128)(2,1)S(1)}, u32[]{:S(2)}, u32[]{:S(2)}) collective-permute-start(bf16[2,3,96,1152]{3,2,1,0:T(8,128)(2,1)S(1)} %get-tuple-element.37), channel_id=1, source_target_pairs={{0,6},{1,7},{2,0},{3,1},{4,2},{5,3},{6,4},{7,5},{8,14},{9,15},{10,... | collective-permute-start | bytes 3981320 | tf_op jit(solution)/shard_map/ppermute | solution.py:763
  53.9 11.0 %all_weights.1.mark_ref.weights_ref = bf16[8,3,4096,256]{3,2,1,0:T(8,128)(2,1)} custom-call(bf16[3,96,1152]{2,1,0:T(8,128)(2,1)S(1)} %get-tuple-element.34.mark_ref.up_ref, f32[8,2048]{1,0:T(8,128)S(1)} %get-tuple-element.60.conn_ref, f32[24,2048]{1,0:T(8,128)S(1)} %slice.43.grads_ref), custom_call_target="tpu_custom_call" | custom-call | flops 1 | bytes 1 | tf_op jit(solution)/shard_map/all_weights/pallas_call | solution.py:512
  64.9 16.8 %collective-permute-done.10.minus_ref.direct_ref = bf16[2,3,96,1152]{3,2,1,0:T(8,128)(2,1)S(1)} collective-permute-done((bf16[2,3,96,1152]{3,2,1,0:T(8,128)(2,1)S(1)}, bf16[2,3,96,1152]{3,2,1,0:T(8,128)(2,1)S(1)}, u32[]{:S(2)}, u32[]{:S(2)}) %collective-permute-start.10) | collective-permute-done | bytes 1327136 | tf_op jit(solution)/shard_map/ppermute | solution.py:763
  81.7 3.1 %collective-permute-done.9.plus_ref.direct_ref = bf16[2,3,96,1152]{3,2,1,0:T(8,128)(2,1)S(1)} collective-permute-done((bf16[2,3,96,1152]{3,2,1,0:T(8,128)(2,1)S(1)}, bf16[2,3,96,1152]{3,2,1,0:T(8,128)(2,1)S(1)}, u32[]{:S(2)}, u32[]{:S(2)}) %collective-permute-start.9) | collective-permute-done | bytes 1327136 | tf_op jit(solution)/shard_map/ppermute | solution.py:762
  85.2 2.7 %collective-permute-start.13 = (bf16[3,96,1152]{2,1,0:T(8,128)(2,1)S(1)}, bf16[3,96,1152]{2,1,0:T(8,128)(2,1)S(1)}, u32[]{:S(2)}, u32[]{:S(2)}) collective-permute-start(bf16[3,96,1152]{2,1,0:T(8,128)(2,1)S(1)} %get-tuple-element.42), channel_id=1, source_target_pairs={{0,6},{1,7},{2,0},{3,1},{4,2},{5,3},{6,4},{7,5},{8,14},{9,15},{10,... | collective-permute-start | bytes 1990664 | tf_op jit(solution)/shard_map/ppermute | solution.py:763
  94.6 6.3 %element_weights.3.mark_ref.after_ref.weights_ref = bf16[3,1152,2048]{2,1,0:T(8,128)(2,1)S(1)} custom-call(bf16[3,48,896]{2,1,0:T(8,128)(2,1)S(1)} %get-tuple-element.40.mark_ref.up_ref, f32[8,2048]{1,0:T(8,128)S(1)} %get-tuple-element.60.conn_ref, f32[24,2048]{1,0:T(8,128)S(1)} %slice.43.grads_ref), custom_call_target="tpu_custom_call" | custom-call | flops 1 | bytes 1 | tf_op jit(solution)/shard_map/element_weights/pallas_call | solution.py:526
  103.0 6.3 %element_weights.4.mark_ref.weights_ref = bf16[3,1152,2048]{2,1,0:T(8,128)(2,1)S(1)} custom-call(bf16[3,96,1152]{2,1,0:T(8,128)(2,1)S(1)} %half_sum.3.mark_ref.own_ref, f32[8,2048]{1,0:T(8,128)S(1)} %get-tuple-element.60.conn_ref, f32[24,2048]{1,0:T(8,128)S(1)} %slice.43.grads_ref), custom_call_target="tpu_custom_call" | custom-call | flops 1 | bytes 1 | tf_op jit(solution)/shard_map/element_weights/pallas_call | solution.py:526
  109.3 2.7 %collective-permute-done.14.plus_ref = bf16[2,3,48,896]{3,2,1,0:T(8,128)(2,1)S(1)} collective-permute-done((bf16[2,3,48,896]{3,2,1,0:T(8,128)(2,1)S(1)}, bf16[2,3,48,896]{3,2,1,0:T(8,128)(2,1)S(1)}, u32[]{:S(2)}, u32[]{:S(2)}) %collective-permute-start.14) | collective-permute-done | bytes 516128 | tf_op jit(solution)/shard_map/ppermute | solution.py:762
  112.3 2.7 %collective-permute-start.18 = (bf16[3,48,896]{2,1,0:T(8,128)(2,1)S(1)}, bf16[3,48,896]{2,1,0:T(8,128)(2,1)S(1)}, u32[]{:S(2)}, u32[]{:S(2)}) collective-permute-start(bf16[3,48,896]{2,1,0:T(8,128)(2,1)S(1)} %get-tuple-element.50), channel_id=1, source_target_pairs={{0,6},{1,7},{2,0},{3,1},{4,2},{5,3},{6,4},{7,5},{8,14},{9,15},{10,... | collective-permute-start | bytes 774152 | tf_op jit(solution)/shard_map/ppermute | solution.py:763
  116.6 6.2 %multiply.2.mark_ref.refs_0_ = f32[3,288,2048]{2,1,0:T(8,128)S(1)} custom-call(bf16[3,96,512]{2,1,0:T(8,128)(2,1)S(1)} %get-tuple-element.47.mark_ref.refs_0_, bf16[3,96,1152]{2,1,0:T(8,128)(2,1)S(1)} %get-tuple-element.48.values_ref, bf16[3,1152,2048]{2,1,0:T(8,128)(2,1)S(1)} %element_weights.3.mark_ref.after_ref.weights_ref), custom_call_target="tpu_custom_call" | custom-call | flops 1 | bytes 1 | tf_op jit(solution)/shard_map/multiply/pallas_call | solution.py:557
  124.4 2.9 %element_weights.5.mark_ref.weights_ref = bf16[3,512,2048]{2,1,0:T(8,128)(2,1)S(1)} custom-call(bf16[3,48,1792]{2,1,0:T(8,128)(2,1)S(1)} %ring_sum.1.mark_ref.own_ref, f32[8,2048]{1,0:T(8,128)S(1)} %get-tuple-element.60.conn_ref, f32[24,2048]{1,0:T(8,128)S(1)} %slice.43.grads_ref), custom_call_target="tpu_custom_call" | custom-call | flops 1 | bytes 1 | tf_op jit(solution)/shard_map/element_weights/pallas_call | solution.py:526
  130.8 6.6 %multiply.3.mark_ref.acc_ref = f32[3,288,2048]{2,1,0:T(8,128)S(1)} custom-call(bf16[3,96,512]{2,1,0:T(8,128)(2,1)S(1)} %get-tuple-element.51.mark_ref.refs_0_, bf16[3,96,1152]{2,1,0:T(8,128)(2,1)S(1)} %get-tuple-element.52.values_ref, bf16[3,1152,2048]{2,1,0:T(8,128)(2,1)S(1)} %element_weights.4.mark_ref.weights_ref, ...), custom_call_target="tpu_custom_call", output_to_operand_aliasing={{}: (3, {})} | custom-call | flops 1 | bytes 1 | tf_op jit(solution)/shard_map/multiply/pallas_call | solution.py:557
  137.4 3.1 %collective-permute-done.20.got_ref = bf16[3,48,1792]{2,1,0:T(8,128)(2,1)S(1)} collective-permute-done((bf16[3,48,1792]{2,1,0:T(8,128)(2,1)S(1)}, bf16[3,48,1792]{2,1,0:T(8,128)(2,1)S(1)}, u32[]{:S(2)}, u32[]{:S(2)}) %collective-permute-start.20) | collective-permute-done | bytes 516128 | tf_op jit(solution)/shard_map/ppermute | solution.py:764
  141.9 8.1 %collective-permute-start.21 = (bf16[3,96,256]{2,1,0:T(8,128)(2,1)S(1)}, bf16[3,96,256]{2,1,0:T(8,128)(2,1)S(1)}, u32[]{:S(2)}, u32[]{:S(2)}) collective-permute-start(bf16[3,96,256]{2,1,0:T(8,128)(2,1)S(1)} %get-tuple-element.62), channel_id=1, source_target_pairs={{0,8},{8,16},{16,24},{24,32},{32,40},{40,48},{48,56},{56,64},{64,7... | collective-permute-start | bytes 442376 | tf_op jit(solution)/shard_map/ppermute | solution.py:801
  151.9 13.0 %fetch_multiply.1.acc_ref = f32[3,288,2048]{2,1,0:T(8,128)S(1)} custom-call(bf16[3,96,512]{2,1,0:T(8,128)(2,1)S(1)} %get-tuple-element.53.mark_ref, bf16[3,96,1792]{2,1,0:T(8,128)(2,1)S(1)} %get-tuple-element.54.values_ref, bf16[8,3,4096,256]{3,2,1,0:T(8,128)(2,1)} %all_weights.1.mark_ref.weights_ref, ...), custom_call_target="tpu_custom_call", output_to_operand_aliasing={{}: (3, {})} | custom-call | flops 1 | bytes 1 | tf_op jit(solution)/shard_map/fetch_multiply/pallas_call | solution.py:602
  164.9 6.1 %element_spectra.1 = f32[4,36,512]{2,1,0:T(8,128)S(1)} custom-call(bf16[3,96,256]{2,1,0:T(8,128)(2,1)S(1)} %collective-permute-done.21.before_ref, bf16[3,96,256]{2,1,0:T(8,128)(2,1)S(1)} %collective-permute-done.22.after_ref, bf16[3,512,2048]{2,1,0:T(8,128)(2,1)S(1)} %element_weights.5.mark_ref.weights_ref, f32[3,288,2048]{2,1,0:T(8,128)S(1)} %fetch_multiply.1.acc_ref, ...), custom_call_target="tpu_custom_call" | custom-call | flops 1 | bytes 1 | tf_op jit(solution)/shard_map/element_spectra/pallas_call | solution.py:679
  171.1 2.5 %collective-permute-start.24 = (f32[36,512]{1,0:T(8,128)S(1)}, f32[36,512]{1,0:T(8,128)S(1)}, u32[]{:S(2)}, u32[]{:S(2)}) collective-permute-start(f32[36,512]{1,0:T(8,128)S(1)} %get-tuple-element.56), channel_id=1, source_target_pairs={{0,4},{1,5},{2,6},{3,7},{4,0},{5,1},{6,2},{7,3},{8,12},{9,13},{10,... | collective-permute-start | bytes 221192 | tf_op jit(solution)/shard_map/ppermute | solution.py:805
  (82 shorter events, 37.6 us)
Async XLA Ops:
  15.0 7.7 %collective-permute-start.4 = (bf16[256,384]{1,0:T(8,128)(2,1)S(1)}, bf16[256,384]{1,0:T(8,128)(2,1)S(1)}, u32[]{:S(2)}, u32[]{:S(2)}) collective-permute-start(bf16[256,384]{1,0:T(8,128)(2,1)S(1)} %add_convert_fusion.1.mark_ref), channel_id=1, source_target_pairs={{0,16},{8,24},{16,0},{24,8},{32,48},{40,56},{48,32},{56,40},{64,80... | collective-permute-start | bytes 589832 | tf_op jit(solution)/shard_map/ppermute | solution.py:753
  18.2 8.6 %collective-permute-start.1 = (f32[40,512]{1,0:T(8,128)S(1)}, f32[40,512]{1,0:T(8,128)S(1)}, u32[]{:S(2)}, u32[]{:S(2)}) collective-permute-start(f32[40,512]{1,0:T(8,128)S(1)} %element_data.1), channel_id=1, source_target_pairs={{0,6},{1,7},{2,0},{3,1},{4,2},{5,3},{6,4},{7,5},{8,14},{9,15},{10,... | collective-permute-start | bytes 245768 | tf_op jit(solution)/shard_map/ppermute | solution.py:759
  22.0 5.9 %collective-permute-start.2 = (f32[40,512]{1,0:T(8,128)S(1)}, f32[40,512]{1,0:T(8,128)S(1)}, u32[]{:S(2)}, u32[]{:S(2)}) collective-permute-start(f32[40,512]{1,0:T(8,128)S(1)} %element_data.1), channel_id=1, source_target_pairs={{0,4},{1,5},{2,6},{3,7},{4,0},{5,1},{6,2},{7,3},{8,12},{9,13},{10,... | collective-permute-start | bytes 245768 | tf_op jit(solution)/shard_map/ppermute | solution.py:759
  22.0 6.4 %collective-permute-start.3 = (f32[40,512]{1,0:T(8,128)S(1)}, f32[40,512]{1,0:T(8,128)S(1)}, u32[]{:S(2)}, u32[]{:S(2)}) collective-permute-start(f32[40,512]{1,0:T(8,128)S(1)} %element_data.1), channel_id=1, source_target_pairs={{0,2},{1,3},{2,4},{3,5},{4,6},{5,7},{6,0},{7,1},{8,10},{9,11},{10,... | collective-permute-start | bytes 245768 | tf_op jit(solution)/shard_map/ppermute | solution.py:759
  22.8 6.4 %collective-permute-start.5 = (bf16[256,384]{1,0:T(8,128)(2,1)S(1)}, bf16[256,384]{1,0:T(8,128)(2,1)S(1)}, u32[]{:S(2)}, u32[]{:S(2)}) collective-permute-start(bf16[256,384]{1,0:T(8,128)(2,1)S(1)} %add_convert_fusion.a_ref), channel_id=1, source_target_pairs={{0,32},{8,40},{16,48},{24,56},{32,64},{40,72},{48,80},{56,88},{64,... | collective-permute-start | bytes 589832 | tf_op jit(solution)/shard_map/ppermute | solution.py:755
  24.2 10.3 %collective-permute-start.6 = (bf16[256,384]{1,0:T(8,128)(2,1)S(1)}, bf16[256,384]{1,0:T(8,128)(2,1)S(1)}, u32[]{:S(2)}, u32[]{:S(2)}) collective-permute-start(bf16[256,384]{1,0:T(8,128)(2,1)S(1)} %add_convert_fusion.a_ref), channel_id=1, source_target_pairs={{0,64},{8,72},{16,80},{24,88},{32,96},{40,104},{48,112},{56,120},{... | collective-permute-start | bytes 589832 | tf_op jit(solution)/shard_map/ppermute | solution.py:755
  26.8 7.7 %collective-permute-start.7 = (bf16[256,384]{1,0:T(8,128)(2,1)S(1)}, bf16[256,384]{1,0:T(8,128)(2,1)S(1)}, u32[]{:S(2)}, u32[]{:S(2)}) collective-permute-start(bf16[256,384]{1,0:T(8,128)(2,1)S(1)} %add_convert_fusion.a_ref), channel_id=1, source_target_pairs={{0,96},{8,104},{16,112},{24,120},{32,0},{40,8},{48,16},{56,24},{64... | collective-permute-start | bytes 589832 | tf_op jit(solution)/shard_map/ppermute | solution.py:755
  34.9 3.5 %collective-permute-start.8 = (bf16[256,384]{1,0:T(8,128)(2,1)S(1)}, bf16[256,384]{1,0:T(8,128)(2,1)S(1)}, u32[]{:S(2)}, u32[]{:S(2)}) collective-permute-start(bf16[256,384]{1,0:T(8,128)(2,1)S(1)} %modal_response.1.mine_ref), channel_id=1, source_target_pairs={{0,8},{8,0},{16,24},{24,16},{32,40},{40,32},{48,56},{56,48},{64,72... | collective-permute-start | bytes 589832 | tf_op jit(solution)/shard_map/ppermute | solution.py:773
  43.6 46.2 %collective-permute-start.11 = (bf16[4,3,48,1792]{3,2,1,0:T(8,128)(2,1)S(1)}, bf16[4,3,48,1792]{3,2,1,0:T(8,128)(2,1)S(1)}, u32[]{:S(2)}, u32[]{:S(2)}) collective-permute-start(bf16[4,3,48,1792]{3,2,1,0:T(8,128)(2,1)S(1)} %get-tuple-element.39), channel_id=1, source_target_pairs={{0,1},{1,0},{2,3},{3,2},{4,5},{5,4},{6,7},{7,6},{8,9},{9,8},{10,11... | collective-permute-start | bytes 6193160 | tf_op jit(solution)/shard_map/ppermute | solution.py:764
  50.1 31.7 %collective-permute-start.10 = (bf16[2,3,96,1152]{3,2,1,0:T(8,128)(2,1)S(1)}, bf16[2,3,96,1152]{3,2,1,0:T(8,128)(2,1)S(1)}, u32[]{:S(2)}, u32[]{:S(2)}) collective-permute-start(bf16[2,3,96,1152]{3,2,1,0:T(8,128)(2,1)S(1)} %get-tuple-element.37), channel_id=1, source_target_pairs={{0,6},{1,7},{2,0},{3,1},{4,2},{5,3},{6,4},{7,5},{8,14},{9,15},{10,... | collective-permute-start | bytes 3981320 | tf_op jit(solution)/shard_map/ppermute | solution.py:763
  53.9 30.9 %collective-permute-start.9 = (bf16[2,3,96,1152]{3,2,1,0:T(8,128)(2,1)S(1)}, bf16[2,3,96,1152]{3,2,1,0:T(8,128)(2,1)S(1)}, u32[]{:S(2)}, u32[]{:S(2)}) collective-permute-start(bf16[2,3,96,1152]{3,2,1,0:T(8,128)(2,1)S(1)} %get-tuple-element.36), channel_id=1, source_target_pairs={{0,2},{1,3},{2,4},{3,5},{4,6},{5,7},{6,0},{7,1},{8,10},{9,11},{10,... | collective-permute-start | bytes 3981320 | tf_op jit(solution)/shard_map/ppermute | solution.py:762
  85.2 15.8 %collective-permute-start.12 = (bf16[3,96,1152]{2,1,0:T(8,128)(2,1)S(1)}, bf16[3,96,1152]{2,1,0:T(8,128)(2,1)S(1)}, u32[]{:S(2)}, u32[]{:S(2)}) collective-permute-start(bf16[3,96,1152]{2,1,0:T(8,128)(2,1)S(1)} %get-tuple-element.38.mark_ref), channel_id=1, source_target_pairs={{0,2},{1,3},{2,4},{3,5},{4,6},{5,7},{6,0},{7,1},{8,10},{9,11},{10,... | collective-permute-start | bytes 1990664 | tf_op jit(solution)/shard_map/ppermute | solution.py:762
  85.2 17.4 %collective-permute-start.13 = (bf16[3,96,1152]{2,1,0:T(8,128)(2,1)S(1)}, bf16[3,96,1152]{2,1,0:T(8,128)(2,1)S(1)}, u32[]{:S(2)}, u32[]{:S(2)}) collective-permute-start(bf16[3,96,1152]{2,1,0:T(8,128)(2,1)S(1)} %get-tuple-element.42), channel_id=1, source_target_pairs={{0,6},{1,7},{2,0},{3,1},{4,2},{5,3},{6,4},{7,5},{8,14},{9,15},{10,... | collective-permute-start | bytes 1990664 | tf_op jit(solution)/shard_map/ppermute | solution.py:763
  90.7 21.3 %collective-permute-start.14 = (bf16[2,3,48,896]{3,2,1,0:T(8,128)(2,1)S(1)}, bf16[2,3,48,896]{3,2,1,0:T(8,128)(2,1)S(1)}, u32[]{:S(2)}, u32[]{:S(2)}) collective-permute-start(bf16[2,3,48,896]{3,2,1,0:T(8,128)(2,1)S(1)} %get-tuple-element.44), channel_id=1, source_target_pairs={{0,2},{1,3},{2,4},{3,5},{4,6},{5,7},{6,0},{7,1},{8,10},{9,11},{10,... | collective-permute-start | bytes 1548296 | tf_op jit(solution)/shard_map/ppermute | solution.py:762
  92.7 19.4 %collective-permute-start.15 = (bf16[2,3,48,896]{3,2,1,0:T(8,128)(2,1)S(1)}, bf16[2,3,48,896]{3,2,1,0:T(8,128)(2,1)S(1)}, u32[]{:S(2)}, u32[]{:S(2)}) collective-permute-start(bf16[2,3,48,896]{3,2,1,0:T(8,128)(2,1)S(1)} %get-tuple-element.45), channel_id=1, source_target_pairs={{0,6},{1,7},{2,0},{3,1},{4,2},{5,3},{6,4},{7,5},{8,14},{9,15},{10,... | collective-permute-start | bytes 1548296 | tf_op jit(solution)/shard_map/ppermute | solution.py:763
  101.4 13.9 %collective-permute-start.16 = (bf16[3,96,1152]{2,1,0:T(8,128)(2,1)S(1)}, bf16[3,96,1152]{2,1,0:T(8,128)(2,1)S(1)}, u32[]{:S(2)}, u32[]{:S(2)}) collective-permute-start(bf16[3,96,1152]{2,1,0:T(8,128)(2,1)S(1)} %half_sum.2.mark_ref.after_ref.own_ref), channel_id=1, source_target_pairs={{0,1},{1,0},{2,3},{3,2},{4,5},{5,4},{6,7},{7,6},{8,9},{9,8},{10,11... | collective-permute-start | bytes 1990664 | tf_op jit(solution)/shard_map/ppermute | solution.py:764
  112.2 10.6 %collective-permute-start.17 = (bf16[3,48,896]{2,1,0:T(8,128)(2,1)S(1)}, bf16[3,48,896]{2,1,0:T(8,128)(2,1)S(1)}, u32[]{:S(2)}, u32[]{:S(2)}) collective-permute-start(bf16[3,48,896]{2,1,0:T(8,128)(2,1)S(1)} %get-tuple-element.46.mark_ref), channel_id=1, source_target_pairs={{0,2},{1,3},{2,4},{3,5},{4,6},{5,7},{6,0},{7,1},{8,10},{9,11},{10,... | collective-permute-start | bytes 774152 | tf_op jit(solution)/shard_map/ppermute | solution.py:762
  112.3 10.5 %collective-permute-start.18 = (bf16[3,48,896]{2,1,0:T(8,128)(2,1)S(1)}, bf16[3,48,896]{2,1,0:T(8,128)(2,1)S(1)}, u32[]{:S(2)}, u32[]{:S(2)}) collective-permute-start(bf16[3,48,896]{2,1,0:T(8,128)(2,1)S(1)} %get-tuple-element.50), channel_id=1, source_target_pairs={{0,6},{1,7},{2,0},{3,1},{4,2},{5,3},{6,4},{7,5},{8,14},{9,15},{10,... | collective-permute-start | bytes 774152 | tf_op jit(solution)/shard_map/ppermute | solution.py:763
  115.0 14.5 %collective-permute-start.19 = (bf16[3,96,1152]{2,1,0:T(8,128)(2,1)S(1)}, bf16[3,96,1152]{2,1,0:T(8,128)(2,1)S(1)}, u32[]{:S(2)}, u32[]{:S(2)}) collective-permute-start(bf16[3,96,1152]{2,1,0:T(8,128)(2,1)S(1)} %half_sum.3.mark_ref.own_ref), channel_id=1, source_target_pairs={{0,1},{1,0},{2,3},{3,2},{4,5},{5,4},{6,7},{7,6},{8,9},{9,8},{10,11... | collective-permute-start | bytes 1990664 | tf_op jit(solution)/shard_map/ppermute | solution.py:764
  123.1 17.4 %collective-permute-start.20 = (bf16[3,48,1792]{2,1,0:T(8,128)(2,1)S(1)}, bf16[3,48,1792]{2,1,0:T(8,128)(2,1)S(1)}, u32[]{:S(2)}, u32[]{:S(2)}) collective-permute-start(bf16[3,48,1792]{2,1,0:T(8,128)(2,1)S(1)} %ring_sum.1.mark_ref.own_ref), channel_id=1, source_target_pairs={{0,1},{1,0},{2,3},{3,2},{4,5},{5,4},{6,7},{7,6},{8,9},{9,8},{10,11... | collective-permute-start | bytes 1548296 | tf_op jit(solution)/shard_map/ppermute | solution.py:764
  141.9 23.0 %collective-permute-start.21 = (bf16[3,96,256]{2,1,0:T(8,128)(2,1)S(1)}, bf16[3,96,256]{2,1,0:T(8,128)(2,1)S(1)}, u32[]{:S(2)}, u32[]{:S(2)}) collective-permute-start(bf16[3,96,256]{2,1,0:T(8,128)(2,1)S(1)} %get-tuple-element.62), channel_id=1, source_target_pairs={{0,8},{8,16},{16,24},{24,32},{32,40},{40,48},{48,56},{56,64},{64,7... | collective-permute-start | bytes 442376 | tf_op jit(solution)/shard_map/ppermute | solution.py:801
  149.9 15.0 %collective-permute-start.22 = (bf16[3,96,256]{2,1,0:T(8,128)(2,1)S(1)}, bf16[3,96,256]{2,1,0:T(8,128)(2,1)S(1)}, u32[]{:S(2)}, u32[]{:S(2)}) collective-permute-start(bf16[3,96,256]{2,1,0:T(8,128)(2,1)S(1)} %get-tuple-element.61), channel_id=1, source_target_pairs={{8,0},{16,8},{24,16},{32,24},{40,32},{48,40},{56,48},{64,56},{72,6... | collective-permute-start | bytes 442376 | tf_op jit(solution)/shard_map/ppermute | solution.py:802
  171.0 5.4 %collective-permute-start.23 = (f32[36,512]{1,0:T(8,128)S(1)}, f32[36,512]{1,0:T(8,128)S(1)}, u32[]{:S(2)}, u32[]{:S(2)}) collective-permute-start(f32[36,512]{1,0:T(8,128)S(1)} %get-tuple-element.57), channel_id=1, source_target_pairs={{0,2},{1,3},{2,4},{3,5},{4,6},{5,7},{6,0},{7,1},{8,10},{9,11},{10,... | collective-permute-start | bytes 221192 | tf_op jit(solution)/shard_map/ppermute | solution.py:805
  171.1 5.4 %collective-permute-start.24 = (f32[36,512]{1,0:T(8,128)S(1)}, f32[36,512]{1,0:T(8,128)S(1)}, u32[]{:S(2)}, u32[]{:S(2)}) collective-permute-start(f32[36,512]{1,0:T(8,128)S(1)} %get-tuple-element.56), channel_id=1, source_target_pairs={{0,4},{1,5},{2,6},{3,7},{4,0},{5,1},{6,2},{7,3},{8,12},{9,13},{10,... | collective-permute-start | bytes 221192 | tf_op jit(solution)/shard_map/ppermute | solution.py:805
  (9 other events, 102.1 us)
